TPU v7x, 32 devices: a whole 2x2x4 slice. The times are simulated.
32 devices in a mesh: group: 2 (over z_hi), shard: 8 (over y, x, core), tensor: 2 (over z_lo).
Axes of the slice: x: 2, y: 2, z: 4 (z_hi: 2, z_lo: 2; z = z_hi * 2 + z_lo), core: 2. Of those that a mesh axis runs over, the one named last changes fastest.
Arguments:
- down_anchor: float32 [8192, 4096], P('shard', 'tensor'), may hold values from -6 to 6
- down_local: float32 [2, 8192, 4096], P('group', 'shard', 'tensor'), may hold values from -6 to 6
- down_moment: float32 [8192, 4096], P(('shard', 'group'), 'tensor'), may hold values from -4 to 4
- norm_anchor: float32 [2, 4096], P(None, ('shard', 'tensor')), may hold values from 0.5 to 1.5
- norm_local: float32 [2, 2, 4096], P('group', None, ('shard', 'tensor')), may hold values from 0.1 to 1.9
- norm_moment: float32 [2, 4096], P('group', ('shard', 'tensor')), may hold values from -4 to 4
- gate_anchor: float32 [8192, 4096], P('tensor', 'shard'), may hold values from -6 to 6
- gate_local: float32 [2, 8192, 4096], P('group', 'tensor', 'shard'), may hold values from -6 to 6
- gate_moment: float32 [8192, 4096], P('tensor', 'shard'), may hold values from -4 to 4
- factor_basis: float32 [64, 4096], P(None, 'shard'), may hold values from -0.09375 to 0.09375
Outputs:
- new_down_anchor: float32 [8192, 4096], P('shard', 'tensor')
- new_down_moment: float32 [8192, 4096], P(('shard', 'group'), 'tensor')
- new_norm_anchor: float32 [2, 4096], P(None, ('shard', 'tensor'))
- new_norm_moment: float32 [2, 4096], P('group', ('shard', 'tensor'))
- new_gate_anchor: float32 [8192, 4096], P('tensor', 'shard')
- new_gate_moment: float32 [8192, 4096], P('tensor', 'shard')
All inputs are finite; a program needn't handle non-finite values.
Results may differ from a plain program's by a relative error of at most 0.000096.
Values sent between devices are 32-bit elements; how exact they have to be, the bound alone decides.
No kernel may reach another device: no remote copies, remote signals or barrier semaphores. Data moves between devices by JAX's collectives and lax.ppermute only.
A program may use at most 128 MiB of HBM per device.

v0:
```python
import jax
from jax import lax
from jax.sharding import PartitionSpec as P

outer_rate = 0.7
momentum = 0.9


def advance(anchor, moment, delta):
    moment_next = momentum * moment + delta
    anchor_next = anchor - outer_rate * (delta + momentum * moment_next)
    return (anchor_next, moment_next)


def rebuild(factors, factor_basis):
    return lax.dot_general(
        factors, factor_basis, (((0,), (0,)), ((), ())), precision=lax.Precision.HIGHEST
    )


def body(
    down_anchor,
    down_local,
    down_moment,
    norm_anchor,
    norm_local,
    norm_moment,
    gate_anchor,
    gate_local,
    gate_moment,
    factor_basis,
):
    groups = lax.axis_size("group")
    group_index = lax.axis_index("group")
    down_diff = down_anchor - down_local[0]
    norm_diff = norm_anchor - norm_local[0]
    gate_diff = gate_anchor - gate_local[0]
    partial_factors = lax.dot_general(
        factor_basis, gate_diff, (((1,), (1,)), ((), ())), precision=lax.Precision.HIGHEST
    )
    down_sum, norm_sum = (
        lax.psum_scatter(down_diff, "group", scatter_dimension=0, tiled=True),
        lax.psum_scatter(norm_diff, "group", scatter_dimension=0, tiled=True),
    )
    factors = lax.psum(partial_factors, ("group", "shard")) / groups
    half_rows = down_sum.shape[0]
    norm_rows = norm_sum.shape[0]
    down_piece = lax.dynamic_slice_in_dim(down_anchor, group_index * half_rows, half_rows, 0)
    norm_piece = lax.dynamic_slice_in_dim(norm_anchor, group_index * norm_rows, norm_rows, 0)
    down_next, new_down_moment = advance(down_piece, down_moment, down_sum / groups)
    norm_next, new_norm_moment = advance(norm_piece, norm_moment, norm_sum / groups)
    new_down_anchor, new_norm_anchor = (
        lax.all_gather(down_next, "group", axis=0, tiled=True),
        lax.all_gather(norm_next, "group", axis=0, tiled=True),
    )
    gate_delta = rebuild(factors, factor_basis)
    new_gate_anchor, new_gate_moment = advance(gate_anchor, gate_moment, gate_delta)
    return (
        new_down_anchor,
        new_down_moment,
        new_norm_anchor,
        new_norm_moment,
        new_gate_anchor,
        new_gate_moment,
    )


def solution(mesh):
    placed = (
        P("shard", "tensor"),
        P("group", "shard", "tensor"),
        P(("shard", "group"), "tensor"),
        P(None, ("shard", "tensor")),
        P("group", None, ("shard", "tensor")),
        P("group", ("shard", "tensor")),
        P("tensor", "shard"),
        P("group", "tensor", "shard"),
        P("tensor", "shard"),
        P(None, "shard"),
    )
    return jax.shard_map(
        body,
        mesh=mesh,
        in_specs=placed,
        out_specs=(
            P("shard", "tensor"),
            P(("shard", "group"), "tensor"),
            P(None, ("shard", "tensor")),
            P("group", ("shard", "tensor")),
            P("tensor", "shard"),
            P("tensor", "shard"),
        ),
        check_vma=False,
    )
```

profile of v0, /device:TPU:10, one launch (start us, length us, event | category | flops | bytes accessed | tf_op | source)
XLA Modules:
  0.0 524.4 jit_solution(13802184867258133490)
XLA Ops:
  8.0 0.0 copy-start
  8.0 0.0 reduce-scatter.2.cloned.1.call-start
  8.1 11.9 %bitcast_subtract_fusion.2 = f32[1024,2048]{1,0:T(8,128)} fusion(f32[1024,2048]{1,0:T(8,128)} %param.10, f32[1,1024,2048]{2,1,0:T(8,128)} %param.11), kind=kLoop, calls=%fused_computation.2 | loop fusion | flops 2097152 | bytes 25165824 | tf_op jit(solution)/shard_map/sub | solution.py:35
  20.0 0.0 reduce-scatter.2.cloned.1.call-update
  20.0 0.0 all-reduce.3.cloned.1.call-start
  20.0 11.7 %fusion.1 = f32[64,4096]{0,1:T(8,128)} fusion(f32[64,512]{1,0:T(8,128)S(1)} %copy-done, f32[4096,512]{1,0:T(8,128)} %param.16, f32[1,4096,512]{2,1,0:T(8,128)} %param.17), kind=kOutput, calls=%fused_computation.5 | convolution fusion | flops 1612709888 | bytes 17956864 | tf_op jit(solution)/shard_map/dot_general | solution.py:38
  31.8 0.0 all-reduce.3.cloned.1.call-update
  31.8 0.0 all-gather.3.cloned.1.call-start
  31.9 0.0 copy-start.4
  31.9 0.0 copy-start.1
  31.9 0.0 copy-start.2
  31.9 0.0 copy-start.3
  31.9 175.3 %reduce-scatter.2.cloned.1.call-done = f32[512,2048]{1,0:T(8,128)} async-done(((f32[1024,2048]{1,0:T(8,128)}), f32[512,2048]{1,0:T(8,128)}) %reduce-scatter.2.cloned.1.call-update) | async-done | bytes 4194320 | tf_op jit(solution)/shard_map/reduce_scatter | solution.py:42
  207.2 10.5 %multiply_subtract_fusion.1 = (f32[512,2048]{1,0:T(8,128)}, f32[512,2048]{1,0:T(8,128)}) fusion(f32[1024,2048]{1,0:T(8,128)} %param.10, s32[]{:T(128)S(6)} %select_n.6, f32[512,2048]{1,0:T(8,128)} %reduce-scatter.2.cloned.1.call-done, f32[512,2048]{1,0:T(8,128)} %param.12), kind=kLoop, calls=%fused_computation.6 | loop fusion | flops 7340032 | bytes 20971524 | tf_op jit(solution)/shard_map/sub | solution.py:11
  217.7 0.0 all-gather.3.cloned.1.call-update
  217.8 0.6 dynamic-slice
  218.4 0.0 copy-done.1
  218.4 7.5 %all-reduce = f32[2,256]{1,0:T(2,128)S(1)} all-reduce(f32[2,256]{1,0:T(2,128)S(1)} %bitcast_subtract_fusion.5), channel_id=3, replica_groups=mesh['group'=2,'shard'=8,'tensor'=2] {'group'}, use_global_device_ids=true, to_apply=%region_1.0.clone | all-reduce | flops 512 | bytes 4096
  225.9 1.2 subtract_bitcast_fusion
  227.1 5.3 %all-gather = f32[2,1,256]{2,1,0:T(1,128)S(1)} all-gather(f32[1,1,256]{2,1,0:T(1,128)S(1)} %get-tuple-element.8), channel_id=1, replica_groups=mesh['group'=2,'shard'=8,'tensor'=2] {'group'}, dimensions={0}, use_global_device_ids=true | all-gather | bytes 3072 | tf_op jit(solution)/shard_map/all_gather | solution.py:54
  232.4 0.6 copy.18
  233.0 260.9 %all-reduce.3.cloned.1.call-done = f32[64,4096]{0,1:T(8,128)} async-done(((f32[64,4096]{0,1:T(8,128)}), f32[64,4096]{0,1:T(8,128)}) %all-reduce.3.cloned.1.call-update) | async-done | bytes 1048592 | tf_op jit(solution)/shard_map/psum | solution.py:45
  493.9 15.2 %multiply_subtract_fusion = (f32[4096,512]{1,0:T(8,128)}, f32[4096,512]{1,0:T(8,128)}) fusion(f32[4096,512]{1,0:T(8,128)} %param.16, f32[4096,512]{1,0:T(8,128)} %param.18, f32[64,512]{1,0:T(8,128)S(1)} %copy-done, f32[64,4096]{0,1:T(8,128)} %all-reduce.3.cloned.1.call-done), kind=kOutput, calls=%fused_computation.3 | convolution fusion | flops 1623457792 | bytes 34734080 | tf_op jit(solution)/shard_map/dot_general | solution.py:16
  509.1 7.9 %copy.21 = f32[1024,2048]{1,0:T(8,128)} copy(f32[1024,2048]{1,0:T(8,128)} %all-gather.3.cloned.1.call-done) | data formatting | bytes 16777216
  (6 shorter events, 0.0 us)
Async XLA Ops:
  8.0 12.0 %copy-start = (f32[64,512]{1,0:T(8,128)S(1)}, f32[64,512]{1,0:T(8,128)}, u32[]{:S(2)}) copy-start(f32[64,512]{1,0:T(8,128)} %param.19) | copy-start | bytes 393220
  8.0 199.2 %reduce-scatter.2.cloned.1.call-start = ((), (), s32[]{:S(2)}) async-start(), calls=%async_computation.1 | async-start | bytes 12582912 | tf_op jit(solution)/shard_map/reduce_scatter | solution.py:42
  20.0 473.9 %all-reduce.3.cloned.1.call-start = ((), (), s32[]{:S(2)}) async-start(), calls=%async_computation.3 | async-start | bytes 4194304 | tf_op jit(solution)/shard_map/psum | solution.py:45
  31.8 477.2 %all-gather.3.cloned.1.call-start = ((), (), s32[]{:S(2)}) async-start(), calls=%async_computation.2 | async-start | bytes 12582912 | tf_op jit(solution)/shard_map/all_gather | solution.py:53
  31.9 185.9 %copy-start.4 = (u32[32]{0:T(128)S(1)}, u32[32]{0:T(128)}, u32[]{:S(2)}) copy-start(u32[32]{0:T(128)} %constant.35) | copy-start | bytes 388
  31.9 186.5 %copy-start.1 = (f32[2,256]{1,0:T(2,128)S(1)}, f32[2,256]{1,0:T(2,128)}, u32[]{:S(2)}) copy-start(f32[2,256]{1,0:T(2,128)} %param.13) | copy-start | bytes 6148
  31.9 186.5 %copy-start.2 = (f32[1,2,256]{2,1,0:T(2,128)S(1)}, f32[1,2,256]{2,1,0:T(2,128)}, u32[]{:S(2)}) copy-start(f32[1,2,256]{2,1,0:T(2,128)} %param.14) | copy-start | bytes 6148
  31.9 194.0 %copy-start.3 = (f32[1,256]{1,0:T(1,128)S(1)}, f32[1,256]{1,0:T(1,128)}, u32[]{:S(2)}) copy-start(f32[1,256]{1,0:T(1,128)} %param.15) | copy-start | bytes 3076
Sparse Core Ops, SparseCore 0:
  20.1 187.0 reduce-scatter.1
  217.9 199.2 all-gather.2
Sparse Core Ops, SparseCore 1:
  31.9 461.9 all-reduce.2
where the time goes:
time: 530 us; the launch traced here: 524 us
  waiting for transfers between devices  436 us (82%)
  matrix products  26.9 us (5%)
  other arithmetic  23.6 us (4%)
  between operations  15.6 us (3%)
  blocking collectives  12.8 us (2%)
  local copies, waits for them, and re-layouts  9.09 us (2%)
    psum x1, waiting for transfers between devices, body(): factors = lax.psum(partial_factors, ('group', 'shard')) / groups  261 us
    reduce_scatter x1, waiting for transfers between devices, body(): lax.psum_scatter(down_diff, 'group', scatter_dimension=0, tiled=True)  175 us
    dot_general x1, matrix products, rebuild(): lax.dot_general(factors, factor_basis, (((0,), (0,)), ((), ())), precisio...  15.2 us
    sub x1, other arithmetic, body(): down_diff = down_anchor - down_local[0]  11.9 us
    dot_general x1, matrix products, body(): lax.dot_general(factor_basis, gate_diff, (((1,), (1,)), ((), ())), precis...  11.7 us
  transfers between devices with their start and end apart: 3, of which 2 were waited for; matrix products, arithmetic and copies ran while one was open for 8% of the time, Pallas kernels for 0%

commit v1 on v0

--- a/solution.py
+++ b/solution.py
@@ -4,6 +4,7 @@
 
 outer_rate = 0.7
 momentum = 0.9
+chunks = 8
 
 
 def advance(anchor, moment, delta):
@@ -16,6 +17,45 @@
     return lax.dot_general(
         factors, factor_basis, (((0,), (0,)), ((), ())), precision=lax.Precision.HIGHEST
     )
+
+
+def rows_of(array, start, size):
+    return lax.dynamic_slice_in_dim(array, start, size, 0)
+
+
+def swap(array):
+    return lax.ppermute(array, "group", [(0, 1), (1, 0)])
+
+
+def exchange(anchor, local, moment, parts):
+    a = outer_rate * (1 + momentum)
+    b = outer_rate * momentum * momentum
+    group_index = lax.axis_index("group")
+    half = moment.shape[0]
+    size = half // parts
+    own = group_index * half
+    other = half - own
+    own_local = rows_of(local, own, half)
+    mixed = (a / 2) * own_local - b * moment
+    received = [swap(rows_of(local, other + i * size, size)) for i in range(parts)]
+    mixed_received = [swap(mixed[i * size : (i + 1) * size]) for i in range(parts)]
+    anchor_next = (1 - a) * anchor + (a / 2) * local
+    moment_next = []
+    for i, piece in enumerate(received):
+        start = own + i * size
+        old = moment[i * size : (i + 1) * size]
+        moment_next.append(
+            momentum * old
+            + rows_of(anchor, start, size)
+            - 0.5 * (rows_of(local, start, size) + piece)
+        )
+        value = rows_of(anchor_next, start, size) + ((a / 2) * piece - b * old)
+        anchor_next = lax.dynamic_update_slice_in_dim(anchor_next, value, start, 0)
+    for i, piece in enumerate(mixed_received):
+        start = other + i * size
+        value = rows_of(anchor_next, start, size) + piece
+        anchor_next = lax.dynamic_update_slice_in_dim(anchor_next, value, start, 0)
+    return anchor_next, lax.concatenate(moment_next, 0)
 
 
 def body(
@@ -31,28 +71,15 @@
     factor_basis,
 ):
     groups = lax.axis_size("group")
-    group_index = lax.axis_index("group")
-    down_diff = down_anchor - down_local[0]
-    norm_diff = norm_anchor - norm_local[0]
     gate_diff = gate_anchor - gate_local[0]
     partial_factors = lax.dot_general(
         factor_basis, gate_diff, (((1,), (1,)), ((), ())), precision=lax.Precision.HIGHEST
     )
-    down_sum, norm_sum = (
-        lax.psum_scatter(down_diff, "group", scatter_dimension=0, tiled=True),
-        lax.psum_scatter(norm_diff, "group", scatter_dimension=0, tiled=True),
-    )
-    factors = lax.psum(partial_factors, ("group", "shard")) / groups
-    half_rows = down_sum.shape[0]
-    norm_rows = norm_sum.shape[0]
-    down_piece = lax.dynamic_slice_in_dim(down_anchor, group_index * half_rows, half_rows, 0)
-    norm_piece = lax.dynamic_slice_in_dim(norm_anchor, group_index * norm_rows, norm_rows, 0)
-    down_next, new_down_moment = advance(down_piece, down_moment, down_sum / groups)
-    norm_next, new_norm_moment = advance(norm_piece, norm_moment, norm_sum / groups)
-    new_down_anchor, new_norm_anchor = (
-        lax.all_gather(down_next, "group", axis=0, tiled=True),
-        lax.all_gather(norm_next, "group", axis=0, tiled=True),
-    )
+    piece = lax.psum_scatter(partial_factors, "shard", scatter_dimension=0, tiled=True)
+    piece = (piece + swap(piece)) / groups
+    factors = lax.all_gather(piece, "shard", axis=0, tiled=True)
+    new_down_anchor, new_down_moment = exchange(down_anchor, down_local[0], down_moment, chunks)
+    new_norm_anchor, new_norm_moment = exchange(norm_anchor, norm_local[0], norm_moment, 1)
     gate_delta = rebuild(factors, factor_basis)
     new_gate_anchor, new_gate_moment = advance(gate_anchor, gate_moment, gate_delta)
     return (

time: 530 us -> 435 us (0.82)
  waiting for transfers between devices: 436 us -> 282 us
  starting transfers between devices: 0.12 us -> 47.6 us
  other arithmetic: 23.6 us -> 54.9 us
  blocking collectives: 12.8 us -> 0 us
    ppermute x0 -> x19, waiting for transfers between devices: none -> 265 us  [swap(): return lax.ppermute(array, 'group', [(0, 1), (1, 0)])]
    psum x1 -> x0, waiting for transfers between devices: 261 us -> none  [body(): factors = lax.psum(partial_factors, ('group', 'shard')) / groups]
    reduce_scatter x1, waiting for transfers between devices: 175 us -> 0.01 us  [body(): lax.psum_scatter(partial_factors, 'shard', scatter_dimension=0, tiled=True)]
    ppermute x0 -> x19, starting transfers between devices: none -> 47.5 us  [swap(): return lax.ppermute(array, 'group', [(0, 1), (1, 0)])]
    sub x3 -> x2, other arithmetic: 22.4 us -> 5 us  [the longest x1 4.42 us: exchange(): mixed = a / 2 * own_local - b * moment]
    all_gather x1, waiting for transfers between devices: 0.01 us -> 17.4 us  [body(): factors = lax.all_gather(piece, 'shard', axis=0, tiled=True)]
    unnamed x1 -> x7, other arithmetic: 1.22 us -> 17.9 us
    dynamic_update_slice x0 -> x8, other arithmetic: none -> 15.8 us  [exchange(): anchor_next = lax.dynamic_update_slice_in_dim(anchor_next, value, start, 0)]
  transfers between devices with their start and end apart: 3 -> 21, of which waited for: 2 -> 12; matrix products, arithmetic and copies ran while one was open for 8% -> 16% of each run, Pallas kernels for 0% -> 0%
where the time goes in v1:
time: 435 us; the launch traced here: 433 us
  waiting for transfers between devices  282 us (65%)
  other arithmetic  54.9 us (13%)
  starting transfers between devices  47.6 us (11%)
  matrix products  28.6 us (7%)
  between operations  14.2 us (3%)
  local copies, waits for them, and re-layouts  5.79 us (1%)
    ppermute x19, waiting for transfers between devices, swap(): return lax.ppermute(array, 'group', [(0, 1), (1, 0)])  265 us
    ppermute x19, starting transfers between devices, swap(): return lax.ppermute(array, 'group', [(0, 1), (1, 0)])  47.5 us
    unnamed x7, other arithmetic  17.9 us
    all_gather x1, waiting for transfers between devices, body(): factors = lax.all_gather(piece, 'shard', axis=0, tiled=True)  17.4 us
    dynamic_update_slice x8, other arithmetic, exchange(): anchor_next = lax.dynamic_update_slice_in_dim(anchor_next, value, start, 0)  15.8 us
    dot_general x1, matrix products, rebuild(): lax.dot_general(factors, factor_basis, (((0,), (0,)), ((), ())), precisio...  15.5 us
    dot_general x1, matrix products, body(): lax.dot_general(factor_basis, gate_diff, (((1,), (1,)), ((), ())), precis...  13.1 us
    add x2, other arithmetic, exchange(): anchor_next = (1 - a) * anchor + a / 2 * local  12.2 us
  transfers between devices with their start and end apart: 21, of which 12 were waited for; matrix products, arithmetic and copies ran while one was open for 16% of the time, Pallas kernels for 0%

profile of v1, /device:TPU:10, one launch (start us, length us, event | category | flops | bytes accessed | tf_op | source)
XLA Modules:
  0.0 433.2 jit_solution(12502611562935426959)
XLA Ops:
  7.2 4.2 dynamic-slice_bitcast_fusion
  20.0 13.1 %fusion.1 = f32[64,4096]{1,0:T(8,128)} fusion(f32[64,512]{1,0:T(8,128)S(1)} %copy-done, f32[4096,512]{1,0:T(8,128)} %param.16, f32[1,4096,512]{2,1,0:T(8,128)} %param.17), kind=kOutput, calls=%fused_computation.5 | convolution fusion | flops 1612709888 | bytes 17956864 | tf_op jit(solution)/shard_map/dot_general | solution.py:75
  33.2 12.2 %bitcast_add_fusion = f32[1024,2048]{1,0:T(8,128)} fusion(f32[1,1024,2048]{2,1,0:T(8,128)} %param.11, f32[1024,2048]{1,0:T(8,128)} %param.10), kind=kLoop, calls=%fused_computation.2 | loop fusion | flops 6291456 | bytes 25165824 | tf_op jit(solution)/shard_map/add | solution.py:42
  45.4 4.4 %bitcast_subtract_fusion.4 = f32[512,2048]{1,0:T(8,128)S(1)} fusion(f32[512,2048]{1,0:T(8,128)} %param.12, f32[1,1024,2048]{2,1,0:T(8,128)} %param.11, s32[]{:T(128)S(6)} %select_n.36), kind=kLoop, calls=%fused_computation.6 | loop fusion | flops 3145728 | bytes 12582916 | tf_op jit(solution)/shard_map/sub | solution.py:39
  51.1 53.0 %collective-permute-done.16 = f32[1,256]{1,0:T(1,128)S(1)} collective-permute-done((f32[1,256]{1,0:T(1,128)S(1)}, f32[1,256]{1,0:T(1,128)S(1)}, u32[]{:S(2)}, u32[]{:S(2)}) %collective-permute-start.16) | collective-permute-done | bytes 1056 | tf_op jit(solution)/shard_map/ppermute | solution.py:27
  104.7 3.4 collective-permute-start.17
  129.4 46.7 %collective-permute-done.4 = f32[64,2048]{1,0:T(8,128)} collective-permute-done((f32[64,2048]{1,0:T(8,128)}, f32[64,2048]{1,0:T(8,128)}, u32[]{:S(2)}, u32[]{:S(2)}) %collective-permute-start.4) | collective-permute-done | bytes 524320 | tf_op jit(solution)/shard_map/ppermute | solution.py:27
  176.0 3.4 collective-permute-start.9
  181.9 16.6 %collective-permute-done.5 = f32[64,2048]{1,0:T(8,128)S(1)} collective-permute-done((f32[64,2048]{1,0:T(8,128)}, f32[64,2048]{1,0:T(8,128)S(1)}, u32[]{:S(2)}, u32[]{:S(2)}) %collective-permute-start.5) | collective-permute-done | bytes 524320 | tf_op jit(solution)/shard_map/ppermute | solution.py:27
  198.5 3.3 collective-permute-start.10
  204.2 16.8 %collective-permute-done.6 = f32[64,2048]{1,0:T(8,128)S(1)} collective-permute-done((f32[64,2048]{1,0:T(8,128)}, f32[64,2048]{1,0:T(8,128)S(1)}, u32[]{:S(2)}, u32[]{:S(2)}) %collective-permute-start.6) | collective-permute-done | bytes 524320 | tf_op jit(solution)/shard_map/ppermute | solution.py:27
  221.0 3.3 collective-permute-start.11
  226.6 16.8 %collective-permute-done.7 = f32[64,2048]{1,0:T(8,128)S(1)} collective-permute-done((f32[64,2048]{1,0:T(8,128)}, f32[64,2048]{1,0:T(8,128)S(1)}, u32[]{:S(2)}, u32[]{:S(2)}) %collective-permute-start.7) | collective-permute-done | bytes 524320 | tf_op jit(solution)/shard_map/ppermute | solution.py:27
  249.1 16.7 %collective-permute-done.8 = f32[64,2048]{1,0:T(8,128)S(1)} collective-permute-done((f32[64,2048]{1,0:T(8,128)S(1)}, f32[64,2048]{1,0:T(8,128)S(1)}, u32[]{:S(2)}, u32[]{:S(2)}) %collective-permute-start.8) | collective-permute-done | bytes 524320 | tf_op jit(solution)/shard_map/ppermute | solution.py:27
  265.8 3.4 collective-permute-start.13
  271.1 17.2 %collective-permute-done.9 = f32[64,2048]{1,0:T(8,128)S(1)} collective-permute-done((f32[64,2048]{1,0:T(8,128)S(1)}, f32[64,2048]{1,0:T(8,128)S(1)}, u32[]{:S(2)}, u32[]{:S(2)}) %collective-permute-start.9) | collective-permute-done | bytes 524320 | tf_op jit(solution)/shard_map/ppermute | solution.py:27
  288.3 3.4 collective-permute-start.14
  293.6 17.2 %collective-permute-done.10 = f32[64,2048]{1,0:T(8,128)S(1)} collective-permute-done((f32[64,2048]{1,0:T(8,128)S(1)}, f32[64,2048]{1,0:T(8,128)S(1)}, u32[]{:S(2)}, u32[]{:S(2)}) %collective-permute-start.10) | collective-permute-done | bytes 524320 | tf_op jit(solution)/shard_map/ppermute | solution.py:27
  310.7 3.4 collective-permute-start.15
  316.0 17.2 %collective-permute-done.11 = f32[64,2048]{1,0:T(8,128)} collective-permute-done((f32[64,2048]{1,0:T(8,128)S(1)}, f32[64,2048]{1,0:T(8,128)}, u32[]{:S(2)}, u32[]{:S(2)}) %collective-permute-start.11) | collective-permute-done | bytes 524320 | tf_op jit(solution)/shard_map/ppermute | solution.py:27
  333.2 3.5 collective-permute-start.18
  338.8 45.0 %collective-permute-done.18 = f32[8,4096]{1,0:T(8,128)S(1)} collective-permute-done((f32[8,4096]{1,0:T(8,128)}, f32[8,4096]{1,0:T(8,128)S(1)}, u32[]{:S(2)}, u32[]{:S(2)}) %collective-permute-start.18) | collective-permute-done | bytes 131104 | tf_op jit(solution)/shard_map/ppermute | solution.py:27
  393.5 17.4 %all-gather.2.cloned.1.call-done = f32[64,4096]{1,0:T(8,128)} async-done(((f32[8,4096]{1,0:T(8,128)}), f32[64,4096]{1,0:T(8,128)}) %all-gather.2.cloned.1.call-update) | async-done | bytes 1048592 | tf_op jit(solution)/shard_map/all_gather | solution.py:80
  410.9 15.5 %multiply_subtract_fusion = (f32[4096,512]{1,0:T(8,128)}, f32[4096,512]{1,0:T(8,128)}) fusion(f32[4096,512]{1,0:T(8,128)} %param.16, f32[4096,512]{1,0:T(8,128)} %param.18, f32[64,4096]{1,0:T(8,128)} %all-gather.2.cloned.1.call-done, f32[64,512]{1,0:T(8,128)S(1)} %copy-done), kind=kOutput, calls=%fused_computation.3 | convolution fusion | flops 1623195648 | bytes 34734080 | tf_op jit(solution)/shard_map/dot_general | solution.py:17
  (67 shorter events, 62.1 us)
Async XLA Ops:
  7.2 326.0 %reduce-scatter.2.cloned.1.call-start = ((), (), s32[]{:S(2)}) async-start(), calls=%async_computation.1 | async-start | bytes 1179648 | tf_op jit(solution)/shard_map/reduce_scatter | solution.py:78
  11.5 101.4 %collective-permute-start = (f32[64,2048]{1,0:T(8,128)}, f32[64,2048]{1,0:T(8,128)}, u32[]{:S(2)}, u32[]{:S(2)}) collective-permute-start(f32[64,2048]{1,0:T(8,128)} %get-tuple-element.15), channel_id=1, source_target_pairs={{0,16},{16,0},{1,17},{17,1},{2,18},{18,2},{3,19},{19,3},{4,20},{20... | collective-permute-start | bytes 1572872 | tf_op jit(solution)/shard_map/ppermute | solution.py:27
  14.1 101.8 %collective-permute-start.1 = (f32[64,2048]{1,0:T(8,128)}, f32[64,2048]{1,0:T(8,128)}, u32[]{:S(2)}, u32[]{:S(2)}) collective-permute-start(f32[64,2048]{1,0:T(8,128)} %get-tuple-element.14), channel_id=1, source_target_pairs={{0,16},{16,0},{1,17},{17,1},{2,18},{18,2},{3,19},{19,3},{4,20},{20... | collective-permute-start | bytes 1572872 | tf_op jit(solution)/shard_map/ppermute | solution.py:27
  14.4 106.8 %collective-permute-start.2 = (f32[64,2048]{1,0:T(8,128)}, f32[64,2048]{1,0:T(8,128)}, u32[]{:S(2)}, u32[]{:S(2)}) collective-permute-start(f32[64,2048]{1,0:T(8,128)} %get-tuple-element.13), channel_id=1, source_target_pairs={{0,16},{16,0},{1,17},{17,1},{2,18},{18,2},{3,19},{19,3},{4,20},{20... | collective-permute-start | bytes 1572872 | tf_op jit(solution)/shard_map/ppermute | solution.py:27
  17.0 107.1 %collective-permute-start.3 = (f32[64,2048]{1,0:T(8,128)}, f32[64,2048]{1,0:T(8,128)}, u32[]{:S(2)}, u32[]{:S(2)}) collective-permute-start(f32[64,2048]{1,0:T(8,128)} %get-tuple-element.12), channel_id=1, source_target_pairs={{0,16},{16,0},{1,17},{17,1},{2,18},{18,2},{3,19},{19,3},{4,20},{20... | collective-permute-start | bytes 1572872 | tf_op jit(solution)/shard_map/ppermute | solution.py:27
  17.3 86.8 %collective-permute-start.16 = (f32[1,256]{1,0:T(1,128)S(1)}, f32[1,256]{1,0:T(1,128)S(1)}, u32[]{:S(2)}, u32[]{:S(2)}) collective-permute-start(f32[1,256]{1,0:T(1,128)S(1)} %fusion.26), channel_id=1, source_target_pairs={{0,16},{16,0},{1,17},{17,1},{2,18},{18,2},{3,19},{19,3},{4,20},{20... | collective-permute-start | bytes 3080 | tf_op jit(solution)/shard_map/ppermute | solution.py:27
  33.1 377.7 %all-gather.2.cloned.1.call-start = ((), (), s32[]{:S(2)}) async-start(), calls=%async_computation.2 | async-start | bytes 1179648 | tf_op jit(solution)/shard_map/all_gather | solution.py:80
  104.7 4.9 %collective-permute-start.17 = (f32[1,256]{1,0:T(1,128)S(1)}, f32[1,256]{1,0:T(1,128)S(1)}, u32[]{:S(2)}, u32[]{:S(2)}) collective-permute-start(f32[1,256]{1,0:T(1,128)S(1)} %get-tuple-element.41), channel_id=1, source_target_pairs={{0,16},{16,0},{1,17},{17,1},{2,18},{18,2},{3,19},{19,3},{4,20},{20... | collective-permute-start | bytes 3080 | tf_op jit(solution)/shard_map/ppermute | solution.py:27
  109.6 66.4 %collective-permute-start.4 = (f32[64,2048]{1,0:T(8,128)}, f32[64,2048]{1,0:T(8,128)}, u32[]{:S(2)}, u32[]{:S(2)}) collective-permute-start(f32[64,2048]{1,0:T(8,128)} %get-tuple-element.11), channel_id=1, source_target_pairs={{0,16},{16,0},{1,17},{17,1},{2,18},{18,2},{3,19},{19,3},{4,20},{20... | collective-permute-start | bytes 1572872 | tf_op jit(solution)/shard_map/ppermute | solution.py:27
  112.9 69.1 %copy-start.6 = (f32[2,256]{1,0:T(2,128)}, f32[2,256]{1,0:T(2,128)S(1)}, u32[]{:S(2)}) copy-start(f32[2,256]{1,0:T(2,128)S(1)} %dynamic_update_slice.71) | copy-start | bytes 6148
  112.9 63.1 %copy-start.2 = (f32[64,2048]{1,0:T(8,128)S(1)}, f32[64,2048]{1,0:T(8,128)}, u32[]{:S(2)}) copy-start(f32[64,2048]{1,0:T(8,128)} %get-tuple-element.38) | copy-start | bytes 1572868
  112.9 85.6 %collective-permute-start.5 = (f32[64,2048]{1,0:T(8,128)}, f32[64,2048]{1,0:T(8,128)S(1)}, u32[]{:S(2)}, u32[]{:S(2)}) collective-permute-start(f32[64,2048]{1,0:T(8,128)} %get-tuple-element.10), channel_id=1, source_target_pairs={{0,16},{16,0},{1,17},{17,1},{2,18},{18,2},{3,19},{19,3},{4,20},{20... | collective-permute-start | bytes 1572872 | tf_op jit(solution)/shard_map/ppermute | solution.py:27
  115.8 105.1 %collective-permute-start.6 = (f32[64,2048]{1,0:T(8,128)}, f32[64,2048]{1,0:T(8,128)S(1)}, u32[]{:S(2)}, u32[]{:S(2)}) collective-permute-start(f32[64,2048]{1,0:T(8,128)} %get-tuple-element.9), channel_id=1, source_target_pairs={{0,16},{16,0},{1,17},{17,1},{2,18},{18,2},{3,19},{19,3},{4,20},{20... | collective-permute-start | bytes 1572872 | tf_op jit(solution)/shard_map/ppermute | solution.py:27
  121.2 122.2 %collective-permute-start.7 = (f32[64,2048]{1,0:T(8,128)}, f32[64,2048]{1,0:T(8,128)S(1)}, u32[]{:S(2)}, u32[]{:S(2)}) collective-permute-start(f32[64,2048]{1,0:T(8,128)} %get-tuple-element.8), channel_id=1, source_target_pairs={{0,16},{16,0},{1,17},{17,1},{2,18},{18,2},{3,19},{19,3},{4,20},{20... | collective-permute-start | bytes 1572872 | tf_op jit(solution)/shard_map/ppermute | solution.py:27
  124.1 141.7 %collective-permute-start.8 = (f32[64,2048]{1,0:T(8,128)S(1)}, f32[64,2048]{1,0:T(8,128)S(1)}, u32[]{:S(2)}, u32[]{:S(2)}) collective-permute-start(f32[64,2048]{1,0:T(8,128)S(1)} %copy-done.3), channel_id=1, source_target_pairs={{0,16},{16,0},{1,17},{17,1},{2,18},{18,2},{3,19},{19,3},{4,20},{20... | collective-permute-start | bytes 1572872 | tf_op jit(solution)/shard_map/ppermute | solution.py:27
  176.0 112.2 %collective-permute-start.9 = (f32[64,2048]{1,0:T(8,128)S(1)}, f32[64,2048]{1,0:T(8,128)S(1)}, u32[]{:S(2)}, u32[]{:S(2)}) collective-permute-start(f32[64,2048]{1,0:T(8,128)S(1)} %copy-done.2), channel_id=1, source_target_pairs={{0,16},{16,0},{1,17},{17,1},{2,18},{18,2},{3,19},{19,3},{4,20},{20... | collective-permute-start | bytes 1572872 | tf_op jit(solution)/shard_map/ppermute | solution.py:27
  198.5 112.2 %collective-permute-start.10 = (f32[64,2048]{1,0:T(8,128)S(1)}, f32[64,2048]{1,0:T(8,128)S(1)}, u32[]{:S(2)}, u32[]{:S(2)}) collective-permute-start(f32[64,2048]{1,0:T(8,128)S(1)} %get-tuple-element.37), channel_id=1, source_target_pairs={{0,16},{16,0},{1,17},{17,1},{2,18},{18,2},{3,19},{19,3},{4,20},{20... | collective-permute-start | bytes 1572872 | tf_op jit(solution)/shard_map/ppermute | solution.py:27
  221.0 112.2 %collective-permute-start.11 = (f32[64,2048]{1,0:T(8,128)S(1)}, f32[64,2048]{1,0:T(8,128)}, u32[]{:S(2)}, u32[]{:S(2)}) collective-permute-start(f32[64,2048]{1,0:T(8,128)S(1)} %get-tuple-element.36), channel_id=1, source_target_pairs={{0,16},{16,0},{1,17},{17,1},{2,18},{18,2},{3,19},{19,3},{4,20},{20... | collective-permute-start | bytes 1572872 | tf_op jit(solution)/shard_map/ppermute | solution.py:27
  243.4 142.0 %collective-permute-start.12 = (f32[64,2048]{1,0:T(8,128)S(1)}, f32[64,2048]{1,0:T(8,128)}, u32[]{:S(2)}, u32[]{:S(2)}) collective-permute-start(f32[64,2048]{1,0:T(8,128)S(1)} %get-tuple-element.35), channel_id=1, source_target_pairs={{0,16},{16,0},{1,17},{17,1},{2,18},{18,2},{3,19},{19,3},{4,20},{20... | collective-permute-start | bytes 1572872 | tf_op jit(solution)/shard_map/ppermute | solution.py:27
  249.1 66.9 %copy-start.4 = (f32[512,2048]{1,0:T(8,128)}, f32[512,2048]{1,0:T(8,128)S(1)}, u32[]{:S(2)}) copy-start(f32[512,2048]{1,0:T(8,128)S(1)} %get-tuple-element.16) | copy-start | bytes 12582916
  265.8 121.7 %collective-permute-start.13 = (f32[64,2048]{1,0:T(8,128)S(1)}, f32[64,2048]{1,0:T(8,128)}, u32[]{:S(2)}, u32[]{:S(2)}) collective-permute-start(f32[64,2048]{1,0:T(8,128)S(1)} %get-tuple-element.34), channel_id=1, source_target_pairs={{0,16},{16,0},{1,17},{17,1},{2,18},{18,2},{3,19},{19,3},{4,20},{20... | collective-permute-start | bytes 1572872 | tf_op jit(solution)/shard_map/ppermute | solution.py:27
  288.3 101.2 %collective-permute-start.14 = (f32[64,2048]{1,0:T(8,128)S(1)}, f32[64,2048]{1,0:T(8,128)}, u32[]{:S(2)}, u32[]{:S(2)}) collective-permute-start(f32[64,2048]{1,0:T(8,128)S(1)} %get-tuple-element.33), channel_id=1, source_target_pairs={{0,16},{16,0},{1,17},{17,1},{2,18},{18,2},{3,19},{19,3},{4,20},{20... | collective-permute-start | bytes 1572872 | tf_op jit(solution)/shard_map/ppermute | solution.py:27
  310.7 80.8 %collective-permute-start.15 = (f32[64,2048]{1,0:T(8,128)S(1)}, f32[64,2048]{1,0:T(8,128)S(1)}, u32[]{:S(2)}, u32[]{:S(2)}) collective-permute-start(f32[64,2048]{1,0:T(8,128)S(1)} %get-tuple-element.32), channel_id=1, source_target_pairs={{0,16},{16,0},{1,17},{17,1},{2,18},{18,2},{3,19},{19,3},{4,20},{20... | collective-permute-start | bytes 1572872 | tf_op jit(solution)/shard_map/ppermute | solution.py:27
  333.2 50.6 %collective-permute-start.18 = (f32[8,4096]{1,0:T(8,128)}, f32[8,4096]{1,0:T(8,128)S(1)}, u32[]{:S(2)}, u32[]{:S(2)}) collective-permute-start(f32[8,4096]{1,0:T(8,128)} %reduce-scatter.2.cloned.1.call-done), channel_id=1, source_target_pairs={{0,16},{16,0},{1,17},{17,1},{2,18},{18,2},{3,19},{19,3},{4,20},{20... | collective-permute-start | bytes 393224 | tf_op jit(solution)/shard_map/ppermute | solution.py:27
  (6 other events, 112.5 us)
Sparse Core Ops, SparseCore 0:
  33.3 35.1 reduce-scatter.1
  385.5 25.2 all-gather.1

commit v2 on v0

v2 whole, which is shorter than its diff:
```python
import jax
import jax.numpy as jnp
from jax import lax
from jax.sharding import PartitionSpec as P

outer_rate = 0.7
momentum = 0.9
rate = outer_rate * (1 + momentum)
decay = outer_rate * momentum * momentum
first_sizes = (1, 1, 2, 4, 4, 4, 4, 4, 4, 4)
last_sizes = (4, 4, 4, 4, 4, 4, 4, 2, 1, 1)
after_scatter = 8
after_swap = 3
after_gate = 5


def advance(anchor, moment, delta):
    moment_next = momentum * moment + delta
    anchor_next = anchor - outer_rate * (delta + momentum * moment_next)
    return (anchor_next, moment_next)


def rebuild(factors, factor_basis):
    return lax.dot_general(
        factors, factor_basis, (((0,), (0,)), ((), ())), precision=lax.Precision.HIGHEST
    )


def swap(array):
    return lax.ppermute(array, "group", [(0, 1), (1, 0)])


def after(array, *earlier):
    return lax.optimization_barrier((array, *earlier))[0]


def pieces(half, sizes):
    unit = half // sum(sizes)
    start = 0
    for size in sizes:
        yield start * unit, size * unit
        start += size


def exchange_whole(anchor, local, moment):
    group_index = lax.axis_index("group")
    half = moment.shape[0]
    mine = lax.broadcasted_iota(jnp.int32, anchor.shape, 0) // half == group_index
    wide = lax.concatenate([moment, moment], 0)
    mixed = (rate / 2) * local - decay * wide
    received = swap(jnp.where(mine, mixed, local))
    anchor_next = (1 - rate) * anchor + (rate / 2) * local
    anchor_next += jnp.where(mine, (rate / 2) * received - decay * wide, received)
    step = anchor - 0.5 * (local + received)
    moment_next = momentum * moment + lax.dynamic_slice_in_dim(step, group_index * half, half, 0)
    return anchor_next, moment_next


def body(
    down_anchor,
    down_local,
    down_moment,
    norm_anchor,
    norm_local,
    norm_moment,
    gate_anchor,
    gate_local,
    gate_moment,
    factor_basis,
):
    groups = lax.axis_size("group")
    group_index = lax.axis_index("group")
    local = down_local[0]
    half = down_moment.shape[0]
    own = group_index * half
    other = half - own

    def rows_of(array, start, size):
        return lax.dynamic_slice_in_dim(array, start, size, 0)

    spans = list(pieces(half, first_sizes))
    mixed_spans = list(pieces(half, last_sizes))
    sent = [rows_of(local, other + start, size) for start, size in spans]
    mixed = (rate / 2) * rows_of(local, own, half) - decay * down_moment
    mixed_sent = [mixed[start : start + size] for start, size in mixed_spans]

    gate_diff = gate_anchor - gate_local[0]
    partial_factors = lax.dot_general(
        factor_basis, gate_diff, (((1,), (1,)), ((), ())), precision=lax.Precision.HIGHEST
    )
    piece = lax.psum_scatter(partial_factors, "shard", scatter_dimension=0, tiled=True)
    sent[after_scatter] = after(sent[after_scatter], piece)
    piece_other = swap(piece)
    mixed_sent[after_swap] = after(mixed_sent[after_swap], piece_other)
    piece = (piece + piece_other) / groups
    factors = lax.all_gather(piece, "shard", axis=0, tiled=True)
    gate_delta = rebuild(factors, factor_basis)
    new_gate_anchor, new_gate_moment = advance(gate_anchor, gate_moment, gate_delta)
    mixed_sent[after_gate] = after(mixed_sent[after_gate], new_gate_anchor, new_gate_moment)

    received = [swap(part) for part in sent]
    new_norm_anchor, new_norm_moment = exchange_whole(norm_anchor, norm_local[0], norm_moment)
    mixed_received = [swap(part) for part in mixed_sent]

    anchor_next = (1 - rate) * down_anchor + (rate / 2) * local
    moment_next = []
    for (start, size), part in zip(spans, received):
        old = down_moment[start : start + size]
        moment_next.append(
            momentum * old
            + rows_of(down_anchor, own + start, size)
            - 0.5 * (rows_of(local, own + start, size) + part)
        )
        value = rows_of(anchor_next, own + start, size) + ((rate / 2) * part - decay * old)
        anchor_next = lax.dynamic_update_slice_in_dim(anchor_next, value, own + start, 0)
    for (start, size), part in zip(mixed_spans, mixed_received):
        value = rows_of(anchor_next, other + start, size) + part
        anchor_next = lax.dynamic_update_slice_in_dim(anchor_next, value, other + start, 0)
    return (
        anchor_next,
        lax.concatenate(moment_next, 0),
        new_norm_anchor,
        new_norm_moment,
        new_gate_anchor,
        new_gate_moment,
    )


def solution(mesh):
    placed = (
        P("shard", "tensor"),
        P("group", "shard", "tensor"),
        P(("shard", "group"), "tensor"),
        P(None, ("shard", "tensor")),
        P("group", None, ("shard", "tensor")),
        P("group", ("shard", "tensor")),
        P("tensor", "shard"),
        P("group", "tensor", "shard"),
        P("tensor", "shard"),
        P(None, "shard"),
    )
    return jax.shard_map(
        body,
        mesh=mesh,
        in_specs=placed,
        out_specs=(
            P("shard", "tensor"),
            P(("shard", "group"), "tensor"),
            P(None, ("shard", "tensor")),
            P("group", ("shard", "tensor")),
            P("tensor", "shard"),
            P("tensor", "shard"),
        ),
        check_vma=False,
    )
```

time: 530 us -> 405 us (0.76)
  waiting for transfers between devices: 436 us -> 236 us
  starting transfers between devices: 0.12 us -> 47.3 us
  other arithmetic: 23.6 us -> 63.6 us
  blocking collectives: 12.8 us -> 0 us
    psum x1 -> x0, waiting for transfers between devices: 261 us -> none  [body(): factors = lax.psum(partial_factors, ('group', 'shard')) / groups]
    ppermute x0 -> x22, waiting for transfers between devices: none -> 236 us  [swap(): return lax.ppermute(array, 'group', [(0, 1), (1, 0)])]
    reduce_scatter x1, waiting for transfers between devices: 175 us -> 0.01 us  [body(): lax.psum_scatter(partial_factors, 'shard', scatter_dimension=0, tiled=True)]
    ppermute x0 -> x22, starting transfers between devices: none -> 47.2 us  [swap(): return lax.ppermute(array, 'group', [(0, 1), (1, 0)])]
    unnamed x1 -> x9, other arithmetic: 1.22 us -> 21.7 us
    dynamic_update_slice x0 -> x10, other arithmetic: none -> 18.2 us  [body(): lax.dynamic_update_slice_in_dim(anchor_next, value, other + start, 0)]
    sub x3 -> x1, other arithmetic: 22.4 us -> 4.58 us  [body(): mixed = rate / 2 * rows_of(local, own, half) - decay * down_moment]
    add x0 -> x3, other arithmetic: none -> 13.3 us  [the longest x1 12.2 us: body(): anchor_next = (1 - rate) * down_anchor + rate / 2 * local]
  transfers between devices with their start and end apart: 3 -> 24, of which waited for: 2 -> 11; matrix products, arithmetic and copies ran while one was open for 8% -> 24% of each run, Pallas kernels for 0% -> 0%
where the time goes in v2:
time: 405 us; the launch traced here: 401 us
  waiting for transfers between devices  236 us (58%)
  other arithmetic  63.6 us (16%)
  starting transfers between devices  47.3 us (12%)
  matrix products  28.6 us (7%)
  between operations  14.1 us (3%)
  local copies, waits for them, and re-layouts  11.1 us (3%)
    ppermute x22, waiting for transfers between devices, swap(): return lax.ppermute(array, 'group', [(0, 1), (1, 0)])  236 us
    ppermute x22, starting transfers between devices, swap(): return lax.ppermute(array, 'group', [(0, 1), (1, 0)])  47.2 us
    unnamed x9, other arithmetic  21.7 us
    dynamic_update_slice x10, other arithmetic, body(): lax.dynamic_update_slice_in_dim(anchor_next, value, other + start, 0)  18.2 us
    dot_general x1, matrix products, rebuild(): lax.dot_general(factors, factor_basis, (((0,), (0,)), ((), ())), precisio...  15.5 us
    dot_general x1, matrix products, body(): lax.dot_general(factor_basis, gate_diff, (((1,), (1,)), ((), ())), precis...  13.1 us
    add x1, other arithmetic, body(): anchor_next = (1 - rate) * down_anchor + rate / 2 * local  12.2 us
  transfers between devices with their start and end apart: 24, of which 11 were waited for; matrix products, arithmetic and copies ran while one was open for 24% of the time, Pallas kernels for 0%

profile of v2, /device:TPU:10, one launch (start us, length us, event | category | flops | bytes accessed | tf_op | source)
XLA Modules:
  0.0 401.2 jit_solution(6374558566030841020)
XLA Ops:
  17.2 13.1 %fusion.1 = f32[64,4096]{1,0:T(8,128)} fusion(f32[64,512]{1,0:T(8,128)S(1)} %copy-done, f32[4096,512]{1,0:T(8,128)} %param.16, f32[1,4096,512]{2,1,0:T(8,128)} %param.17), kind=kOutput, calls=%fused_computation.5 | convolution fusion | flops 1612709888 | bytes 17956864 | tf_op jit(solution)/shard_map/dot_general | solution.py:88
  30.4 3.9 dynamic-slice_bitcast_fusion
  36.8 4.6 %bitcast_subtract_fusion.4 = f32[512,2048]{1,0:T(8,128)S(1)} fusion(f32[512,2048]{1,0:T(8,128)} %param.12, f32[1,1024,2048]{2,1,0:T(8,128)} %param.11, s32[]{:T(128)S(6)} %select_n.56), kind=kLoop, calls=%fused_computation.6 | loop fusion | flops 3145728 | bytes 12582916 | tf_op jit(solution)/shard_map/sub | solution.py:84
  43.9 12.2 %bitcast_add_fusion = f32[1024,2048]{1,0:T(8,128)} fusion(f32[1,1024,2048]{2,1,0:T(8,128)} %param.11, f32[1024,2048]{1,0:T(8,128)} %param.10), kind=kLoop, calls=%fused_computation.2 | loop fusion | flops 6291456 | bytes 25165824 | tf_op jit(solution)/shard_map/add | solution.py:105
  69.0 68.1 %collective-permute-done.3 = f32[64,2048]{1,0:T(8,128)S(1)} collective-permute-done((f32[64,2048]{1,0:T(8,128)}, f32[64,2048]{1,0:T(8,128)S(1)}, u32[]{:S(2)}, u32[]{:S(2)}) %collective-permute-start.3) | collective-permute-done | bytes 524320 | tf_op jit(solution)/shard_map/ppermute | solution.py:30
  137.1 3.3 collective-permute-start.5
  142.9 16.7 %collective-permute-done.4 = f32[64,2048]{1,0:T(8,128)S(1)} collective-permute-done((f32[64,2048]{1,0:T(8,128)}, f32[64,2048]{1,0:T(8,128)S(1)}, u32[]{:S(2)}, u32[]{:S(2)}) %collective-permute-start.4) | collective-permute-done | bytes 524320 | tf_op jit(solution)/shard_map/ppermute | solution.py:30
  159.5 3.3 collective-permute-start.20
  165.3 8.2 %collective-permute-done.5 = f32[64,2048]{1,0:T(8,128)S(1)} collective-permute-done((f32[64,2048]{1,0:T(8,128)}, f32[64,2048]{1,0:T(8,128)S(1)}, u32[]{:S(2)}, u32[]{:S(2)}) %collective-permute-start.5) | collective-permute-done | bytes 524320 | tf_op jit(solution)/shard_map/ppermute | solution.py:30
  173.6 3.3 collective-permute-start.19
  189.7 9.1 %collective-permute-done.13 = f32[8,4096]{1,0:T(8,128)S(1)} collective-permute-done((f32[8,4096]{1,0:T(8,128)}, f32[8,4096]{1,0:T(8,128)S(1)}, u32[]{:S(2)}, u32[]{:S(2)}) %collective-permute-start.13) | collective-permute-done | bytes 131104 | tf_op jit(solution)/shard_map/ppermute | solution.py:30
  198.8 3.3 collective-permute-start.8
  203.6 20.8 %collective-permute-done.8 = f32[64,2048]{1,0:T(8,128)} collective-permute-done((f32[64,2048]{1,0:T(8,128)}, f32[64,2048]{1,0:T(8,128)}, u32[]{:S(2)}, u32[]{:S(2)}) %collective-permute-start.8) | collective-permute-done | bytes 524320 | tf_op jit(solution)/shard_map/ppermute | solution.py:30
  224.4 3.4 collective-permute-start.10
  233.6 27.0 %collective-permute-done.10 = f32[64,2048]{1,0:T(8,128)S(1)} collective-permute-done((f32[64,2048]{1,0:T(8,128)}, f32[64,2048]{1,0:T(8,128)S(1)}, u32[]{:S(2)}, u32[]{:S(2)}) %collective-permute-start.10) | collective-permute-done | bytes 524320 | tf_op jit(solution)/shard_map/ppermute | solution.py:30
  265.8 17.2 %collective-permute-done.11 = f32[64,2048]{1,0:T(8,128)S(1)} collective-permute-done((f32[64,2048]{1,0:T(8,128)S(1)}, f32[64,2048]{1,0:T(8,128)S(1)}, u32[]{:S(2)}, u32[]{:S(2)}) %collective-permute-start.11) | collective-permute-done | bytes 524320 | tf_op jit(solution)/shard_map/ppermute | solution.py:30
  283.0 3.4 collective-permute-start.15
  288.3 17.2 %collective-permute-done.12 = f32[64,2048]{1,0:T(8,128)S(1)} collective-permute-done((f32[64,2048]{1,0:T(8,128)S(1)}, f32[64,2048]{1,0:T(8,128)S(1)}, u32[]{:S(2)}, u32[]{:S(2)}) %collective-permute-start.12) | collective-permute-done | bytes 524320 | tf_op jit(solution)/shard_map/ppermute | solution.py:30
  305.4 3.4 collective-permute-start.14
  310.7 15.5 %multiply_subtract_fusion = (f32[4096,512]{1,0:T(8,128)}, f32[4096,512]{1,0:T(8,128)}) fusion(f32[4096,512]{1,0:T(8,128)} %param.16, f32[4096,512]{1,0:T(8,128)} %param.18, f32[64,4096]{1,0:T(8,128)} %all-gather.2.cloned.1.call-done, f32[64,512]{1,0:T(8,128)S(1)} %copy-done), kind=kOutput, calls=%fused_computation.3 | convolution fusion | flops 1623195648 | bytes 34734080 | tf_op jit(solution)/shard_map/dot_general | solution.py:24
  326.2 12.8 %collective-permute-done.14 = f32[64,2048]{1,0:T(8,128)S(1)} collective-permute-done((f32[64,2048]{1,0:T(8,128)S(1)}, f32[64,2048]{1,0:T(8,128)S(1)}, u32[]{:S(2)}, u32[]{:S(2)}) %collective-permute-start.14) | collective-permute-done | bytes 524320 | tf_op jit(solution)/shard_map/ppermute | solution.py:30
  339.1 3.4 collective-permute-start.16
  346.2 30.1 %collective-permute-done.16 = f32[64,2048]{1,0:T(8,128)S(1)} collective-permute-done((f32[64,2048]{1,0:T(8,128)S(1)}, f32[64,2048]{1,0:T(8,128)S(1)}, u32[]{:S(2)}, u32[]{:S(2)}) %collective-permute-start.16) | collective-permute-done | bytes 524320 | tf_op jit(solution)/shard_map/ppermute | solution.py:30
  378.2 9.3 %collective-permute-done.17 = f32[64,2048]{1,0:T(8,128)S(1)} collective-permute-done((f32[64,2048]{1,0:T(8,128)S(1)}, f32[64,2048]{1,0:T(8,128)S(1)}, u32[]{:S(2)}, u32[]{:S(2)}) %collective-permute-start.17) | collective-permute-done | bytes 524320 | tf_op jit(solution)/shard_map/ppermute | solution.py:30
  (70 shorter events, 74.8 us)
Async XLA Ops:
  7.2 176.8 %reduce-scatter.2.cloned.1.call-start = ((), (), s32[]{:S(2)}) async-start(), calls=%async_computation.1 | async-start | bytes 1179648 | tf_op jit(solution)/shard_map/reduce_scatter | solution.py:91
  8.6 47.6 %collective-permute-start.21 = (f32[2,256]{1,0:T(2,128)}, f32[2,256]{1,0:T(2,128)S(1)}, u32[]{:S(2)}, u32[]{:S(2)}) collective-permute-start(f32[2,256]{1,0:T(2,128)} %subtract_select_fusion), channel_id=1, source_target_pairs={{0,16},{16,0},{1,17},{17,1},{2,18},{18,2},{3,19},{19,3},{4,20},{20... | collective-permute-start | bytes 6152 | tf_op jit(solution)/shard_map/ppermute | solution.py:30
  12.9 49.2 %collective-permute-start.1 = (f32[16,2048]{1,0:T(8,128)}, f32[16,2048]{1,0:T(8,128)}, u32[]{:S(2)}, u32[]{:S(2)}) collective-permute-start(f32[16,2048]{1,0:T(8,128)} %get-tuple-element.21), channel_id=1, source_target_pairs={{0,16},{16,0},{1,17},{17,1},{2,18},{18,2},{3,19},{19,3},{4,20},{20... | collective-permute-start | bytes 393224 | tf_op jit(solution)/shard_map/ppermute | solution.py:30
  13.2 44.5 %collective-permute-start = (f32[16,2048]{1,0:T(8,128)}, f32[16,2048]{1,0:T(8,128)}, u32[]{:S(2)}, u32[]{:S(2)}) collective-permute-start(f32[16,2048]{1,0:T(8,128)} %get-tuple-element.22), channel_id=1, source_target_pairs={{0,16},{16,0},{1,17},{17,1},{2,18},{18,2},{3,19},{19,3},{4,20},{20... | collective-permute-start | bytes 393224 | tf_op jit(solution)/shard_map/ppermute | solution.py:30
  16.8 47.6 %collective-permute-start.2 = (f32[32,2048]{1,0:T(8,128)S(1)}, f32[32,2048]{1,0:T(8,128)}, u32[]{:S(2)}, u32[]{:S(2)}) collective-permute-start(f32[32,2048]{1,0:T(8,128)S(1)} %dynamic-slice_bitcast_fusion.7), channel_id=1, source_target_pairs={{0,16},{16,0},{1,17},{17,1},{2,18},{18,2},{3,19},{19,3},{4,20},{20... | collective-permute-start | bytes 786440 | tf_op jit(solution)/shard_map/ppermute | solution.py:30
  30.3 280.4 %all-gather.2.cloned.1.call-start = ((), (), s32[]{:S(2)}) async-start(), calls=%async_computation.2 | async-start | bytes 1179648 | tf_op jit(solution)/shard_map/all_gather | solution.py:96
  34.2 196.4 %collective-permute-start.9 = (f32[64,2048]{1,0:T(8,128)}, f32[64,2048]{1,0:T(8,128)}, u32[]{:S(2)}, u32[]{:S(2)}) collective-permute-start(f32[64,2048]{1,0:T(8,128)} %get-tuple-element.14), channel_id=1, source_target_pairs={{0,16},{16,0},{1,17},{17,1},{2,18},{18,2},{3,19},{19,3},{4,20},{20... | collective-permute-start | bytes 1572872 | tf_op jit(solution)/shard_map/ppermute | solution.py:30
  56.1 127.8 %collective-permute-start.7 = (f32[64,2048]{1,0:T(8,128)}, f32[64,2048]{1,0:T(8,128)}, u32[]{:S(2)}, u32[]{:S(2)}) collective-permute-start(f32[64,2048]{1,0:T(8,128)} %get-tuple-element.16), channel_id=1, source_target_pairs={{0,16},{16,0},{1,17},{17,1},{2,18},{18,2},{3,19},{19,3},{4,20},{20... | collective-permute-start | bytes 1572872 | tf_op jit(solution)/shard_map/ppermute | solution.py:30
  57.7 121.7 %collective-permute-start.6 = (f32[64,2048]{1,0:T(8,128)}, f32[64,2048]{1,0:T(8,128)S(1)}, u32[]{:S(2)}, u32[]{:S(2)}) collective-permute-start(f32[64,2048]{1,0:T(8,128)} %get-tuple-element.17), channel_id=1, source_target_pairs={{0,16},{16,0},{1,17},{17,1},{2,18},{18,2},{3,19},{19,3},{4,20},{20... | collective-permute-start | bytes 1572872 | tf_op jit(solution)/shard_map/ppermute | solution.py:30
  62.1 75.0 %collective-permute-start.3 = (f32[64,2048]{1,0:T(8,128)}, f32[64,2048]{1,0:T(8,128)S(1)}, u32[]{:S(2)}, u32[]{:S(2)}) collective-permute-start(f32[64,2048]{1,0:T(8,128)} %get-tuple-element.20), channel_id=1, source_target_pairs={{0,16},{16,0},{1,17},{17,1},{2,18},{18,2},{3,19},{19,3},{4,20},{20... | collective-permute-start | bytes 1572872 | tf_op jit(solution)/shard_map/ppermute | solution.py:30
  64.4 95.1 %collective-permute-start.4 = (f32[64,2048]{1,0:T(8,128)}, f32[64,2048]{1,0:T(8,128)S(1)}, u32[]{:S(2)}, u32[]{:S(2)}) collective-permute-start(f32[64,2048]{1,0:T(8,128)} %get-tuple-element.19), channel_id=1, source_target_pairs={{0,16},{16,0},{1,17},{17,1},{2,18},{18,2},{3,19},{19,3},{4,20},{20... | collective-permute-start | bytes 1572872 | tf_op jit(solution)/shard_map/ppermute | solution.py:30
  137.1 36.5 %collective-permute-start.5 = (f32[64,2048]{1,0:T(8,128)}, f32[64,2048]{1,0:T(8,128)S(1)}, u32[]{:S(2)}, u32[]{:S(2)}) collective-permute-start(f32[64,2048]{1,0:T(8,128)} %get-tuple-element.18), channel_id=1, source_target_pairs={{0,16},{16,0},{1,17},{17,1},{2,18},{18,2},{3,19},{19,3},{4,20},{20... | collective-permute-start | bytes 1572872 | tf_op jit(solution)/shard_map/ppermute | solution.py:30
  159.5 233.1 %collective-permute-start.20 = (f32[16,2048]{1,0:T(8,128)}, f32[16,2048]{1,0:T(8,128)}, u32[]{:S(2)}, u32[]{:S(2)}) collective-permute-start(f32[16,2048]{1,0:T(8,128)} %get-tuple-element.43), channel_id=1, source_target_pairs={{0,16},{16,0},{1,17},{17,1},{2,18},{18,2},{3,19},{19,3},{4,20},{20... | collective-permute-start | bytes 393224 | tf_op jit(solution)/shard_map/ppermute | solution.py:30
  173.6 217.5 %collective-permute-start.19 = (f32[16,2048]{1,0:T(8,128)}, f32[16,2048]{1,0:T(8,128)}, u32[]{:S(2)}, u32[]{:S(2)}) collective-permute-start(f32[16,2048]{1,0:T(8,128)} %get-tuple-element.44), channel_id=1, source_target_pairs={{0,16},{16,0},{1,17},{17,1},{2,18},{18,2},{3,19},{19,3},{4,20},{20... | collective-permute-start | bytes 393224 | tf_op jit(solution)/shard_map/ppermute | solution.py:30
  179.4 210.0 %collective-permute-start.18 = (f32[32,2048]{1,0:T(8,128)}, f32[32,2048]{1,0:T(8,128)S(1)}, u32[]{:S(2)}, u32[]{:S(2)}) collective-permute-start(f32[32,2048]{1,0:T(8,128)} %slice.87), channel_id=1, source_target_pairs={{0,16},{16,0},{1,17},{17,1},{2,18},{18,2},{3,19},{19,3},{4,20},{20... | collective-permute-start | bytes 786440 | tf_op jit(solution)/shard_map/ppermute | solution.py:30
  183.9 14.8 %collective-permute-start.13 = (f32[8,4096]{1,0:T(8,128)}, f32[8,4096]{1,0:T(8,128)S(1)}, u32[]{:S(2)}, u32[]{:S(2)}) collective-permute-start(f32[8,4096]{1,0:T(8,128)} %reduce-scatter.2.cloned.1.call-done), channel_id=1, source_target_pairs={{0,16},{16,0},{1,17},{17,1},{2,18},{18,2},{3,19},{19,3},{4,20},{20... | collective-permute-start | bytes 393224 | tf_op jit(solution)/shard_map/ppermute | solution.py:30
  198.8 25.7 %collective-permute-start.8 = (f32[64,2048]{1,0:T(8,128)}, f32[64,2048]{1,0:T(8,128)}, u32[]{:S(2)}, u32[]{:S(2)}) collective-permute-start(f32[64,2048]{1,0:T(8,128)} %get-tuple-element.9), channel_id=1, source_target_pairs={{0,16},{16,0},{1,17},{17,1},{2,18},{18,2},{3,19},{19,3},{4,20},{20... | collective-permute-start | bytes 1572872 | tf_op jit(solution)/shard_map/ppermute | solution.py:30
  224.4 36.2 %collective-permute-start.10 = (f32[64,2048]{1,0:T(8,128)}, f32[64,2048]{1,0:T(8,128)S(1)}, u32[]{:S(2)}, u32[]{:S(2)}) collective-permute-start(f32[64,2048]{1,0:T(8,128)} %get-tuple-element.51), channel_id=1, source_target_pairs={{0,16},{16,0},{1,17},{17,1},{2,18},{18,2},{3,19},{19,3},{4,20},{20... | collective-permute-start | bytes 1572872 | tf_op jit(solution)/shard_map/ppermute | solution.py:30
  230.7 52.3 %collective-permute-start.11 = (f32[64,2048]{1,0:T(8,128)S(1)}, f32[64,2048]{1,0:T(8,128)S(1)}, u32[]{:S(2)}, u32[]{:S(2)}) collective-permute-start(f32[64,2048]{1,0:T(8,128)S(1)} %get-tuple-element.50), channel_id=1, source_target_pairs={{0,16},{16,0},{1,17},{17,1},{2,18},{18,2},{3,19},{19,3},{4,20},{20... | collective-permute-start | bytes 1572872 | tf_op jit(solution)/shard_map/ppermute | solution.py:30
  260.6 44.8 %collective-permute-start.12 = (f32[64,2048]{1,0:T(8,128)S(1)}, f32[64,2048]{1,0:T(8,128)S(1)}, u32[]{:S(2)}, u32[]{:S(2)}) collective-permute-start(f32[64,2048]{1,0:T(8,128)S(1)} %get-tuple-element.49), channel_id=1, source_target_pairs={{0,16},{16,0},{1,17},{17,1},{2,18},{18,2},{3,19},{19,3},{4,20},{20... | collective-permute-start | bytes 1572872 | tf_op jit(solution)/shard_map/ppermute | solution.py:30
  283.0 61.4 %collective-permute-start.15 = (f32[64,2048]{1,0:T(8,128)S(1)}, f32[64,2048]{1,0:T(8,128)S(1)}, u32[]{:S(2)}, u32[]{:S(2)}) collective-permute-start(f32[64,2048]{1,0:T(8,128)S(1)} %get-tuple-element.47), channel_id=1, source_target_pairs={{0,16},{16,0},{1,17},{17,1},{2,18},{18,2},{3,19},{19,3},{4,20},{20... | collective-permute-start | bytes 1572872 | tf_op jit(solution)/shard_map/ppermute | solution.py:30
  305.4 33.6 %collective-permute-start.14 = (f32[64,2048]{1,0:T(8,128)S(1)}, f32[64,2048]{1,0:T(8,128)S(1)}, u32[]{:S(2)}, u32[]{:S(2)}) collective-permute-start(f32[64,2048]{1,0:T(8,128)S(1)} %get-tuple-element.10), channel_id=1, source_target_pairs={{0,16},{16,0},{1,17},{17,1},{2,18},{18,2},{3,19},{19,3},{4,20},{20... | collective-permute-start | bytes 1572872 | tf_op jit(solution)/shard_map/ppermute | solution.py:30
  339.1 37.3 %collective-permute-start.16 = (f32[64,2048]{1,0:T(8,128)S(1)}, f32[64,2048]{1,0:T(8,128)S(1)}, u32[]{:S(2)}, u32[]{:S(2)}) collective-permute-start(f32[64,2048]{1,0:T(8,128)S(1)} %get-tuple-element.11), channel_id=1, source_target_pairs={{0,16},{16,0},{1,17},{17,1},{2,18},{18,2},{3,19},{19,3},{4,20},{20... | collective-permute-start | bytes 1572872 | tf_op jit(solution)/shard_map/ppermute | solution.py:30
  344.3 43.1 %collective-permute-start.17 = (f32[64,2048]{1,0:T(8,128)S(1)}, f32[64,2048]{1,0:T(8,128)S(1)}, u32[]{:S(2)}, u32[]{:S(2)}) collective-permute-start(f32[64,2048]{1,0:T(8,128)S(1)} %get-tuple-element.45), channel_id=1, source_target_pairs={{0,16},{16,0},{1,17},{17,1},{2,18},{18,2},{3,19},{19,3},{4,20},{20... | collective-permute-start | bytes 1572872 | tf_op jit(solution)/shard_map/ppermute | solution.py:30
  (5 other events, 49.8 us)
Sparse Core Ops, SparseCore 0:
  30.4 37.1 reduce-scatter.1
  203.8 23.4 all-gather.1

commit v3 on v2

--- a/solution.py
+++ b/solution.py
@@ -7,11 +7,12 @@
 momentum = 0.9
 rate = outer_rate * (1 + momentum)
 decay = outer_rate * momentum * momentum
-first_sizes = (1, 1, 2, 4, 4, 4, 4, 4, 4, 4)
-last_sizes = (4, 4, 4, 4, 4, 4, 4, 2, 1, 1)
-after_scatter = 8
-after_swap = 3
-after_gate = 5
+first_sizes = (1, 3, 4, 4, 4, 4, 4, 4, 4)
+last_sizes = (4, 4, 4, 4, 4, 4, 4, 3, 1)
+window = 3
+after_scatter = 7
+after_swap = 11
+after_gate = 14
 
 
 def advance(anchor, moment, delta):
@@ -42,18 +43,25 @@
         start += size
 
 
-def exchange_whole(anchor, local, moment):
-    group_index = lax.axis_index("group")
-    half = moment.shape[0]
-    mine = lax.broadcasted_iota(jnp.int32, anchor.shape, 0) // half == group_index
+def mine_of(shape, half):
+    return lax.broadcasted_iota(jnp.int32, shape, 0) // half == lax.axis_index("group")
+
+
+def norm_message(local, moment):
     wide = lax.concatenate([moment, moment], 0)
     mixed = (rate / 2) * local - decay * wide
-    received = swap(jnp.where(mine, mixed, local))
+    return jnp.where(mine_of(local.shape, moment.shape[0]), mixed, local)
+
+
+def norm_finish(anchor, local, moment, received):
+    half = moment.shape[0]
+    wide = lax.concatenate([moment, moment], 0)
+    mine = mine_of(anchor.shape, half)
     anchor_next = (1 - rate) * anchor + (rate / 2) * local
     anchor_next += jnp.where(mine, (rate / 2) * received - decay * wide, received)
     step = anchor - 0.5 * (local + received)
-    moment_next = momentum * moment + lax.dynamic_slice_in_dim(step, group_index * half, half, 0)
-    return anchor_next, moment_next
+    own = lax.axis_index("group") * half
+    return anchor_next, momentum * moment + lax.dynamic_slice_in_dim(step, own, half, 0)
 
 
 def body(
@@ -80,27 +88,45 @@
 
     spans = list(pieces(half, first_sizes))
     mixed_spans = list(pieces(half, last_sizes))
-    sent = [rows_of(local, other + start, size) for start, size in spans]
     mixed = (rate / 2) * rows_of(local, own, half) - decay * down_moment
-    mixed_sent = [mixed[start : start + size] for start, size in mixed_spans]
 
     gate_diff = gate_anchor - gate_local[0]
     partial_factors = lax.dot_general(
         factor_basis, gate_diff, (((1,), (1,)), ((), ())), precision=lax.Precision.HIGHEST
     )
     piece = lax.psum_scatter(partial_factors, "shard", scatter_dimension=0, tiled=True)
-    sent[after_scatter] = after(sent[after_scatter], piece)
     piece_other = swap(piece)
-    mixed_sent[after_swap] = after(mixed_sent[after_swap], piece_other)
-    piece = (piece + piece_other) / groups
-    factors = lax.all_gather(piece, "shard", axis=0, tiled=True)
-    gate_delta = rebuild(factors, factor_basis)
-    new_gate_anchor, new_gate_moment = advance(gate_anchor, gate_moment, gate_delta)
-    mixed_sent[after_gate] = after(mixed_sent[after_gate], new_gate_anchor, new_gate_moment)
 
-    received = [swap(part) for part in sent]
-    new_norm_anchor, new_norm_moment = exchange_whole(norm_anchor, norm_local[0], norm_moment)
-    mixed_received = [swap(part) for part in mixed_sent]
+    parts = []
+    cut = local
+    for i, (start, size) in enumerate(spans + mixed_spans):
+        if i < len(spans):
+            part = rows_of(cut, other + start, size)
+            if i < window:
+                cut = after(local, part)
+        else:
+            part = mixed[start : start + size]
+        ties = [parts[i - window]] if i >= window else []
+        if i == after_scatter:
+            ties.append(piece)
+        if i == after_swap:
+            ties.append(piece_sum)
+        if i == after_gate:
+            ties += [new_gate_anchor, new_gate_moment]
+        parts.append(swap(after(part, *ties)))
+        if i == 0:
+            norm_sent = after(norm_message(norm_local[0], norm_moment), parts[0])
+            norm_received = swap(norm_sent)
+        if i == after_scatter:
+            piece_sum = piece + after(piece_other, parts[i - 1])
+            factors = lax.all_gather(piece_sum / groups, "shard", axis=0, tiled=True)
+            gate_delta = rebuild(factors, factor_basis)
+            new_gate_anchor, new_gate_moment = advance(gate_anchor, gate_moment, gate_delta)
+    received, mixed_received = parts[: len(spans)], parts[len(spans) :]
+    norm_received = after(norm_received, parts[after_swap])
+    new_norm_anchor, new_norm_moment = norm_finish(
+        norm_anchor, norm_local[0], norm_moment, norm_received
+    )
 
     anchor_next = (1 - rate) * down_anchor + (rate / 2) * local
     moment_next = []

time: 405 us -> 388 us (0.958)
  waiting for transfers between devices: 236 us -> 226 us
  other arithmetic: 63.6 us -> 58.9 us
    ppermute x22 -> x20, waiting for transfers between devices: 236 us -> 226 us  [swap(): return lax.ppermute(array, 'group', [(0, 1), (1, 0)])]
    unnamed x9 -> x8, other arithmetic: 21.7 us -> 19.5 us
    dynamic_slice x3 -> x4, local copies, waits for them, and re-layouts: 6.55 us -> 8.59 us  [rows_of(): return lax.dynamic_slice_in_dim(array, start, size, 0)]
    ppermute x22 -> x20, starting transfers between devices: 47.2 us -> 45.5 us  [swap(): return lax.ppermute(array, 'group', [(0, 1), (1, 0)])]
    dynamic_update_slice x10 -> x9, other arithmetic: 18.2 us -> 16.8 us  [body(): lax.dynamic_update_slice_in_dim(anchor_next, value, other + start, 0)]
  transfers between devices with their start and end apart: 24 -> 22, of which waited for: 11 -> 14; matrix products, arithmetic and copies ran while one was open for 24% -> 25% of each run, Pallas kernels for 0% -> 0%
where the time goes in v3:
time: 388 us; the launch traced here: 385 us
  waiting for transfers between devices  226 us (58%)
  other arithmetic  58.9 us (15%)
  starting transfers between devices  45.5 us (12%)
  matrix products  28.8 us (7%)
  between operations  14.1 us (4%)
  local copies, waits for them, and re-layouts  11.3 us (3%)
    ppermute x20, waiting for transfers between devices, swap(): return lax.ppermute(array, 'group', [(0, 1), (1, 0)])  226 us
    ppermute x20, starting transfers between devices, swap(): return lax.ppermute(array, 'group', [(0, 1), (1, 0)])  45.5 us
    unnamed x8, other arithmetic  19.5 us
    dynamic_update_slice x9, other arithmetic, body(): lax.dynamic_update_slice_in_dim(anchor_next, value, other + start, 0)  16.8 us
    dot_general x1, matrix products, rebuild(): lax.dot_general(factors, factor_basis, (((0,), (0,)), ((), ())), precisio...  15.7 us
    dot_general x1, matrix products, body(): lax.dot_general(factor_basis, gate_diff, (((1,), (1,)), ((), ())), precis...  13.1 us
    add x1, other arithmetic, body(): anchor_next = (1 - rate) * down_anchor + rate / 2 * local  12.6 us
    dynamic_slice x4, local copies, waits for them, and re-layouts, rows_of(): return lax.dynamic_slice_in_dim(array, start, size, 0)  8.59 us
  transfers between devices with their start and end apart: 22, of which 14 were waited for; matrix products, arithmetic and copies ran while one was open for 25% of the time, Pallas kernels for 0%

profile of v3, /device:TPU:10, one launch (start us, length us, event | category | flops | bytes accessed | tf_op | source)
XLA Modules:
  0.0 385.1 jit_solution(18341731373131245053)
XLA Ops:
  18.0 13.1 %fusion.1 = f32[64,4096]{1,0:T(8,128)} fusion(f32[64,512]{1,0:T(8,128)S(1)} %copy-done, f32[4096,512]{1,0:T(8,128)} %param.16, f32[1,4096,512]{2,1,0:T(8,128)} %param.17), kind=kOutput, calls=%fused_computation.5 | convolution fusion | flops 1612709888 | bytes 17956864 | tf_op jit(solution)/shard_map/dot_general | solution.py:94
  31.2 4.4 %bitcast_subtract_fusion.4 = f32[512,2048]{1,0:T(8,128)S(1)} fusion(f32[512,2048]{1,0:T(8,128)} %param.12, f32[1,1024,2048]{2,1,0:T(8,128)} %param.11, s32[]{:T(128)S(6)} %select_n.51), kind=kLoop, calls=%fused_computation.6 | loop fusion | flops 3145728 | bytes 12582916 | tf_op jit(solution)/shard_map/sub | solution.py:91
  37.4 12.6 %multiply_add_fusion.1 = f32[1024,2048]{1,0:T(8,128)} fusion(f32[1024,2048]{1,0:T(8,128)} %param.10, f32[1,1024,2048]{2,1,0:T(8,128)} %param.11), kind=kLoop, calls=%fused_computation.4 | loop fusion | flops 6291456 | bytes 25165824 | tf_op jit(solution)/shard_map/add | solution.py:131
  60.7 29.6 %collective-permute-done.2 = f32[64,2048]{1,0:T(8,128)} collective-permute-done((f32[64,2048]{1,0:T(8,128)}, f32[64,2048]{1,0:T(8,128)}, u32[]{:S(2)}, u32[]{:S(2)}) %collective-permute-start.2) | collective-permute-done | bytes 524320 | tf_op jit(solution)/shard_map/ppermute | solution.py:31
  90.3 3.4 collective-permute-start.5
  96.2 16.5 %collective-permute-done.3 = f32[64,2048]{1,0:T(8,128)S(1)} collective-permute-done((f32[64,2048]{1,0:T(8,128)S(1)}, f32[64,2048]{1,0:T(8,128)S(1)}, u32[]{:S(2)}, u32[]{:S(2)}) %collective-permute-start.3) | collective-permute-done | bytes 524320 | tf_op jit(solution)/shard_map/ppermute | solution.py:31
  112.7 3.4 collective-permute-start.6
  118.5 5.5 %collective-permute-done.4 = f32[64,2048]{1,0:T(8,128)S(1)} collective-permute-done((f32[64,2048]{1,0:T(8,128)S(1)}, f32[64,2048]{1,0:T(8,128)S(1)}, u32[]{:S(2)}, u32[]{:S(2)}) %collective-permute-start.4) | collective-permute-done | bytes 524320 | tf_op jit(solution)/shard_map/ppermute | solution.py:31
  126.3 8.9 %collective-permute-done.5 = f32[64,2048]{1,0:T(8,128)S(1)} collective-permute-done((f32[64,2048]{1,0:T(8,128)S(1)}, f32[64,2048]{1,0:T(8,128)S(1)}, u32[]{:S(2)}, u32[]{:S(2)}) %collective-permute-start.5) | collective-permute-done | bytes 524320 | tf_op jit(solution)/shard_map/ppermute | solution.py:31
  135.2 3.4 collective-permute-start.8
  141.0 16.7 %collective-permute-done.6 = f32[64,2048]{1,0:T(8,128)S(1)} collective-permute-done((f32[64,2048]{1,0:T(8,128)S(1)}, f32[64,2048]{1,0:T(8,128)S(1)}, u32[]{:S(2)}, u32[]{:S(2)}) %collective-permute-start.6) | collective-permute-done | bytes 524320 | tf_op jit(solution)/shard_map/ppermute | solution.py:31
  158.5 3.4 collective-permute-start.9
  167.6 40.7 %collective-permute-done.11 = f32[8,4096]{1,0:T(8,128)S(1)} collective-permute-done((f32[8,4096]{1,0:T(8,128)}, f32[8,4096]{1,0:T(8,128)S(1)}, u32[]{:S(2)}, u32[]{:S(2)}) %collective-permute-start.11) | collective-permute-done | bytes 131104 | tf_op jit(solution)/shard_map/ppermute | solution.py:31
  213.4 28.7 %collective-permute-done.7 = f32[64,2048]{1,0:T(8,128)} collective-permute-done((f32[64,2048]{1,0:T(8,128)}, f32[64,2048]{1,0:T(8,128)}, u32[]{:S(2)}, u32[]{:S(2)}) %collective-permute-start.7) | collective-permute-done | bytes 524320 | tf_op jit(solution)/shard_map/ppermute | solution.py:31
  242.0 3.4 collective-permute-start.10
  253.2 11.2 %collective-permute-done.13 = f32[64,2048]{1,0:T(8,128)S(1)} collective-permute-done((f32[64,2048]{1,0:T(8,128)S(1)}, f32[64,2048]{1,0:T(8,128)S(1)}, u32[]{:S(2)}, u32[]{:S(2)}) %collective-permute-start.13) | collective-permute-done | bytes 524320 | tf_op jit(solution)/shard_map/ppermute | solution.py:31
  264.4 3.4 collective-permute-start.16
  267.8 19.1 %collective-permute-done.12 = f32[64,2048]{1,0:T(8,128)S(1)} collective-permute-done((f32[64,2048]{1,0:T(8,128)S(1)}, f32[64,2048]{1,0:T(8,128)S(1)}, u32[]{:S(2)}, u32[]{:S(2)}) %collective-permute-start.12) | collective-permute-done | bytes 524320 | tf_op jit(solution)/shard_map/ppermute | solution.py:31
  288.0 10.1 %collective-permute-done.10 = f32[64,2048]{1,0:T(8,128)S(1)} collective-permute-done((f32[64,2048]{1,0:T(8,128)S(1)}, f32[64,2048]{1,0:T(8,128)S(1)}, u32[]{:S(2)}, u32[]{:S(2)}) %collective-permute-start.10) | collective-permute-done | bytes 524320 | tf_op jit(solution)/shard_map/ppermute | solution.py:31
  305.3 15.7 %multiply_subtract_fusion = (f32[4096,512]{1,0:T(8,128)}, f32[4096,512]{1,0:T(8,128)}) fusion(f32[4096,512]{1,0:T(8,128)} %param.16, f32[4096,512]{1,0:T(8,128)} %param.18, f32[64,4096]{1,0:T(8,128)} %all-gather.2.cloned.1.call-done, f32[64,512]{1,0:T(8,128)S(1)} %copy-done), kind=kOutput, calls=%fused_computation.2 | convolution fusion | flops 1623195648 | bytes 34734080 | tf_op jit(solution)/shard_map/dot_general | solution.py:25
  323.0 20.1 %collective-permute-done.14 = f32[64,2048]{1,0:T(8,128)S(1)} collective-permute-done((f32[64,2048]{1,0:T(8,128)S(1)}, f32[64,2048]{1,0:T(8,128)S(1)}, u32[]{:S(2)}, u32[]{:S(2)}) %collective-permute-start.14) | collective-permute-done | bytes 524320 | tf_op jit(solution)/shard_map/ppermute | solution.py:31
  343.1 3.4 collective-permute-start.17
  348.3 14.4 %collective-permute-done.15 = f32[64,2048]{1,0:T(8,128)S(1)} collective-permute-done((f32[64,2048]{1,0:T(8,128)S(1)}, f32[64,2048]{1,0:T(8,128)S(1)}, u32[]{:S(2)}, u32[]{:S(2)}) %collective-permute-start.15) | collective-permute-done | bytes 524320 | tf_op jit(solution)/shard_map/ppermute | solution.py:31
  369.9 4.0 %collective-permute-done.17 = f32[48,2048]{1,0:T(8,128)S(1)} collective-permute-done((f32[48,2048]{1,0:T(8,128)S(1)}, f32[48,2048]{1,0:T(8,128)S(1)}, u32[]{:S(2)}, u32[]{:S(2)}) %collective-permute-start.17) | collective-permute-done | bytes 393248 | tf_op jit(solution)/shard_map/ppermute | solution.py:31
  (75 shorter events, 76.0 us)
Async XLA Ops:
  7.2 154.7 %reduce-scatter.2.cloned.1.call-start = ((), (), s32[]{:S(2)}) async-start(), calls=%async_computation.1 | async-start | bytes 1179648 | tf_op jit(solution)/shard_map/reduce_scatter | solution.py:97
  8.8 44.6 %collective-permute-start = (f32[16,2048]{1,0:T(8,128)}, f32[16,2048]{1,0:T(8,128)S(1)}, u32[]{:S(2)}, u32[]{:S(2)}) collective-permute-start(f32[16,2048]{1,0:T(8,128)} %dynamic-slice_bitcast_fusion), channel_id=1, source_target_pairs={{0,16},{16,0},{1,17},{17,1},{2,18},{18,2},{3,19},{19,3},{4,20},{20... | collective-permute-start | bytes 393224 | tf_op jit(solution)/shard_map/ppermute | solution.py:31
  13.2 45.0 %collective-permute-start.1 = (f32[48,2048]{1,0:T(8,128)}, f32[48,2048]{1,0:T(8,128)}, u32[]{:S(2)}, u32[]{:S(2)}) collective-permute-start(f32[48,2048]{1,0:T(8,128)} %constant_dynamic-slice_fusion.10), channel_id=1, source_target_pairs={{0,16},{16,0},{1,17},{17,1},{2,18},{18,2},{3,19},{19,3},{4,20},{20... | collective-permute-start | bytes 1179656 | tf_op jit(solution)/shard_map/ppermute | solution.py:31
  15.4 74.9 %collective-permute-start.2 = (f32[64,2048]{1,0:T(8,128)}, f32[64,2048]{1,0:T(8,128)}, u32[]{:S(2)}, u32[]{:S(2)}) collective-permute-start(f32[64,2048]{1,0:T(8,128)} %constant_dynamic-slice_fusion.9), channel_id=1, source_target_pairs={{0,16},{16,0},{1,17},{17,1},{2,18},{18,2},{3,19},{19,3},{4,20},{20... | collective-permute-start | bytes 1572872 | tf_op jit(solution)/shard_map/ppermute | solution.py:31
  31.1 274.2 %all-gather.2.cloned.1.call-start = ((), (), s32[]{:S(2)}) async-start(), calls=%async_computation.2 | async-start | bytes 1179648 | tf_op jit(solution)/shard_map/all_gather | solution.py:122
  50.0 43.7 %copy-start.1 = (f32[512,2048]{1,0:T(8,128)S(1)}, f32[512,2048]{1,0:T(8,128)}, u32[]{:S(2)}) copy-start(f32[512,2048]{1,0:T(8,128)} %param.12) | copy-start | bytes 12582916
  53.4 214.4 %collective-permute-start.19 = (f32[2,256]{1,0:T(2,128)S(1)}, f32[2,256]{1,0:T(2,128)S(1)}, u32[]{:S(2)}, u32[]{:S(2)}) collective-permute-start(f32[2,256]{1,0:T(2,128)S(1)} %subtract_select_fusion), channel_id=1, source_target_pairs={{0,16},{16,0},{1,17},{17,1},{2,18},{18,2},{3,19},{19,3},{4,20},{20... | collective-permute-start | bytes 6152 | tf_op jit(solution)/shard_map/ppermute | solution.py:31
  53.6 59.1 %collective-permute-start.3 = (f32[64,2048]{1,0:T(8,128)S(1)}, f32[64,2048]{1,0:T(8,128)S(1)}, u32[]{:S(2)}, u32[]{:S(2)}) collective-permute-start(f32[64,2048]{1,0:T(8,128)S(1)} %get-tuple-element.30), channel_id=1, source_target_pairs={{0,16},{16,0},{1,17},{17,1},{2,18},{18,2},{3,19},{19,3},{4,20},{20... | collective-permute-start | bytes 1572872 | tf_op jit(solution)/shard_map/ppermute | solution.py:31
  58.2 65.8 %collective-permute-start.4 = (f32[64,2048]{1,0:T(8,128)S(1)}, f32[64,2048]{1,0:T(8,128)S(1)}, u32[]{:S(2)}, u32[]{:S(2)}) collective-permute-start(f32[64,2048]{1,0:T(8,128)S(1)} %get-tuple-element.31), channel_id=1, source_target_pairs={{0,16},{16,0},{1,17},{17,1},{2,18},{18,2},{3,19},{19,3},{4,20},{20... | collective-permute-start | bytes 1572872 | tf_op jit(solution)/shard_map/ppermute | solution.py:31
  90.3 44.9 %collective-permute-start.5 = (f32[64,2048]{1,0:T(8,128)S(1)}, f32[64,2048]{1,0:T(8,128)S(1)}, u32[]{:S(2)}, u32[]{:S(2)}) collective-permute-start(f32[64,2048]{1,0:T(8,128)S(1)} %get-tuple-element.32), channel_id=1, source_target_pairs={{0,16},{16,0},{1,17},{17,1},{2,18},{18,2},{3,19},{19,3},{4,20},{20... | collective-permute-start | bytes 1572872 | tf_op jit(solution)/shard_map/ppermute | solution.py:31
  112.7 44.9 %collective-permute-start.6 = (f32[64,2048]{1,0:T(8,128)S(1)}, f32[64,2048]{1,0:T(8,128)S(1)}, u32[]{:S(2)}, u32[]{:S(2)}) collective-permute-start(f32[64,2048]{1,0:T(8,128)S(1)} %get-tuple-element.33), channel_id=1, source_target_pairs={{0,16},{16,0},{1,17},{17,1},{2,18},{18,2},{3,19},{19,3},{4,20},{20... | collective-permute-start | bytes 1572872 | tf_op jit(solution)/shard_map/ppermute | solution.py:31
  135.2 74.7 %collective-permute-start.8 = (f32[64,2048]{1,0:T(8,128)}, f32[64,2048]{1,0:T(8,128)}, u32[]{:S(2)}, u32[]{:S(2)}) collective-permute-start(f32[64,2048]{1,0:T(8,128)} %get-tuple-element.35), channel_id=1, source_target_pairs={{0,16},{16,0},{1,17},{17,1},{2,18},{18,2},{3,19},{19,3},{4,20},{20... | collective-permute-start | bytes 1572872 | tf_op jit(solution)/shard_map/ppermute | solution.py:31
  138.6 148.3 %copy-start.8 = (f32[2,256]{1,0:T(2,128)S(1)}, f32[2,256]{1,0:T(2,128)}, u32[]{:S(2)}) copy-start(f32[2,256]{1,0:T(2,128)} %param.13) | copy-start | bytes 6148
  158.5 51.5 %collective-permute-start.9 = (f32[64,2048]{1,0:T(8,128)}, f32[64,2048]{1,0:T(8,128)}, u32[]{:S(2)}, u32[]{:S(2)}) collective-permute-start(f32[64,2048]{1,0:T(8,128)} %get-tuple-element.36), channel_id=1, source_target_pairs={{0,16},{16,0},{1,17},{17,1},{2,18},{18,2},{3,19},{19,3},{4,20},{20... | collective-permute-start | bytes 1572872 | tf_op jit(solution)/shard_map/ppermute | solution.py:31
  161.9 46.5 %collective-permute-start.11 = (f32[8,4096]{1,0:T(8,128)}, f32[8,4096]{1,0:T(8,128)S(1)}, u32[]{:S(2)}, u32[]{:S(2)}) collective-permute-start(f32[8,4096]{1,0:T(8,128)} %reduce-scatter.2.cloned.1.call-done), channel_id=1, source_target_pairs={{0,16},{16,0},{1,17},{17,1},{2,18},{18,2},{3,19},{19,3},{4,20},{20... | collective-permute-start | bytes 393224 | tf_op jit(solution)/shard_map/ppermute | solution.py:31
  164.8 77.3 %collective-permute-start.7 = (f32[64,2048]{1,0:T(8,128)}, f32[64,2048]{1,0:T(8,128)}, u32[]{:S(2)}, u32[]{:S(2)}) collective-permute-start(f32[64,2048]{1,0:T(8,128)} %get-tuple-element.34), channel_id=1, source_target_pairs={{0,16},{16,0},{1,17},{17,1},{2,18},{18,2},{3,19},{19,3},{4,20},{20... | collective-permute-start | bytes 1572872 | tf_op jit(solution)/shard_map/ppermute | solution.py:31
  210.0 54.5 %collective-permute-start.13 = (f32[64,2048]{1,0:T(8,128)S(1)}, f32[64,2048]{1,0:T(8,128)S(1)}, u32[]{:S(2)}, u32[]{:S(2)}) collective-permute-start(f32[64,2048]{1,0:T(8,128)S(1)} %get-tuple-element.40), channel_id=1, source_target_pairs={{0,16},{16,0},{1,17},{17,1},{2,18},{18,2},{3,19},{19,3},{4,20},{20... | collective-permute-start | bytes 1572872 | tf_op jit(solution)/shard_map/ppermute | solution.py:31
  213.3 73.6 %collective-permute-start.12 = (f32[64,2048]{1,0:T(8,128)S(1)}, f32[64,2048]{1,0:T(8,128)S(1)}, u32[]{:S(2)}, u32[]{:S(2)}) collective-permute-start(f32[64,2048]{1,0:T(8,128)S(1)} %get-tuple-element.39), channel_id=1, source_target_pairs={{0,16},{16,0},{1,17},{17,1},{2,18},{18,2},{3,19},{19,3},{4,20},{20... | collective-permute-start | bytes 1572872 | tf_op jit(solution)/shard_map/ppermute | solution.py:31
  242.0 56.1 %collective-permute-start.10 = (f32[64,2048]{1,0:T(8,128)S(1)}, f32[64,2048]{1,0:T(8,128)S(1)}, u32[]{:S(2)}, u32[]{:S(2)}) collective-permute-start(f32[64,2048]{1,0:T(8,128)S(1)} %get-tuple-element.37), channel_id=1, source_target_pairs={{0,16},{16,0},{1,17},{17,1},{2,18},{18,2},{3,19},{19,3},{4,20},{20... | collective-permute-start | bytes 1572872 | tf_op jit(solution)/shard_map/ppermute | solution.py:31
  264.4 103.6 %collective-permute-start.16 = (f32[64,2048]{1,0:T(8,128)S(1)}, f32[64,2048]{1,0:T(8,128)S(1)}, u32[]{:S(2)}, u32[]{:S(2)}) collective-permute-start(f32[64,2048]{1,0:T(8,128)S(1)} %get-tuple-element.43), channel_id=1, source_target_pairs={{0,16},{16,0},{1,17},{17,1},{2,18},{18,2},{3,19},{19,3},{4,20},{20... | collective-permute-start | bytes 1572872 | tf_op jit(solution)/shard_map/ppermute | solution.py:31
  298.1 44.9 %collective-permute-start.14 = (f32[64,2048]{1,0:T(8,128)S(1)}, f32[64,2048]{1,0:T(8,128)S(1)}, u32[]{:S(2)}, u32[]{:S(2)}) collective-permute-start(f32[64,2048]{1,0:T(8,128)S(1)} %get-tuple-element.41), channel_id=1, source_target_pairs={{0,16},{16,0},{1,17},{17,1},{2,18},{18,2},{3,19},{19,3},{4,20},{20... | collective-permute-start | bytes 1572872 | tf_op jit(solution)/shard_map/ppermute | solution.py:31
  321.1 41.7 %collective-permute-start.15 = (f32[64,2048]{1,0:T(8,128)S(1)}, f32[64,2048]{1,0:T(8,128)S(1)}, u32[]{:S(2)}, u32[]{:S(2)}) collective-permute-start(f32[64,2048]{1,0:T(8,128)S(1)} %get-tuple-element.42), channel_id=1, source_target_pairs={{0,16},{16,0},{1,17},{17,1},{2,18},{18,2},{3,19},{19,3},{4,20},{20... | collective-permute-start | bytes 1572872 | tf_op jit(solution)/shard_map/ppermute | solution.py:31
  343.1 30.9 %collective-permute-start.17 = (f32[48,2048]{1,0:T(8,128)S(1)}, f32[48,2048]{1,0:T(8,128)S(1)}, u32[]{:S(2)}, u32[]{:S(2)}) collective-permute-start(f32[48,2048]{1,0:T(8,128)S(1)} %copy-done.5), channel_id=1, source_target_pairs={{0,16},{16,0},{1,17},{17,1},{2,18},{18,2},{3,19},{19,3},{4,20},{20... | collective-permute-start | bytes 1179656 | tf_op jit(solution)/shard_map/ppermute | solution.py:31
  362.7 14.0 %collective-permute-start.18 = (f32[16,2048]{1,0:T(8,128)S(1)}, f32[16,2048]{1,0:T(8,128)S(1)}, u32[]{:S(2)}, u32[]{:S(2)}) collective-permute-start(f32[16,2048]{1,0:T(8,128)S(1)} %slice.80), channel_id=1, source_target_pairs={{0,16},{16,0},{1,17},{17,1},{2,18},{18,2},{3,19},{19,3},{4,20},{20... | collective-permute-start | bytes 393224 | tf_op jit(solution)/shard_map/ppermute | solution.py:31
  (8 other events, 151.5 us)
Sparse Core Ops, SparseCore 0:
  31.2 35.1 reduce-scatter.1
  210.1 25.2 all-gather.1

commit v4 on v3

--- a/solution.py
+++ b/solution.py
@@ -7,12 +7,11 @@
 momentum = 0.9
 rate = outer_rate * (1 + momentum)
 decay = outer_rate * momentum * momentum
-first_sizes = (1, 3, 4, 4, 4, 4, 4, 4, 4)
-last_sizes = (4, 4, 4, 4, 4, 4, 4, 3, 1)
+first_sizes = (1, 3, 4) + (2,) * 12
+last_sizes = (2,) * 14 + (3, 1)
 window = 3
-after_scatter = 7
-after_swap = 11
-after_gate = 14
+chain_start = 2
+chain_end = 23
 
 
 def advance(anchor, moment, delta):
@@ -29,6 +28,11 @@
 
 def swap(array):
     return lax.ppermute(array, "group", [(0, 1), (1, 0)])
+
+
+def across(array, k):
+    shards = lax.axis_size("shard")
+    return lax.ppermute(array, "shard", [(i, i ^ k) for i in range(shards)])
 
 
 def after(array, *earlier):
@@ -41,6 +45,19 @@
     for size in sizes:
         yield start * unit, size * unit
         start += size
+
+
+def factor_chain(value, bits):
+    for bit in bits:
+        rest = value.shape[0] // 2
+        received = yield value[rest:], across(value[rest:], bit)
+        value = value[:rest] + received
+    received = yield value, swap(value)
+    value = (value + received) / lax.axis_size("group")
+    for bit in reversed(bits):
+        received = yield value, across(value, bit)
+        value = lax.concatenate([value, received], 0)
+    return value
 
 
 def mine_of(shape, half):
@@ -90,15 +107,27 @@
     mixed_spans = list(pieces(half, last_sizes))
     mixed = (rate / 2) * rows_of(local, own, half) - decay * down_moment
 
+    shards = lax.axis_size("shard")
+    bits = [1 << n for n in range(shards.bit_length() - 1)]
+    masks = [0]
+    for bit in reversed(bits):
+        masks += [mask | bit for mask in masks]
+    block = factor_basis.shape[0] // shards
+    basis = lax.concatenate(
+        [rows_of(factor_basis, (lax.axis_index("shard") ^ mask) * block, block) for mask in masks],
+        0,
+    )
     gate_diff = gate_anchor - gate_local[0]
     partial_factors = lax.dot_general(
-        factor_basis, gate_diff, (((1,), (1,)), ((), ())), precision=lax.Precision.HIGHEST
-    )
-    piece = lax.psum_scatter(partial_factors, "shard", scatter_dimension=0, tiled=True)
-    piece_other = swap(piece)
-
+        basis, gate_diff, (((1,), (1,)), ((), ())), precision=lax.Precision.HIGHEST
+    )
+    chain = factor_chain(partial_factors, bits)
+
+    stride = (chain_end - chain_start) // (2 * len(bits) + 1)
     parts = []
     cut = local
+    step_at = chain_start
+    step_sent = step_received = gate = None
     for i, (start, size) in enumerate(spans + mixed_spans):
         if i < len(spans):
             part = rows_of(cut, other + start, size)
@@ -107,23 +136,26 @@
         else:
             part = mixed[start : start + size]
         ties = [parts[i - window]] if i >= window else []
-        if i == after_scatter:
-            ties.append(piece)
-        if i == after_swap:
-            ties.append(piece_sum)
-        if i == after_gate:
-            ties += [new_gate_anchor, new_gate_moment]
+        if step_sent is not None:
+            ties.append(step_sent)
+            step_sent = None
+        if gate is not None and i == step_at + window:
+            ties += gate
         parts.append(swap(after(part, *ties)))
         if i == 0:
             norm_sent = after(norm_message(norm_local[0], norm_moment), parts[0])
             norm_received = swap(norm_sent)
-        if i == after_scatter:
-            piece_sum = piece + after(piece_other, parts[i - 1])
-            factors = lax.all_gather(piece_sum / groups, "shard", axis=0, tiled=True)
-            gate_delta = rebuild(factors, factor_basis)
-            new_gate_anchor, new_gate_moment = advance(gate_anchor, gate_moment, gate_delta)
+        if gate is None and i == step_at:
+            if step_received is not None:
+                step_received = after(step_received, parts[i - stride])
+            try:
+                step_sent, step_received = chain.send(step_received)
+                step_at += stride
+            except StopIteration as end:
+                gate = advance(gate_anchor, gate_moment, rebuild(end.value, basis))
+    new_gate_anchor, new_gate_moment = gate
     received, mixed_received = parts[: len(spans)], parts[len(spans) :]
-    norm_received = after(norm_received, parts[after_swap])
+    norm_received = after(norm_received, parts[chain_end])
     new_norm_anchor, new_norm_moment = norm_finish(
         norm_anchor, norm_local[0], norm_moment, norm_received
     )

time: 388 us -> 384 us (0.990)
  waiting for transfers between devices: 226 us -> 174 us
  starting transfers between devices: 45.5 us -> 90.3 us
  other arithmetic: 58.9 us -> 75.3 us
  between operations: 14.1 us -> 0.91 us
  matrix products: 28.8 us -> 24.3 us
  local copies, waits for them, and re-layouts: 11.3 us -> 15.8 us
    ppermute x20 -> x33, waiting for transfers between devices: 226 us -> 174 us  [swap(): return lax.ppermute(array, 'group', [(0, 1), (1, 0)])]
    ppermute x20 -> x33, starting transfers between devices: 45.5 us -> 85.8 us  [swap(): return lax.ppermute(array, 'group', [(0, 1), (1, 0)])]
    dynamic_update_slice x9 -> x16, other arithmetic: 16.8 us -> 27.3 us  [body(): lax.dynamic_update_slice_in_dim(anchor_next, value, other + start, 0)]
    unnamed x8 -> x16, other arithmetic: 19.5 us -> 28.2 us
    ppermute x0 -> x6, starting transfers between devices: none -> 4.52 us  [across(): return lax.ppermute(array, 'shard', [(i, i ^ k) for i in range(shards)])]
    unnamed x20 -> x55, local copies, waits for them, and re-layouts: 0.83 us -> 5.12 us
  transfers between devices with their start and end apart: 22 -> 39, of which waited for: 14 -> 22; matrix products, arithmetic and copies ran while one was open for 25% -> 29% of each run, Pallas kernels for 0% -> 0%
where the time goes in v4:
time: 384 us; the launch traced here: 380 us
  waiting for transfers between devices  174 us (45%)
  starting transfers between devices  90.3 us (24%)
  other arithmetic  75.3 us (20%)
  matrix products  24.3 us (6%)
  local copies, waits for them, and re-layouts  15.8 us (4%)
    ppermute x33, waiting for transfers between devices, swap(): return lax.ppermute(array, 'group', [(0, 1), (1, 0)])  174 us
    ppermute x33, starting transfers between devices, swap(): return lax.ppermute(array, 'group', [(0, 1), (1, 0)])  85.8 us
    unnamed x16, other arithmetic  28.2 us
    dynamic_update_slice x16, other arithmetic, body(): lax.dynamic_update_slice_in_dim(anchor_next, value, other + start, 0)  27.3 us
    dot_general x1, matrix products, rebuild(): lax.dot_general(factors, factor_basis, (((0,), (0,)), ((), ())), precisio...  12.6 us
    add x1, other arithmetic, body(): anchor_next = (1 - rate) * down_anchor + rate / 2 * local  12.2 us
    dot_general x1, matrix products, body(): lax.dot_general(basis, gate_diff, (((1,), (1,)), ((), ())), precision=lax...  11.7 us
  transfers between devices with their start and end apart: 39, of which 22 were waited for; matrix products, arithmetic and copies ran while one was open for 29% of the time, Pallas kernels for 0%

profile of v4, /device:TPU:10, one launch (start us, length us, event | category | flops | bytes accessed | tf_op | source)
XLA Modules:
  0.0 380.5 jit_solution(5707572654679645799)
XLA Ops:
  16.4 11.7 %fusion = f32[64,4096]{1,0:T(8,128)S(1)} fusion(f32[64,512]{1,0:T(8,128)S(1)} %constant_dynamic-update-slice_fusion, f32[4096,512]{1,0:T(8,128)} %param.16, f32[1,4096,512]{2,1,0:T(8,128)} %param.17), kind=kOutput, calls=%fused_computation.1 | convolution fusion | flops 1612709888 | bytes 17956864 | tf_op jit(solution)/shard_map/dot_general | solution.py:121
  35.9 12.2 %multiply_add_fusion.1 = f32[1024,2048]{1,0:T(8,128)} fusion(f32[1024,2048]{1,0:T(8,128)} %param.10, f32[1,1024,2048]{2,1,0:T(8,128)} %param.11), kind=kLoop, calls=%fused_computation.4 | loop fusion | flops 6291456 | bytes 25165824 | tf_op jit(solution)/shard_map/add | solution.py:163
  58.5 11.9 %collective-permute-done.3 = f32[32,2048]{1,0:T(8,128)S(1)} collective-permute-done((f32[32,2048]{1,0:T(8,128)S(1)}, f32[32,2048]{1,0:T(8,128)S(1)}, u32[]{:S(2)}, u32[]{:S(2)}) %collective-permute-start.3) | collective-permute-done | bytes 262176 | tf_op jit(solution)/shard_map/ppermute | solution.py:30
  78.2 9.1 %collective-permute-done.4 = f32[32,2048]{1,0:T(8,128)S(1)} collective-permute-done((f32[32,2048]{1,0:T(8,128)S(1)}, f32[32,2048]{1,0:T(8,128)S(1)}, u32[]{:S(2)}, u32[]{:S(2)}) %collective-permute-start.4) | collective-permute-done | bytes 262176 | tf_op jit(solution)/shard_map/ppermute | solution.py:30
  92.6 11.5 %collective-permute-done.5 = f32[32,2048]{1,0:T(8,128)S(1)} collective-permute-done((f32[32,2048]{1,0:T(8,128)S(1)}, f32[32,2048]{1,0:T(8,128)S(1)}, u32[]{:S(2)}, u32[]{:S(2)}) %collective-permute-start.5) | collective-permute-done | bytes 262176 | tf_op jit(solution)/shard_map/ppermute | solution.py:30
  113.1 10.7 %collective-permute-done.8 = f32[32,2048]{1,0:T(8,128)S(1)} collective-permute-done((f32[32,2048]{1,0:T(8,128)S(1)}, f32[32,2048]{1,0:T(8,128)S(1)}, u32[]{:S(2)}, u32[]{:S(2)}) %collective-permute-start.8) | collective-permute-done | bytes 262176 | tf_op jit(solution)/shard_map/ppermute | solution.py:30
  123.8 6.2 %collective-permute-start.12 = (f32[32,2048]{1,0:T(8,128)S(1)}, f32[32,2048]{1,0:T(8,128)S(1)}, u32[]{:S(2)}, u32[]{:S(2)}) collective-permute-start(f32[32,2048]{1,0:T(8,128)S(1)} %get-tuple-element.58), channel_id=1, source_target_pairs={{0,16},{16,0},{1,17},{17,1},{2,18},{18,2},{3,19},{19,3},{4,20},{20... | collective-permute-start | bytes 786440 | tf_op jit(solution)/shard_map/ppermute | solution.py:30
  132.1 5.8 %collective-permute-done.9 = f32[32,2048]{1,0:T(8,128)S(1)} collective-permute-done((f32[32,2048]{1,0:T(8,128)S(1)}, f32[32,2048]{1,0:T(8,128)S(1)}, u32[]{:S(2)}, u32[]{:S(2)}) %collective-permute-start.9) | collective-permute-done | bytes 262176 | tf_op jit(solution)/shard_map/ppermute | solution.py:30
  148.1 9.4 %collective-permute-done.12 = f32[32,2048]{1,0:T(8,128)S(1)} collective-permute-done((f32[32,2048]{1,0:T(8,128)S(1)}, f32[32,2048]{1,0:T(8,128)S(1)}, u32[]{:S(2)}, u32[]{:S(2)}) %collective-permute-start.12) | collective-permute-done | bytes 262176 | tf_op jit(solution)/shard_map/ppermute | solution.py:30
  165.9 5.6 %collective-permute-done.13 = f32[32,2048]{1,0:T(8,128)S(1)} collective-permute-done((f32[32,2048]{1,0:T(8,128)S(1)}, f32[32,2048]{1,0:T(8,128)S(1)}, u32[]{:S(2)}, u32[]{:S(2)}) %collective-permute-start.13) | collective-permute-done | bytes 262176 | tf_op jit(solution)/shard_map/ppermute | solution.py:30
  176.5 9.0 %collective-permute-done.15 = f32[32,2048]{1,0:T(8,128)S(1)} collective-permute-done((f32[32,2048]{1,0:T(8,128)S(1)}, f32[32,2048]{1,0:T(8,128)S(1)}, u32[]{:S(2)}, u32[]{:S(2)}) %collective-permute-start.15) | collective-permute-done | bytes 262176 | tf_op jit(solution)/shard_map/ppermute | solution.py:30
  185.6 6.2 %collective-permute-start.19 = (f32[32,2048]{1,0:T(8,128)S(1)}, f32[32,2048]{1,0:T(8,128)S(1)}, u32[]{:S(2)}, u32[]{:S(2)}) collective-permute-start(f32[32,2048]{1,0:T(8,128)S(1)} %copy-done.14), channel_id=1, source_target_pairs={{0,16},{16,0},{1,17},{17,1},{2,18},{18,2},{3,19},{19,3},{4,20},{20... | collective-permute-start | bytes 786440 | tf_op jit(solution)/shard_map/ppermute | solution.py:30
  205.9 5.0 %collective-permute-done.19 = f32[32,2048]{1,0:T(8,128)S(1)} collective-permute-done((f32[32,2048]{1,0:T(8,128)S(1)}, f32[32,2048]{1,0:T(8,128)S(1)}, u32[]{:S(2)}, u32[]{:S(2)}) %collective-permute-start.19) | collective-permute-done | bytes 262176 | tf_op jit(solution)/shard_map/ppermute | solution.py:30
  218.3 9.4 %collective-permute-done.20 = f32[32,2048]{1,0:T(8,128)S(1)} collective-permute-done((f32[32,2048]{1,0:T(8,128)S(1)}, f32[32,2048]{1,0:T(8,128)S(1)}, u32[]{:S(2)}, u32[]{:S(2)}) %collective-permute-start.20) | collective-permute-done | bytes 262176 | tf_op jit(solution)/shard_map/ppermute | solution.py:30
  232.8 11.8 %collective-permute-done.21 = f32[32,2048]{1,0:T(8,128)S(1)} collective-permute-done((f32[32,2048]{1,0:T(8,128)S(1)}, f32[32,2048]{1,0:T(8,128)S(1)}, u32[]{:S(2)}, u32[]{:S(2)}) %collective-permute-start.21) | collective-permute-done | bytes 262176 | tf_op jit(solution)/shard_map/ppermute | solution.py:30
  251.5 9.9 %collective-permute-done.24 = f32[32,2048]{1,0:T(8,128)S(1)} collective-permute-done((f32[32,2048]{1,0:T(8,128)S(1)}, f32[32,2048]{1,0:T(8,128)S(1)}, u32[]{:S(2)}, u32[]{:S(2)}) %collective-permute-start.24) | collective-permute-done | bytes 262176 | tf_op jit(solution)/shard_map/ppermute | solution.py:30
  266.5 6.2 %collective-permute-done.25 = f32[32,2048]{1,0:T(8,128)S(1)} collective-permute-done((f32[32,2048]{1,0:T(8,128)S(1)}, f32[32,2048]{1,0:T(8,128)S(1)}, u32[]{:S(2)}, u32[]{:S(2)}) %collective-permute-start.25) | collective-permute-done | bytes 262176 | tf_op jit(solution)/shard_map/ppermute | solution.py:30
  276.1 7.9 %collective-permute-done.27 = f32[32,2048]{1,0:T(8,128)S(1)} collective-permute-done((f32[32,2048]{1,0:T(8,128)S(1)}, f32[32,2048]{1,0:T(8,128)S(1)}, u32[]{:S(2)}, u32[]{:S(2)}) %collective-permute-start.27) | collective-permute-done | bytes 262176 | tf_op jit(solution)/shard_map/ppermute | solution.py:30
  300.2 6.2 %collective-permute-done.29 = f32[32,2048]{1,0:T(8,128)S(1)} collective-permute-done((f32[32,2048]{1,0:T(8,128)S(1)}, f32[32,2048]{1,0:T(8,128)S(1)}, u32[]{:S(2)}, u32[]{:S(2)}) %collective-permute-start.29) | collective-permute-done | bytes 262176 | tf_op jit(solution)/shard_map/ppermute | solution.py:30
  306.4 5.6 %collective-permute-done.30 = f32[32,2048]{1,0:T(8,128)S(1)} collective-permute-done((f32[32,2048]{1,0:T(8,128)S(1)}, f32[32,2048]{1,0:T(8,128)S(1)}, u32[]{:S(2)}, u32[]{:S(2)}) %collective-permute-start.30) | collective-permute-done | bytes 262176 | tf_op jit(solution)/shard_map/ppermute | solution.py:30
  320.0 12.6 %multiply_subtract_fusion = (f32[4096,512]{1,0:T(8,128)}, f32[4096,512]{1,0:T(8,128)}) fusion(f32[4096,512]{1,0:T(8,128)S(1)} %bitcast.138, f32[4096,512]{1,0:T(8,128)S(1)} %bitcast.140, f32[64,512]{1,0:T(8,128)S(1)} %constant_dynamic-update-slice_fusion, f32[32,4096]{1,0:T(8,128)S(1)} %collective-permute-done.32, ...), kind=kOutput, calls=%fused_computation.2 | convolution fusion | flops 1623982080 | bytes 34734080 | tf_op jit(solution)/shard_map/dot_general | solution.py:24
  337.2 18.9 %collective-permute-done.33 = f32[32,2048]{1,0:T(8,128)S(1)} collective-permute-done((f32[32,2048]{1,0:T(8,128)S(1)}, f32[32,2048]{1,0:T(8,128)S(1)}, u32[]{:S(2)}, u32[]{:S(2)}) %collective-permute-start.33) | collective-permute-done | bytes 262176 | tf_op jit(solution)/shard_map/ppermute | solution.py:30
  356.2 7.6 %collective-permute-start.36 = (f32[48,2048]{1,0:T(8,128)S(1)}, f32[48,2048]{1,0:T(8,128)S(1)}, u32[]{:S(2)}, u32[]{:S(2)}) collective-permute-start(f32[48,2048]{1,0:T(8,128)S(1)} %copy-done.1), channel_id=1, source_target_pairs={{0,16},{16,0},{1,17},{17,1},{2,18},{18,2},{3,19},{19,3},{4,20},{20... | collective-permute-start | bytes 1179656 | tf_op jit(solution)/shard_map/ppermute | solution.py:30
  368.8 8.3 %collective-permute-done.36 = f32[48,2048]{1,0:T(8,128)S(1)} collective-permute-done((f32[48,2048]{1,0:T(8,128)S(1)}, f32[48,2048]{1,0:T(8,128)S(1)}, u32[]{:S(2)}, u32[]{:S(2)}) %collective-permute-start.36) | collective-permute-done | bytes 393248 | tf_op jit(solution)/shard_map/ppermute | solution.py:30
  (166 shorter events, 161.0 us)
Async XLA Ops:
  2.2 48.1 %collective-permute-start = (f32[16,2048]{1,0:T(8,128)}, f32[16,2048]{1,0:T(8,128)}, u32[]{:S(2)}, u32[]{:S(2)}) collective-permute-start(f32[16,2048]{1,0:T(8,128)} %dynamic-slice_bitcast_fusion), channel_id=1, source_target_pairs={{0,16},{16,0},{1,17},{17,1},{2,18},{18,2},{3,19},{19,3},{4,20},{20... | collective-permute-start | bytes 393224 | tf_op jit(solution)/shard_map/ppermute | solution.py:30
  6.6 48.6 %collective-permute-start.1 = (f32[48,2048]{1,0:T(8,128)}, f32[48,2048]{1,0:T(8,128)}, u32[]{:S(2)}, u32[]{:S(2)}) collective-permute-start(f32[48,2048]{1,0:T(8,128)} %constant_dynamic-slice_fusion.24), channel_id=1, source_target_pairs={{0,16},{16,0},{1,17},{17,1},{2,18},{18,2},{3,19},{19,3},{4,20},{20... | collective-permute-start | bytes 1179656 | tf_op jit(solution)/shard_map/ppermute | solution.py:30
  8.0 49.8 %collective-permute-start.2 = (f32[64,2048]{1,0:T(8,128)S(1)}, f32[64,2048]{1,0:T(8,128)S(1)}, u32[]{:S(2)}, u32[]{:S(2)}) collective-permute-start(f32[64,2048]{1,0:T(8,128)S(1)} %constant_dynamic-slice_fusion.22), channel_id=1, source_target_pairs={{0,16},{16,0},{1,17},{17,1},{2,18},{18,2},{3,19},{19,3},{4,20},{20... | collective-permute-start | bytes 1572872 | tf_op jit(solution)/shard_map/ppermute | solution.py:30
  50.3 249.9 %collective-permute-start.38 = (f32[2,256]{1,0:T(2,128)S(1)}, f32[2,256]{1,0:T(2,128)S(1)}, u32[]{:S(2)}, u32[]{:S(2)}) collective-permute-start(f32[2,256]{1,0:T(2,128)S(1)} %subtract_select_fusion), channel_id=1, source_target_pairs={{0,16},{16,0},{1,17},{17,1},{2,18},{18,2},{3,19},{19,3},{4,20},{20... | collective-permute-start | bytes 6152 | tf_op jit(solution)/shard_map/ppermute | solution.py:30
  55.2 32.1 %collective-permute-start.4 = (f32[32,2048]{1,0:T(8,128)S(1)}, f32[32,2048]{1,0:T(8,128)S(1)}, u32[]{:S(2)}, u32[]{:S(2)}) collective-permute-start(f32[32,2048]{1,0:T(8,128)S(1)} %get-tuple-element.50), channel_id=1, source_target_pairs={{0,16},{16,0},{1,17},{17,1},{2,18},{18,2},{3,19},{19,3},{4,20},{20... | collective-permute-start | bytes 786440 | tf_op jit(solution)/shard_map/ppermute | solution.py:30
  57.9 34.6 %collective-permute-start.10 = (f32[16,4096]{1,0:T(8,128)S(1)}, f32[16,4096]{1,0:T(8,128)S(1)}, u32[]{:S(2)}, u32[]{:S(2)}) collective-permute-start(f32[16,4096]{1,0:T(8,128)S(1)} %slice.153), channel_id=1, source_target_pairs={{0,4},{2,6},{4,0},{6,2},{8,12},{10,14},{12,8},{14,10},{1,5},{3,7},... | collective-permute-start | bytes 786440 | tf_op jit(solution)/shard_map/ppermute | solution.py:35
  70.4 35.3 %collective-permute-start.7 = (f32[32,2048]{1,0:T(8,128)S(1)}, f32[32,2048]{1,0:T(8,128)S(1)}, u32[]{:S(2)}, u32[]{:S(2)}) collective-permute-start(f32[32,2048]{1,0:T(8,128)S(1)} %get-tuple-element.53), channel_id=1, source_target_pairs={{0,16},{16,0},{1,17},{17,1},{2,18},{18,2},{3,19},{19,3},{4,20},{20... | collective-permute-start | bytes 786440 | tf_op jit(solution)/shard_map/ppermute | solution.py:30
  73.8 30.3 %collective-permute-start.5 = (f32[32,2048]{1,0:T(8,128)S(1)}, f32[32,2048]{1,0:T(8,128)S(1)}, u32[]{:S(2)}, u32[]{:S(2)}) collective-permute-start(f32[32,2048]{1,0:T(8,128)S(1)} %get-tuple-element.51), channel_id=1, source_target_pairs={{0,16},{16,0},{1,17},{17,1},{2,18},{18,2},{3,19},{19,3},{4,20},{20... | collective-permute-start | bytes 786440 | tf_op jit(solution)/shard_map/ppermute | solution.py:30
  87.3 36.5 %collective-permute-start.8 = (f32[32,2048]{1,0:T(8,128)S(1)}, f32[32,2048]{1,0:T(8,128)S(1)}, u32[]{:S(2)}, u32[]{:S(2)}) collective-permute-start(f32[32,2048]{1,0:T(8,128)S(1)} %get-tuple-element.54), channel_id=1, source_target_pairs={{0,16},{16,0},{1,17},{17,1},{2,18},{18,2},{3,19},{19,3},{4,20},{20... | collective-permute-start | bytes 786440 | tf_op jit(solution)/shard_map/ppermute | solution.py:30
  105.8 35.5 %collective-permute-start.11 = (f32[32,2048]{1,0:T(8,128)S(1)}, f32[32,2048]{1,0:T(8,128)S(1)}, u32[]{:S(2)}, u32[]{:S(2)}) collective-permute-start(f32[32,2048]{1,0:T(8,128)S(1)} %get-tuple-element.57), channel_id=1, source_target_pairs={{0,16},{16,0},{1,17},{17,1},{2,18},{18,2},{3,19},{19,3},{4,20},{20... | collective-permute-start | bytes 786440 | tf_op jit(solution)/shard_map/ppermute | solution.py:30
  123.8 33.7 %collective-permute-start.12 = (f32[32,2048]{1,0:T(8,128)S(1)}, f32[32,2048]{1,0:T(8,128)S(1)}, u32[]{:S(2)}, u32[]{:S(2)}) collective-permute-start(f32[32,2048]{1,0:T(8,128)S(1)} %get-tuple-element.58), channel_id=1, source_target_pairs={{0,16},{16,0},{1,17},{17,1},{2,18},{18,2},{3,19},{19,3},{4,20},{20... | collective-permute-start | bytes 786440 | tf_op jit(solution)/shard_map/ppermute | solution.py:30
  141.4 44.2 %collective-permute-start.15 = (f32[32,2048]{1,0:T(8,128)S(1)}, f32[32,2048]{1,0:T(8,128)S(1)}, u32[]{:S(2)}, u32[]{:S(2)}) collective-permute-start(f32[32,2048]{1,0:T(8,128)S(1)} %get-tuple-element.61), channel_id=1, source_target_pairs={{0,16},{16,0},{1,17},{17,1},{2,18},{18,2},{3,19},{19,3},{4,20},{20... | collective-permute-start | bytes 786440 | tf_op jit(solution)/shard_map/ppermute | solution.py:30
  157.5 42.1 %collective-permute-start.16 = (f32[32,2048]{1,0:T(8,128)S(1)}, f32[32,2048]{1,0:T(8,128)S(1)}, u32[]{:S(2)}, u32[]{:S(2)}) collective-permute-start(f32[32,2048]{1,0:T(8,128)S(1)} %get-tuple-element.62), channel_id=1, source_target_pairs={{0,16},{16,0},{1,17},{17,1},{2,18},{18,2},{3,19},{19,3},{4,20},{20... | collective-permute-start | bytes 786440 | tf_op jit(solution)/shard_map/ppermute | solution.py:30
  171.6 33.5 %collective-permute-start.22 = (f32[8,4096]{1,0:T(8,128)S(1)}, f32[8,4096]{1,0:T(8,128)S(1)}, u32[]{:S(2)}, u32[]{:S(2)}) collective-permute-start(f32[8,4096]{1,0:T(8,128)S(1)} %add_multiply_fusion), channel_id=1, source_target_pairs={{0,8},{2,10},{4,12},{6,14},{8,0},{10,2},{12,4},{14,6},{1,9},{3,11}... | collective-permute-start | bytes 393224 | tf_op jit(solution)/shard_map/ppermute | solution.py:35
  173.2 32.1 %collective-permute-start.17 = (f32[32,2048]{1,0:T(8,128)S(1)}, f32[32,2048]{1,0:T(8,128)S(1)}, u32[]{:S(2)}, u32[]{:S(2)}) collective-permute-start(f32[32,2048]{1,0:T(8,128)S(1)} %get-tuple-element.63), channel_id=1, source_target_pairs={{0,16},{16,0},{1,17},{17,1},{2,18},{18,2},{3,19},{19,3},{4,20},{20... | collective-permute-start | bytes 786440 | tf_op jit(solution)/shard_map/ppermute | solution.py:30
  210.9 37.2 %collective-permute-start.23 = (f32[32,2048]{1,0:T(8,128)S(1)}, f32[32,2048]{1,0:T(8,128)S(1)}, u32[]{:S(2)}, u32[]{:S(2)}) collective-permute-start(f32[32,2048]{1,0:T(8,128)S(1)} %copy-done.11), channel_id=1, source_target_pairs={{0,16},{16,0},{1,17},{17,1},{2,18},{18,2},{3,19},{19,3},{4,20},{20... | collective-permute-start | bytes 786440 | tf_op jit(solution)/shard_map/ppermute | solution.py:30
  227.7 33.7 %collective-permute-start.24 = (f32[32,2048]{1,0:T(8,128)S(1)}, f32[32,2048]{1,0:T(8,128)S(1)}, u32[]{:S(2)}, u32[]{:S(2)}) collective-permute-start(f32[32,2048]{1,0:T(8,128)S(1)} %copy-done.10), channel_id=1, source_target_pairs={{0,16},{16,0},{1,17},{17,1},{2,18},{18,2},{3,19},{19,3},{4,20},{20... | collective-permute-start | bytes 786440 | tf_op jit(solution)/shard_map/ppermute | solution.py:30
  248.0 71.9 %collective-permute-start.32 = (f32[32,4096]{1,0:T(8,128)S(1)}, f32[32,4096]{1,0:T(8,128)S(1)}, u32[]{:S(2)}, u32[]{:S(2)}) collective-permute-start(f32[32,4096]{1,0:T(8,128)S(1)} %pad_maximum_fusion), channel_id=1, source_target_pairs={{0,2},{2,0},{4,6},{6,4},{8,10},{10,8},{12,14},{14,12},{1,3},{3,1},... | collective-permute-start | bytes 1572872 | tf_op jit(solution)/shard_map/ppermute | solution.py:35
  248.1 35.8 %collective-permute-start.27 = (f32[32,2048]{1,0:T(8,128)S(1)}, f32[32,2048]{1,0:T(8,128)S(1)}, u32[]{:S(2)}, u32[]{:S(2)}) collective-permute-start(f32[32,2048]{1,0:T(8,128)S(1)} %copy-done.8), channel_id=1, source_target_pairs={{0,16},{16,0},{1,17},{17,1},{2,18},{18,2},{3,19},{19,3},{4,20},{20... | collective-permute-start | bytes 786440 | tf_op jit(solution)/shard_map/ppermute | solution.py:30
  261.4 33.7 %collective-permute-start.28 = (f32[32,2048]{1,0:T(8,128)S(1)}, f32[32,2048]{1,0:T(8,128)S(1)}, u32[]{:S(2)}, u32[]{:S(2)}) collective-permute-start(f32[32,2048]{1,0:T(8,128)S(1)} %copy-done.7), channel_id=1, source_target_pairs={{0,16},{16,0},{1,17},{17,1},{2,18},{18,2},{3,19},{19,3},{4,20},{20... | collective-permute-start | bytes 786440 | tf_op jit(solution)/shard_map/ppermute | solution.py:30
  272.7 33.7 %collective-permute-start.29 = (f32[32,2048]{1,0:T(8,128)S(1)}, f32[32,2048]{1,0:T(8,128)S(1)}, u32[]{:S(2)}, u32[]{:S(2)}) collective-permute-start(f32[32,2048]{1,0:T(8,128)S(1)} %copy-done.6), channel_id=1, source_target_pairs={{0,16},{16,0},{1,17},{17,1},{2,18},{18,2},{3,19},{19,3},{4,20},{20... | collective-permute-start | bytes 786440 | tf_op jit(solution)/shard_map/ppermute | solution.py:30
  295.1 37.4 %collective-permute-start.31 = (f32[32,2048]{1,0:T(8,128)S(1)}, f32[32,2048]{1,0:T(8,128)S(1)}, u32[]{:S(2)}, u32[]{:S(2)}) collective-permute-start(f32[32,2048]{1,0:T(8,128)S(1)} %copy-done.4), channel_id=1, source_target_pairs={{0,16},{16,0},{1,17},{17,1},{2,18},{18,2},{3,19},{19,3},{4,20},{20... | collective-permute-start | bytes 786440 | tf_op jit(solution)/shard_map/ppermute | solution.py:30
  332.6 34.5 %collective-permute-start.35 = (f32[32,2048]{1,0:T(8,128)S(1)}, f32[32,2048]{1,0:T(8,128)S(1)}, u32[]{:S(2)}, u32[]{:S(2)}) collective-permute-start(f32[32,2048]{1,0:T(8,128)S(1)} %get-tuple-element.81), channel_id=1, source_target_pairs={{0,16},{16,0},{1,17},{17,1},{2,18},{18,2},{3,19},{19,3},{4,20},{20... | collective-permute-start | bytes 786440 | tf_op jit(solution)/shard_map/ppermute | solution.py:30
  337.2 41.8 %collective-permute-start.37 = (f32[16,2048]{1,0:T(8,128)S(1)}, f32[16,2048]{1,0:T(8,128)S(1)}, u32[]{:S(2)}, u32[]{:S(2)}) collective-permute-start(f32[16,2048]{1,0:T(8,128)S(1)} %copy-done.15), channel_id=1, source_target_pairs={{0,16},{16,0},{1,17},{17,1},{2,18},{18,2},{3,19},{19,3},{4,20},{20... | collective-permute-start | bytes 393224 | tf_op jit(solution)/shard_map/ppermute | solution.py:30
  (39 other events, 2744.3 us)

commit v5 on v4

--- a/solution.py
+++ b/solution.py
@@ -8,7 +8,7 @@
 rate = outer_rate * (1 + momentum)
 decay = outer_rate * momentum * momentum
 first_sizes = (1, 3, 4) + (2,) * 12
-last_sizes = (2,) * 14 + (3, 1)
+last_sizes = (2,) * 14 + (1, 1, 1, 1)
 window = 3
 chain_start = 2
 chain_end = 23
@@ -105,7 +105,6 @@
 
     spans = list(pieces(half, first_sizes))
     mixed_spans = list(pieces(half, last_sizes))
-    mixed = (rate / 2) * rows_of(local, own, half) - decay * down_moment
 
     shards = lax.axis_size("shard")
     bits = [1 << n for n in range(shards.bit_length() - 1)]
@@ -142,6 +141,9 @@
         if gate is not None and i == step_at + window:
             ties += gate
         parts.append(swap(after(part, *ties)))
+        if i == 1:
+            mixed = (rate / 2) * rows_of(local, own, half) - decay * after(down_moment, parts[1])
+            anchor_next = (1 - rate) * after(down_anchor, parts[1]) + (rate / 2) * local
         if i == 0:
             norm_sent = after(norm_message(norm_local[0], norm_moment), parts[0])
             norm_received = swap(norm_sent)
@@ -160,7 +162,6 @@
         norm_anchor, norm_local[0], norm_moment, norm_received
     )
 
-    anchor_next = (1 - rate) * down_anchor + (rate / 2) * local
     moment_next = []
     for (start, size), part in zip(spans, received):
         old = down_moment[start : start + size]

time: 384 us -> 385 us (level)
  waiting for transfers between devices: 174 us -> 220 us
  other arithmetic: 75.3 us -> 37.6 us
  starting transfers between devices: 90.3 us -> 79.9 us
    ppermute x33 -> x35, waiting for transfers between devices: 174 us -> 220 us  [swap(): return lax.ppermute(array, 'group', [(0, 1), (1, 0)])]
    dynamic_update_slice x16 -> x18, other arithmetic: 27.3 us -> 0.71 us  [body(): lax.dynamic_update_slice_in_dim(anchor_next, value, other + start, 0)]
    unnamed x16 -> x15, other arithmetic: 28.2 us -> 19.1 us
    ppermute x33 -> x35, starting transfers between devices: 85.8 us -> 78.2 us  [swap(): return lax.ppermute(array, 'group', [(0, 1), (1, 0)])]
    unnamed x55 -> x57, local copies, waits for them, and re-layouts: 5.12 us -> 9.26 us
  transfers between devices with their start and end apart: 39 -> 41, of which waited for: 22 -> 25; matrix products, arithmetic and copies ran while one was open for 29% -> 20% of each run, Pallas kernels for 0% -> 0%
where the time goes in v5:
time: 385 us; the launch traced here: 384 us
  waiting for transfers between devices  220 us (57%)
  starting transfers between devices  79.9 us (21%)
  other arithmetic  37.6 us (10%)
  matrix products  26.4 us (7%)
  local copies, waits for them, and re-layouts  19.5 us (5%)
    ppermute x35, waiting for transfers between devices, swap(): return lax.ppermute(array, 'group', [(0, 1), (1, 0)])  220 us
    ppermute x35, starting transfers between devices, swap(): return lax.ppermute(array, 'group', [(0, 1), (1, 0)])  78.2 us
    unnamed x15, other arithmetic  19.1 us
    dot_general x1, matrix products, rebuild(): lax.dot_general(factors, factor_basis, (((0,), (0,)), ((), ())), precisio...  14.6 us
    add x1, other arithmetic, body(): anchor_next = (1 - rate) * after(down_anchor, parts[1]) + rate / 2 * local  12.1 us
    dot_general x1, matrix products, body(): lax.dot_general(basis, gate_diff, (((1,), (1,)), ((), ())), precision=lax...  11.8 us
    unnamed x57, local copies, waits for them, and re-layouts  9.26 us
  transfers between devices with their start and end apart: 41, of which 25 were waited for; matrix products, arithmetic and copies ran while one was open for 20% of the time, Pallas kernels for 0%

profile of v5, /device:TPU:10, one launch (start us, length us, event | category | flops | bytes accessed | tf_op | source)
XLA Modules:
  0.0 384.3 jit_solution(16915169788772989318)
XLA Ops:
  15.9 11.8 %fusion = f32[64,4096]{1,0:T(8,128)S(1)} fusion(f32[64,512]{1,0:T(8,128)S(1)} %constant_dynamic-update-slice_fusion, f32[4096,512]{1,0:T(8,128)} %param.16, f32[1,4096,512]{2,1,0:T(8,128)} %param.17), kind=kOutput, calls=%fused_computation.1 | convolution fusion | flops 1612709888 | bytes 17956864 | tf_op jit(solution)/shard_map/dot_general | solution.py:120
  27.8 3.7 constant_dynamic-slice_fusion.1
  34.5 9.0 %collective-permute-done = f32[48,2048]{1,0:T(8,128)S(1)} collective-permute-done((f32[48,2048]{1,0:T(8,128)S(1)}, f32[48,2048]{1,0:T(8,128)S(1)}, u32[]{:S(2)}, u32[]{:S(2)}) %collective-permute-start) | collective-permute-done | bytes 393248 | tf_op jit(solution)/shard_map/ppermute | solution.py:30
  51.6 12.1 %multiply_add_fusion.1 = f32[1024,2048]{1,0:T(8,128)} fusion(f32[1024,2048]{1,0:T(8,128)} %param.10, f32[1,1024,2048]{2,1,0:T(8,128)} %param.11), kind=kLoop, calls=%fused_computation.4 | loop fusion | flops 6291456 | bytes 25165824 | tf_op jit(solution)/shard_map/add | solution.py:146
  75.8 12.8 %collective-permute-done.4 = f32[32,2048]{1,0:T(8,128)} collective-permute-done((f32[32,2048]{1,0:T(8,128)}, f32[32,2048]{1,0:T(8,128)}, u32[]{:S(2)}, u32[]{:S(2)}) %collective-permute-start.4) | collective-permute-done | bytes 262176 | tf_op jit(solution)/shard_map/ppermute | solution.py:30
  93.2 24.8 %collective-permute-done.5 = f32[32,2048]{1,0:T(8,128)S(1)} collective-permute-done((f32[32,2048]{1,0:T(8,128)}, f32[32,2048]{1,0:T(8,128)S(1)}, u32[]{:S(2)}, u32[]{:S(2)}) %collective-permute-start.5) | collective-permute-done | bytes 262176 | tf_op jit(solution)/shard_map/ppermute | solution.py:30
  124.0 17.9 %collective-permute-done.8 = f32[32,2048]{1,0:T(8,128)S(1)} collective-permute-done((f32[32,2048]{1,0:T(8,128)S(1)}, f32[32,2048]{1,0:T(8,128)S(1)}, u32[]{:S(2)}, u32[]{:S(2)}) %collective-permute-start.8) | collective-permute-done | bytes 262176 | tf_op jit(solution)/shard_map/ppermute | solution.py:30
  146.4 43.1 %collective-permute-done.9 = f32[32,2048]{1,0:T(8,128)S(1)} collective-permute-done((f32[32,2048]{1,0:T(8,128)S(1)}, f32[32,2048]{1,0:T(8,128)S(1)}, u32[]{:S(2)}, u32[]{:S(2)}) %collective-permute-start.9) | collective-permute-done | bytes 262176 | tf_op jit(solution)/shard_map/ppermute | solution.py:30
  189.6 3.5 collective-permute-start.18
  198.3 11.0 %collective-permute-done.12 = f32[32,2048]{1,0:T(8,128)S(1)} collective-permute-done((f32[32,2048]{1,0:T(8,128)S(1)}, f32[32,2048]{1,0:T(8,128)S(1)}, u32[]{:S(2)}, u32[]{:S(2)}) %collective-permute-start.12) | collective-permute-done | bytes 262176 | tf_op jit(solution)/shard_map/ppermute | solution.py:30
  214.8 5.7 %collective-permute-done.13 = f32[32,2048]{1,0:T(8,128)S(1)} collective-permute-done((f32[32,2048]{1,0:T(8,128)S(1)}, f32[32,2048]{1,0:T(8,128)S(1)}, u32[]{:S(2)}, u32[]{:S(2)}) %collective-permute-start.13) | collective-permute-done | bytes 262176 | tf_op jit(solution)/shard_map/ppermute | solution.py:30
  220.6 3.4 collective-permute-start.17
  224.1 10.4 %collective-permute-done.15 = f32[32,2048]{1,0:T(8,128)S(1)} collective-permute-done((f32[32,2048]{1,0:T(8,128)S(1)}, f32[32,2048]{1,0:T(8,128)S(1)}, u32[]{:S(2)}, u32[]{:S(2)}) %collective-permute-start.15) | collective-permute-done | bytes 262176 | tf_op jit(solution)/shard_map/ppermute | solution.py:30
  234.5 6.2 %collective-permute-start.19 = (f32[32,2048]{1,0:T(8,128)S(1)}, f32[32,2048]{1,0:T(8,128)S(1)}, u32[]{:S(2)}, u32[]{:S(2)}) collective-permute-start(f32[32,2048]{1,0:T(8,128)S(1)} %get-tuple-element.71), channel_id=1, source_target_pairs={{0,16},{16,0},{1,17},{17,1},{2,18},{18,2},{3,19},{19,3},{4,20},{20... | collective-permute-start | bytes 786440 | tf_op jit(solution)/shard_map/ppermute | solution.py:30
  252.0 7.8 %collective-permute-done.19 = f32[32,2048]{1,0:T(8,128)S(1)} collective-permute-done((f32[32,2048]{1,0:T(8,128)S(1)}, f32[32,2048]{1,0:T(8,128)S(1)}, u32[]{:S(2)}, u32[]{:S(2)}) %collective-permute-start.19) | collective-permute-done | bytes 262176 | tf_op jit(solution)/shard_map/ppermute | solution.py:30
  264.5 3.8 collective-permute-done.20
  271.7 26.0 %collective-permute-done.21 = f32[32,2048]{1,0:T(8,128)S(1)} collective-permute-done((f32[32,2048]{1,0:T(8,128)S(1)}, f32[32,2048]{1,0:T(8,128)S(1)}, u32[]{:S(2)}, u32[]{:S(2)}) %collective-permute-start.21) | collective-permute-done | bytes 262176 | tf_op jit(solution)/shard_map/ppermute | solution.py:30
  301.5 4.7 %collective-permute-done.24 = f32[32,2048]{1,0:T(8,128)S(1)} collective-permute-done((f32[32,2048]{1,0:T(8,128)S(1)}, f32[32,2048]{1,0:T(8,128)S(1)}, u32[]{:S(2)}, u32[]{:S(2)}) %collective-permute-start.24) | collective-permute-done | bytes 262176 | tf_op jit(solution)/shard_map/ppermute | solution.py:30
  328.7 5.6 %collective-permute-done.30 = f32[32,2048]{1,0:T(8,128)S(1)} collective-permute-done((f32[32,2048]{1,0:T(8,128)S(1)}, f32[32,2048]{1,0:T(8,128)S(1)}, u32[]{:S(2)}, u32[]{:S(2)}) %collective-permute-start.30) | collective-permute-done | bytes 262176 | tf_op jit(solution)/shard_map/ppermute | solution.py:30
  339.0 14.6 %multiply_subtract_fusion = (f32[4096,512]{1,0:T(8,128)}, f32[4096,512]{1,0:T(8,128)}) fusion(f32[4096,512]{1,0:T(8,128)S(1)} %bitcast.138, f32[4096,512]{1,0:T(8,128)} %param.18, f32[64,512]{1,0:T(8,128)S(1)} %constant_dynamic-update-slice_fusion, f32[32,4096]{1,0:T(8,128)S(1)} %collective-permute-done.32, f32[16,4096]{1,0:T(8,128)S(1)} %collective-permute-done.26, ...), kind=kOutput, calls=%fused_computation.2 | convolution fusion | flops 1623982080 | bytes 34734080 | tf_op jit(solution)/shard_map/dot_general | solution.py:24
  356.8 7.0 %collective-permute-done.33 = f32[32,2048]{1,0:T(8,128)S(1)} collective-permute-done((f32[32,2048]{1,0:T(8,128)S(1)}, f32[32,2048]{1,0:T(8,128)S(1)}, u32[]{:S(2)}, u32[]{:S(2)}) %collective-permute-start.33) | collective-permute-done | bytes 262176 | tf_op jit(solution)/shard_map/ppermute | solution.py:30
  363.8 5.5 %collective-permute-done.35 = f32[32,2048]{1,0:T(8,128)S(1)} collective-permute-done((f32[32,2048]{1,0:T(8,128)S(1)}, f32[32,2048]{1,0:T(8,128)S(1)}, u32[]{:S(2)}, u32[]{:S(2)}) %collective-permute-start.35) | collective-permute-done | bytes 262176 | tf_op jit(solution)/shard_map/ppermute | solution.py:30
  369.4 5.6 %collective-permute-done.36 = f32[16,2048]{1,0:T(8,128)S(1)} collective-permute-done((f32[16,2048]{1,0:T(8,128)S(1)}, f32[16,2048]{1,0:T(8,128)S(1)}, u32[]{:S(2)}, u32[]{:S(2)}) %collective-permute-start.36) | collective-permute-done | bytes 131104 | tf_op jit(solution)/shard_map/ppermute | solution.py:30
  376.9 3.9 %collective-permute-done.39 = f32[16,2048]{1,0:T(8,128)S(1)} collective-permute-done((f32[16,2048]{1,0:T(8,128)S(1)}, f32[16,2048]{1,0:T(8,128)S(1)}, u32[]{:S(2)}, u32[]{:S(2)}) %collective-permute-start.39) | collective-permute-done | bytes 131104 | tf_op jit(solution)/shard_map/ppermute | solution.py:30
  (172 shorter events, 123.1 us)
Async XLA Ops:
  1.6 29.9 %collective-permute-start.1 = (f32[16,2048]{1,0:T(8,128)S(1)}, f32[16,2048]{1,0:T(8,128)S(1)}, u32[]{:S(2)}, u32[]{:S(2)}) collective-permute-start(f32[16,2048]{1,0:T(8,128)S(1)} %dynamic-slice_bitcast_fusion), channel_id=1, source_target_pairs={{0,16},{16,0},{1,17},{17,1},{2,18},{18,2},{3,19},{19,3},{4,20},{20... | collective-permute-start | bytes 393224 | tf_op jit(solution)/shard_map/ppermute | solution.py:30
  5.2 38.3 %collective-permute-start = (f32[48,2048]{1,0:T(8,128)S(1)}, f32[48,2048]{1,0:T(8,128)S(1)}, u32[]{:S(2)}, u32[]{:S(2)}) collective-permute-start(f32[48,2048]{1,0:T(8,128)S(1)} %constant_dynamic-slice_fusion.24), channel_id=1, source_target_pairs={{0,16},{16,0},{1,17},{17,1},{2,18},{18,2},{3,19},{19,3},{4,20},{20... | collective-permute-start | bytes 1179656 | tf_op jit(solution)/shard_map/ppermute | solution.py:30
  7.5 61.6 %collective-permute-start.2 = (f32[64,2048]{1,0:T(8,128)}, f32[64,2048]{1,0:T(8,128)}, u32[]{:S(2)}, u32[]{:S(2)}) collective-permute-start(f32[64,2048]{1,0:T(8,128)} %constant_dynamic-slice_fusion.22), channel_id=1, source_target_pairs={{0,16},{16,0},{1,17},{17,1},{2,18},{18,2},{3,19},{19,3},{4,20},{20... | collective-permute-start | bytes 1572872 | tf_op jit(solution)/shard_map/ppermute | solution.py:30
  27.7 41.5 %collective-permute-start.6 = (f32[32,4096]{1,0:T(8,128)S(1)}, f32[32,4096]{1,0:T(8,128)S(1)}, u32[]{:S(2)}, u32[]{:S(2)}) collective-permute-start(f32[32,4096]{1,0:T(8,128)S(1)} %slice.159), channel_id=1, source_target_pairs={{0,2},{2,0},{4,6},{6,4},{8,10},{10,8},{12,14},{14,12},{1,3},{3,1},... | collective-permute-start | bytes 1572872 | tf_op jit(solution)/shard_map/ppermute | solution.py:35
  31.5 295.0 %collective-permute-start.40 = (f32[2,256]{1,0:T(2,128)S(1)}, f32[2,256]{1,0:T(2,128)S(1)}, u32[]{:S(2)}, u32[]{:S(2)}) collective-permute-start(f32[2,256]{1,0:T(2,128)S(1)} %subtract_select_fusion), channel_id=1, source_target_pairs={{0,16},{16,0},{1,17},{17,1},{2,18},{18,2},{3,19},{19,3},{4,20},{20... | collective-permute-start | bytes 6152 | tf_op jit(solution)/shard_map/ppermute | solution.py:30
  32.8 37.1 %collective-permute-start.3 = (f32[32,2048]{1,0:T(8,128)}, f32[32,2048]{1,0:T(8,128)}, u32[]{:S(2)}, u32[]{:S(2)}) collective-permute-start(f32[32,2048]{1,0:T(8,128)} %get-tuple-element.54), channel_id=1, source_target_pairs={{0,16},{16,0},{1,17},{17,1},{2,18},{18,2},{3,19},{19,3},{4,20},{20... | collective-permute-start | bytes 786440 | tf_op jit(solution)/shard_map/ppermute | solution.py:30
  44.3 44.3 %collective-permute-start.4 = (f32[32,2048]{1,0:T(8,128)}, f32[32,2048]{1,0:T(8,128)}, u32[]{:S(2)}, u32[]{:S(2)}) collective-permute-start(f32[32,2048]{1,0:T(8,128)} %get-tuple-element.55), channel_id=1, source_target_pairs={{0,16},{16,0},{1,17},{17,1},{2,18},{18,2},{3,19},{19,3},{4,20},{20... | collective-permute-start | bytes 786440 | tf_op jit(solution)/shard_map/ppermute | solution.py:30
  69.9 48.5 %collective-permute-start.7 = (f32[32,2048]{1,0:T(8,128)S(1)}, f32[32,2048]{1,0:T(8,128)S(1)}, u32[]{:S(2)}, u32[]{:S(2)}) collective-permute-start(f32[32,2048]{1,0:T(8,128)S(1)} %copy-done.14), channel_id=1, source_target_pairs={{0,16},{16,0},{1,17},{17,1},{2,18},{18,2},{3,19},{19,3},{4,20},{20... | collective-permute-start | bytes 786440 | tf_op jit(solution)/shard_map/ppermute | solution.py:30
  69.9 48.2 %collective-permute-start.5 = (f32[32,2048]{1,0:T(8,128)}, f32[32,2048]{1,0:T(8,128)S(1)}, u32[]{:S(2)}, u32[]{:S(2)}) collective-permute-start(f32[32,2048]{1,0:T(8,128)} %get-tuple-element.56), channel_id=1, source_target_pairs={{0,16},{16,0},{1,17},{17,1},{2,18},{18,2},{3,19},{19,3},{4,20},{20... | collective-permute-start | bytes 786440 | tf_op jit(solution)/shard_map/ppermute | solution.py:30
  88.6 53.3 %collective-permute-start.8 = (f32[32,2048]{1,0:T(8,128)S(1)}, f32[32,2048]{1,0:T(8,128)S(1)}, u32[]{:S(2)}, u32[]{:S(2)}) collective-permute-start(f32[32,2048]{1,0:T(8,128)S(1)} %copy-done.13), channel_id=1, source_target_pairs={{0,16},{16,0},{1,17},{17,1},{2,18},{18,2},{3,19},{19,3},{4,20},{20... | collective-permute-start | bytes 786440 | tf_op jit(solution)/shard_map/ppermute | solution.py:30
  118.1 28.3 %collective-permute-start.14 = (f32[8,4096]{1,0:T(8,128)S(1)}, f32[8,4096]{1,0:T(8,128)S(1)}, u32[]{:S(2)}, u32[]{:S(2)}) collective-permute-start(f32[8,4096]{1,0:T(8,128)S(1)} %slice.163), channel_id=1, source_target_pairs={{0,8},{2,10},{4,12},{6,14},{8,0},{10,2},{12,4},{14,6},{1,9},{3,11}... | collective-permute-start | bytes 393224 | tf_op jit(solution)/shard_map/ppermute | solution.py:35
  118.3 74.7 %collective-permute-start.11 = (f32[32,2048]{1,0:T(8,128)S(1)}, f32[32,2048]{1,0:T(8,128)S(1)}, u32[]{:S(2)}, u32[]{:S(2)}) collective-permute-start(f32[32,2048]{1,0:T(8,128)S(1)} %copy-done.11), channel_id=1, source_target_pairs={{0,16},{16,0},{1,17},{17,1},{2,18},{18,2},{3,19},{19,3},{4,20},{20... | collective-permute-start | bytes 786440 | tf_op jit(solution)/shard_map/ppermute | solution.py:30
  121.6 67.9 %collective-permute-start.9 = (f32[32,2048]{1,0:T(8,128)S(1)}, f32[32,2048]{1,0:T(8,128)S(1)}, u32[]{:S(2)}, u32[]{:S(2)}) collective-permute-start(f32[32,2048]{1,0:T(8,128)S(1)} %copy-done.12), channel_id=1, source_target_pairs={{0,16},{16,0},{1,17},{17,1},{2,18},{18,2},{3,19},{19,3},{4,20},{20... | collective-permute-start | bytes 786440 | tf_op jit(solution)/shard_map/ppermute | solution.py:30
  141.9 67.4 %collective-permute-start.12 = (f32[32,2048]{1,0:T(8,128)S(1)}, f32[32,2048]{1,0:T(8,128)S(1)}, u32[]{:S(2)}, u32[]{:S(2)}) collective-permute-start(f32[32,2048]{1,0:T(8,128)S(1)} %copy-done.10), channel_id=1, source_target_pairs={{0,16},{16,0},{1,17},{17,1},{2,18},{18,2},{3,19},{19,3},{4,20},{20... | collective-permute-start | bytes 786440 | tf_op jit(solution)/shard_map/ppermute | solution.py:30
  193.1 27.4 %collective-permute-start.13 = (f32[32,2048]{1,0:T(8,128)S(1)}, f32[32,2048]{1,0:T(8,128)S(1)}, u32[]{:S(2)}, u32[]{:S(2)}) collective-permute-start(f32[32,2048]{1,0:T(8,128)S(1)} %copy-done.9), channel_id=1, source_target_pairs={{0,16},{16,0},{1,17},{17,1},{2,18},{18,2},{3,19},{19,3},{4,20},{20... | collective-permute-start | bytes 786440 | tf_op jit(solution)/shard_map/ppermute | solution.py:30
  193.2 41.3 %collective-permute-start.15 = (f32[32,2048]{1,0:T(8,128)S(1)}, f32[32,2048]{1,0:T(8,128)S(1)}, u32[]{:S(2)}, u32[]{:S(2)}) collective-permute-start(f32[32,2048]{1,0:T(8,128)S(1)} %copy-done.8), channel_id=1, source_target_pairs={{0,16},{16,0},{1,17},{17,1},{2,18},{18,2},{3,19},{19,3},{4,20},{20... | collective-permute-start | bytes 786440 | tf_op jit(solution)/shard_map/ppermute | solution.py:30
  209.3 36.5 %collective-permute-start.16 = (f32[32,2048]{1,0:T(8,128)S(1)}, f32[32,2048]{1,0:T(8,128)S(1)}, u32[]{:S(2)}, u32[]{:S(2)}) collective-permute-start(f32[32,2048]{1,0:T(8,128)S(1)} %copy-done.7), channel_id=1, source_target_pairs={{0,16},{16,0},{1,17},{17,1},{2,18},{18,2},{3,19},{19,3},{4,20},{20... | collective-permute-start | bytes 786440 | tf_op jit(solution)/shard_map/ppermute | solution.py:30
  220.5 29.8 %collective-permute-start.22 = (f32[8,4096]{1,0:T(8,128)S(1)}, f32[8,4096]{1,0:T(8,128)S(1)}, u32[]{:S(2)}, u32[]{:S(2)}) collective-permute-start(f32[8,4096]{1,0:T(8,128)S(1)} %add_multiply_fusion), channel_id=1, source_target_pairs={{0,8},{2,10},{4,12},{6,14},{8,0},{10,2},{12,4},{14,6},{1,9},{3,11}... | collective-permute-start | bytes 393224 | tf_op jit(solution)/shard_map/ppermute | solution.py:35
  220.6 30.7 %collective-permute-start.17 = (f32[32,2048]{1,0:T(8,128)S(1)}, f32[32,2048]{1,0:T(8,128)S(1)}, u32[]{:S(2)}, u32[]{:S(2)}) collective-permute-start(f32[32,2048]{1,0:T(8,128)S(1)} %copy-done.6), channel_id=1, source_target_pairs={{0,16},{16,0},{1,17},{17,1},{2,18},{18,2},{3,19},{19,3},{4,20},{20... | collective-permute-start | bytes 786440 | tf_op jit(solution)/shard_map/ppermute | solution.py:30
  259.8 41.4 %collective-permute-start.23 = (f32[32,2048]{1,0:T(8,128)S(1)}, f32[32,2048]{1,0:T(8,128)S(1)}, u32[]{:S(2)}, u32[]{:S(2)}) collective-permute-start(f32[32,2048]{1,0:T(8,128)S(1)} %get-tuple-element.75), channel_id=1, source_target_pairs={{0,16},{16,0},{1,17},{17,1},{2,18},{18,2},{3,19},{19,3},{4,20},{20... | collective-permute-start | bytes 786440 | tf_op jit(solution)/shard_map/ppermute | solution.py:30
  263.2 34.5 %collective-permute-start.21 = (f32[32,2048]{1,0:T(8,128)S(1)}, f32[32,2048]{1,0:T(8,128)S(1)}, u32[]{:S(2)}, u32[]{:S(2)}) collective-permute-start(f32[32,2048]{1,0:T(8,128)S(1)} %get-tuple-element.73), channel_id=1, source_target_pairs={{0,16},{16,0},{1,17},{17,1},{2,18},{18,2},{3,19},{19,3},{4,20},{20... | collective-permute-start | bytes 786440 | tf_op jit(solution)/shard_map/ppermute | solution.py:30
  268.3 37.9 %collective-permute-start.24 = (f32[32,2048]{1,0:T(8,128)S(1)}, f32[32,2048]{1,0:T(8,128)S(1)}, u32[]{:S(2)}, u32[]{:S(2)}) collective-permute-start(f32[32,2048]{1,0:T(8,128)S(1)} %get-tuple-element.76), channel_id=1, source_target_pairs={{0,16},{16,0},{1,17},{17,1},{2,18},{18,2},{3,19},{19,3},{4,20},{20... | collective-permute-start | bytes 786440 | tf_op jit(solution)/shard_map/ppermute | solution.py:30
  301.2 37.8 %collective-permute-start.32 = (f32[32,4096]{1,0:T(8,128)S(1)}, f32[32,4096]{1,0:T(8,128)S(1)}, u32[]{:S(2)}, u32[]{:S(2)}) collective-permute-start(f32[32,4096]{1,0:T(8,128)S(1)} %pad_maximum_fusion), channel_id=1, source_target_pairs={{0,2},{2,0},{4,6},{6,4},{8,10},{10,8},{12,14},{14,12},{1,3},{3,1},... | collective-permute-start | bytes 1572872 | tf_op jit(solution)/shard_map/ppermute | solution.py:35
  323.0 30.6 %collective-permute-start.31 = (f32[32,2048]{1,0:T(8,128)}, f32[32,2048]{1,0:T(8,128)S(1)}, u32[]{:S(2)}, u32[]{:S(2)}) collective-permute-start(f32[32,2048]{1,0:T(8,128)} %get-tuple-element.83), channel_id=1, source_target_pairs={{0,16},{16,0},{1,17},{17,1},{2,18},{18,2},{3,19},{19,3},{4,20},{20... | collective-permute-start | bytes 786440 | tf_op jit(solution)/shard_map/ppermute | solution.py:30
  (42 other events, 1590.6 us)

commit v6 on v4

--- a/solution.py
+++ b/solution.py
@@ -1,17 +1,20 @@
+import functools
+
 import jax
 import jax.numpy as jnp
 from jax import lax
+from jax.experimental import pallas as pl
+from jax.experimental.pallas import tpu as pltpu
 from jax.sharding import PartitionSpec as P
 
 outer_rate = 0.7
 momentum = 0.9
 rate = outer_rate * (1 + momentum)
 decay = outer_rate * momentum * momentum
-first_sizes = (1, 3, 4) + (2,) * 12
-last_sizes = (2,) * 14 + (3, 1)
+first_sizes = (1, 3, 6, 6)
+last_sizes = (4, 4, 2, 2, 2, 1, 1)
 window = 3
-chain_start = 2
-chain_end = 23
+gate_before = 8
 
 
 def advance(anchor, moment, delta):
@@ -47,16 +50,42 @@
         start += size
 
 
-def factor_chain(value, bits):
+def add_kernel(start, half, part, _, total, rows, sem):
+    other = (1 - lax.axis_index("group")) * half
+    span = total.at[pl.ds(pl.multiple_of(other + start, 8), part.shape[0])]
+    read = pltpu.make_async_copy(span, rows, sem)
+    read.start()
+    read.wait()
+    rows[...] += part[...]
+    write = pltpu.make_async_copy(rows, span, sem)
+    write.start()
+    write.wait()
+
+
+def add_rows(total, part, start, half):
+    return pl.pallas_call(
+        functools.partial(add_kernel, start, half),
+        out_shape=jax.ShapeDtypeStruct(total.shape, total.dtype),
+        in_specs=[
+            pl.BlockSpec(memory_space=pltpu.VMEM),
+            pl.BlockSpec(memory_space=pltpu.HBM),
+        ],
+        out_specs=pl.BlockSpec(memory_space=pltpu.HBM),
+        scratch_shapes=[pltpu.VMEM(part.shape, part.dtype), pltpu.SemaphoreType.DMA],
+        input_output_aliases={1: 0},
+        cost_estimate=pl.CostEstimate(
+            flops=part.size, bytes_accessed=12 * part.size, transcendentals=0
+        ),
+    )(part, total)
+
+
+def sum_factors(value, bits):
     for bit in bits:
         rest = value.shape[0] // 2
-        received = yield value[rest:], across(value[rest:], bit)
-        value = value[:rest] + received
-    received = yield value, swap(value)
-    value = (value + received) / lax.axis_size("group")
+        value = value[:rest] + across(value[rest:], bit)
+    value = (value + swap(value)) / lax.axis_size("group")
     for bit in reversed(bits):
-        received = yield value, across(value, bit)
-        value = lax.concatenate([value, received], 0)
+        value = lax.concatenate([value, across(value, bit)], 0)
     return value
 
 
@@ -105,7 +134,6 @@
 
     spans = list(pieces(half, first_sizes))
     mixed_spans = list(pieces(half, last_sizes))
-    mixed = (rate / 2) * rows_of(local, own, half) - decay * down_moment
 
     shards = lax.axis_size("shard")
     bits = [1 << n for n in range(shards.bit_length() - 1)]
@@ -121,13 +149,12 @@
     partial_factors = lax.dot_general(
         basis, gate_diff, (((1,), (1,)), ((), ())), precision=lax.Precision.HIGHEST
     )
-    chain = factor_chain(partial_factors, bits)
-
-    stride = (chain_end - chain_start) // (2 * len(bits) + 1)
+    factors = sum_factors(partial_factors, bits)
+    gate = advance(gate_anchor, gate_moment, rebuild(factors, basis))
+    new_gate_anchor, new_gate_moment = gate
+
     parts = []
     cut = local
-    step_at = chain_start
-    step_sent = step_received = gate = None
     for i, (start, size) in enumerate(spans + mixed_spans):
         if i < len(spans):
             part = rows_of(cut, other + start, size)
@@ -136,31 +163,20 @@
         else:
             part = mixed[start : start + size]
         ties = [parts[i - window]] if i >= window else []
-        if step_sent is not None:
-            ties.append(step_sent)
-            step_sent = None
-        if gate is not None and i == step_at + window:
+        if i == gate_before:
             ties += gate
         parts.append(swap(after(part, *ties)))
         if i == 0:
+            mixed = (rate / 2) * rows_of(local, own, half) - decay * after(down_moment, parts[0])
+            anchor_next = (1 - rate) * after(down_anchor, parts[0]) + (rate / 2) * local
             norm_sent = after(norm_message(norm_local[0], norm_moment), parts[0])
             norm_received = swap(norm_sent)
-        if gate is None and i == step_at:
-            if step_received is not None:
-                step_received = after(step_received, parts[i - stride])
-            try:
-                step_sent, step_received = chain.send(step_received)
-                step_at += stride
-            except StopIteration as end:
-                gate = advance(gate_anchor, gate_moment, rebuild(end.value, basis))
-    new_gate_anchor, new_gate_moment = gate
     received, mixed_received = parts[: len(spans)], parts[len(spans) :]
-    norm_received = after(norm_received, parts[chain_end])
+    norm_received = after(norm_received, parts[1])
     new_norm_anchor, new_norm_moment = norm_finish(
         norm_anchor, norm_local[0], norm_moment, norm_received
     )
 
-    anchor_next = (1 - rate) * down_anchor + (rate / 2) * local
     moment_next = []
     for (start, size), part in zip(spans, received):
         old = down_moment[start : start + size]
@@ -172,8 +188,7 @@
         value = rows_of(anchor_next, own + start, size) + ((rate / 2) * part - decay * old)
         anchor_next = lax.dynamic_update_slice_in_dim(anchor_next, value, own + start, 0)
     for (start, size), part in zip(mixed_spans, mixed_received):
-        value = rows_of(anchor_next, other + start, size) + part
-        anchor_next = lax.dynamic_update_slice_in_dim(anchor_next, value, other + start, 0)
+        anchor_next = add_rows(anchor_next, part, start, half)
     return (
         anchor_next,
         lax.concatenate(moment_next, 0),

time: 384 us -> 377 us (0.982)
  waiting for transfers between devices: 174 us -> 234 us
  starting transfers between devices: 90.3 us -> 34.2 us
  other arithmetic: 75.3 us -> 37.2 us
  Pallas kernels: 0 us -> 21.1 us
  local copies, waits for them, and re-layouts: 15.8 us -> 20.5 us
    ppermute x33 -> x13, starting transfers between devices: 85.8 us -> 28.9 us  [swap(): return lax.ppermute(array, 'group', [(0, 1), (1, 0)])]
    ppermute x33 -> x13, waiting for transfers between devices: 174 us -> 221 us  [swap(): return lax.ppermute(array, 'group', [(0, 1), (1, 0)])]
    unnamed x16 -> x1, other arithmetic: 28.2 us -> 0.01 us
    dynamic_update_slice x16 -> x1, other arithmetic: 27.3 us -> 2.98 us  [body(): lax.dynamic_update_slice_in_dim(anchor_next, value, own + start, 0)]
    pallas_call x0 -> x7, Pallas kernels: none -> 21.1 us  [add_rows(): pl.pallas_call(functools.partial(add_kernel, start, half), out_shape=jax....]
    ppermute x6, waiting for transfers between devices: 0.02 us -> 12.8 us  [across(): return lax.ppermute(array, 'shard', [(i, i ^ k) for i in range(shards)])]
    sub x1 -> x4, other arithmetic: 4.41 us -> 15.9 us  [the longest x3 12.8 us: body(): momentum * old + rows_of(down_anchor, own + start, size)]
    unnamed x55 -> x35, local copies, waits for them, and re-layouts: 5.12 us -> 8.42 us
  transfers between devices with their start and end apart: 39 -> 19, of which waited for: 22 -> 10; matrix products, arithmetic and copies ran while one was open for 29% -> 21% of each run, Pallas kernels for 0% -> 5%
where the time goes in v6:
time: 377 us; the launch traced here: 374 us
  waiting for transfers between devices  234 us (62%)
  other arithmetic  37.2 us (10%)
  starting transfers between devices  34.2 us (9%)
  matrix products  26.1 us (7%)
  Pallas kernels  21.1 us (6%)
  local copies, waits for them, and re-layouts  20.5 us (5%)
    ppermute x13, waiting for transfers between devices, swap(): return lax.ppermute(array, 'group', [(0, 1), (1, 0)])  221 us
    ppermute x13, starting transfers between devices, swap(): return lax.ppermute(array, 'group', [(0, 1), (1, 0)])  28.9 us
    pallas_call x7, Pallas kernels, add_rows(): pl.pallas_call(functools.partial(add_kernel, start, half), out_shape=jax....  21.1 us
    dot_general x1, matrix products, rebuild(): lax.dot_general(factors, factor_basis, (((0,), (0,)), ((), ())), precisio...  14.6 us
    ppermute x6, waiting for transfers between devices, across(): return lax.ppermute(array, 'shard', [(i, i ^ k) for i in range(shards)])  12.8 us
    sub x3, other arithmetic, body(): momentum * old + rows_of(down_anchor, own + start, size)  12.8 us
    add x1, other arithmetic, body(): anchor_next = (1 - rate) * after(down_anchor, parts[0]) + rate / 2 * local  12.1 us
    dot_general x1, matrix products, body(): lax.dot_general(basis, gate_diff, (((1,), (1,)), ((), ())), precision=lax...  11.6 us
  transfers between devices with their start and end apart: 19, of which 10 were waited for; matrix products, arithmetic and copies ran while one was open for 21% of the time, Pallas kernels for 5%

profile of v6, /device:TPU:10, one launch (start us, length us, event | category | flops | bytes accessed | tf_op | source)
XLA Modules:
  0.0 374.4 jit_solution(8309238194014434273)
XLA Ops:
  12.2 11.6 %fusion = f32[64,4096]{1,0:T(8,128)S(1)} fusion(f32[64,512]{1,0:T(8,128)S(1)} %constant_dynamic-update-slice_fusion, f32[4096,512]{1,0:T(8,128)} %param.16, f32[1,4096,512]{2,1,0:T(8,128)} %param.17), kind=kOutput, calls=%fused_computation.1 | convolution fusion | flops 1612709888 | bytes 17956864 | tf_op jit(solution)/shard_map/dot_general | solution.py:149
  33.6 68.5 %collective-permute-done = f32[32,2048]{1,0:T(8,128)} collective-permute-done((f32[32,2048]{1,0:T(8,128)}, f32[32,2048]{1,0:T(8,128)}, u32[]{:S(2)}, u32[]{:S(2)}) %collective-permute-start) | collective-permute-done | bytes 262176 | tf_op jit(solution)/shard_map/ppermute | solution.py:33
  102.1 3.4 collective-permute-start.5
  105.5 12.1 %multiply_add_fusion = f32[1024,2048]{1,0:T(8,128)} fusion(f32[1024,2048]{1,0:T(8,128)} %param.10, f32[1,1024,2048]{2,1,0:T(8,128)} %param.11), kind=kLoop, calls=%fused_computation.2 | loop fusion | flops 6291456 | bytes 25165824 | tf_op jit(solution)/shard_map/add | solution.py:171
  117.6 3.1 bitcast_subtract_fusion.2
  126.3 4.9 %collective-permute-done.11 = f32[16,4096]{1,0:T(8,128)S(1)} collective-permute-done((f32[16,4096]{1,0:T(8,128)S(1)}, f32[16,4096]{1,0:T(8,128)S(1)}, u32[]{:S(2)}, u32[]{:S(2)}) %collective-permute-start.11) | collective-permute-done | bytes 262176 | tf_op jit(solution)/shard_map/ppermute | solution.py:38
  138.9 48.8 %collective-permute-done.18 = f32[2,256]{1,0:T(2,128)S(1)} collective-permute-done((f32[2,256]{1,0:T(2,128)S(1)}, f32[2,256]{1,0:T(2,128)S(1)}, u32[]{:S(2)}, u32[]{:S(2)}) %collective-permute-start.18) | collective-permute-done | bytes 2080 | tf_op jit(solution)/shard_map/ppermute | solution.py:33
  187.8 3.4 collective-permute-start.2
  191.1 77.9 %collective-permute-done.13 = f32[8,4096]{1,0:T(8,128)S(1)} collective-permute-done((f32[8,4096]{1,0:T(8,128)S(1)}, f32[8,4096]{1,0:T(8,128)S(1)}, u32[]{:S(2)}, u32[]{:S(2)}) %collective-permute-start.13) | collective-permute-done | bytes 131104 | tf_op jit(solution)/shard_map/ppermute | solution.py:33
  270.7 3.1 fusion.14
  275.6 5.0 %collective-permute-done.15 = f32[16,4096]{1,0:T(8,128)S(1)} collective-permute-done((f32[16,4096]{1,0:T(8,128)S(1)}, f32[16,4096]{1,0:T(8,128)S(1)}, u32[]{:S(2)}, u32[]{:S(2)}) %collective-permute-start.15) | collective-permute-done | bytes 262176 | tf_op jit(solution)/shard_map/ppermute | solution.py:38
  280.8 4.8 %collective-permute-start.9 = (f32[128,2048]{1,0:T(8,128)S(1)}, f32[128,2048]{1,0:T(8,128)S(1)}, u32[]{:S(2)}, u32[]{:S(2)}) collective-permute-start(f32[128,2048]{1,0:T(8,128)S(1)} %get-tuple-element.31), channel_id=1, source_target_pairs={{0,16},{16,0},{1,17},{17,1},{2,18},{18,2},{3,19},{19,3},{4,20},{20... | collective-permute-start | bytes 3145736 | tf_op jit(solution)/shard_map/ppermute | solution.py:33
  285.5 3.0 add_dynamic-update-slice_fusion.1
  289.0 13.9 %collective-permute-done.2.part = f32[128,2048]{1,0:T(8,128)S(1)} collective-permute-done((f32[128,2048]{1,0:T(8,128)S(1)}, f32[128,2048]{1,0:T(8,128)S(1)}, u32[]{:S(2)}, u32[]{:S(2)}) %collective-permute-start.2) | collective-permute-done | bytes 1048608 | tf_op jit(solution)/shard_map/ppermute | solution.py:33
  302.9 3.4 collective-permute-start.3
  306.3 14.6 %multiply_subtract_fusion = (f32[4096,512]{1,0:T(8,128)}, f32[4096,512]{1,0:T(8,128)}) fusion(f32[4096,512]{1,0:T(8,128)S(1)} %bitcast.42, f32[4096,512]{1,0:T(8,128)} %param.18, f32[64,512]{1,0:T(8,128)S(1)} %constant_dynamic-update-slice_fusion, f32[32,4096]{1,0:T(8,128)S(1)} %collective-permute-done.16, f32[16,4096]{1,0:T(8,128)S(1)} %collective-permute-done.15, ...), kind=kOutput, calls=%fused_computation.3 | convolution fusion | flops 1623982080 | bytes 34734080 | tf_op jit(solution)/shard_map/dot_general | solution.py:27
  320.8 4.5 %collective-permute-done.9.part = f32[128,2048]{1,0:T(8,128)S(1)} collective-permute-done((f32[128,2048]{1,0:T(8,128)S(1)}, f32[128,2048]{1,0:T(8,128)S(1)}, u32[]{:S(2)}, u32[]{:S(2)}) %collective-permute-start.9) | collective-permute-done | bytes 1048608 | tf_op jit(solution)/shard_map/ppermute | solution.py:33
  325.3 3.4 collective-permute-start.17
  328.7 7.5 %fusion.4 = (f32[192,2048]{1,0:T(8,128)S(1)}, f32[192,2048]{1,0:T(8,128)}, f32[1024,2048]{1,0:T(8,128)}) fusion(f32[192,2048]{1,0:T(8,128)} %copy-done.1, f32[1,1024,2048]{2,1,0:T(8,128)} %param.11, s32[]{:T(128)S(6)} %select_n.89, f32[1024,2048]{1,0:T(8,128)} %param.10, f32[512,2048]{1,0:T(8,128)S(1)} %copy-done, f32[192,2048]{1,0:T(8,128)} %collective-permute-done.5, ...), kind=kLoop, calls=%fused_computation.12 | loop fusion | flops 5505024 | bytes 18874376 | tf_op jit(solution)/shard_map/sub | solution.py:184
  336.2 3.5 shard_map.145._
  340.2 7.7 %collective-permute-done.3.part = f32[64,2048]{1,0:T(8,128)} collective-permute-done((f32[64,2048]{1,0:T(8,128)}, f32[64,2048]{1,0:T(8,128)}, u32[]{:S(2)}, u32[]{:S(2)}) %collective-permute-start.3) | collective-permute-done | bytes 524320 | tf_op jit(solution)/shard_map/ppermute | solution.py:33
  347.9 3.5 shard_map.146._
  351.5 3.4 collective-permute-start.4
  357.9 3.8 %pad_maximum_fusion = f32[512,2048]{1,0:T(8,128)} fusion(f32[192,2048]{1,0:T(8,128)} %get-tuple-element.39, f32[192,2048]{1,0:T(8,128)S(1)} %get-tuple-element.38, f32[96,2048]{1,0:T(8,128)S(1)} %get-tuple-element.41, f32[32,2048]{1,0:T(8,128)S(1)} %copy-done.6), kind=kLoop, calls=%fused_computation.5 | loop fusion | flops 3145728 | bytes 8388608 | tf_op jit(solution)/shard_map/concatenate | solution.py:194
  (86 shorter events, 54.6 us)
Async XLA Ops:
  2.3 99.8 %collective-permute-start = (f32[32,2048]{1,0:T(8,128)}, f32[32,2048]{1,0:T(8,128)}, u32[]{:S(2)}, u32[]{:S(2)}) collective-permute-start(f32[32,2048]{1,0:T(8,128)} %dynamic-slice_bitcast_fusion), channel_id=1, source_target_pairs={{0,16},{16,0},{1,17},{17,1},{2,18},{18,2},{3,19},{19,3},{4,20},{20... | collective-permute-start | bytes 786440 | tf_op jit(solution)/shard_map/ppermute | solution.py:33
  6.1 181.7 %collective-permute-start.1 = (f32[96,2048]{1,0:T(8,128)S(1)}, f32[96,2048]{1,0:T(8,128)}, u32[]{:S(2)}, u32[]{:S(2)}) collective-permute-start(f32[96,2048]{1,0:T(8,128)S(1)} %constant_dynamic-slice_fusion.5), channel_id=1, source_target_pairs={{0,16},{16,0},{1,17},{17,1},{2,18},{18,2},{3,19},{19,3},{4,20},{20... | collective-permute-start | bytes 2359304 | tf_op jit(solution)/shard_map/ppermute | solution.py:33
  25.6 95.4 %collective-permute-start.10 = (f32[32,4096]{1,0:T(8,128)}, f32[32,4096]{1,0:T(8,128)}, u32[]{:S(2)}, u32[]{:S(2)}) collective-permute-start(f32[32,4096]{1,0:T(8,128)} %slice.76), channel_id=1, source_target_pairs={{0,2},{2,0},{4,6},{6,4},{8,10},{10,8},{12,14},{14,12},{1,3},{3,1},... | collective-permute-start | bytes 1572872 | tf_op jit(solution)/shard_map/ppermute | solution.py:38
  28.3 252.4 %collective-permute-start.8 = (f32[192,2048]{1,0:T(8,128)}, f32[192,2048]{1,0:T(8,128)S(1)}, u32[]{:S(2)}, u32[]{:S(2)}) collective-permute-start(f32[192,2048]{1,0:T(8,128)} %constant_dynamic-slice_fusion.4), channel_id=1, source_target_pairs={{0,16},{16,0},{1,17},{17,1},{2,18},{18,2},{3,19},{19,3},{4,20},{20... | collective-permute-start | bytes 4718600 | tf_op jit(solution)/shard_map/ppermute | solution.py:33
  33.6 84.0 %copy-start = (f32[512,2048]{1,0:T(8,128)S(1)}, f32[512,2048]{1,0:T(8,128)}, u32[]{:S(2)}) copy-start(f32[512,2048]{1,0:T(8,128)} %param.12) | copy-start | bytes 12582916
  102.1 186.4 %collective-permute-start.5 = (f32[192,2048]{1,0:T(8,128)}, f32[192,2048]{1,0:T(8,128)}, u32[]{:S(2)}, u32[]{:S(2)}) collective-permute-start(f32[192,2048]{1,0:T(8,128)} %constant_dynamic-slice_fusion.3), channel_id=1, source_target_pairs={{0,16},{16,0},{1,17},{17,1},{2,18},{18,2},{3,19},{19,3},{4,20},{20... | collective-permute-start | bytes 4718600 | tf_op jit(solution)/shard_map/ppermute | solution.py:33
  123.1 8.1 %collective-permute-start.11 = (f32[16,4096]{1,0:T(8,128)S(1)}, f32[16,4096]{1,0:T(8,128)S(1)}, u32[]{:S(2)}, u32[]{:S(2)}) collective-permute-start(f32[16,4096]{1,0:T(8,128)S(1)} %slice.78), channel_id=1, source_target_pairs={{0,4},{2,6},{4,0},{6,2},{8,12},{10,14},{12,8},{14,10},{1,5},{3,7},... | collective-permute-start | bytes 786440 | tf_op jit(solution)/shard_map/ppermute | solution.py:38
  131.3 5.0 %collective-permute-start.12 = (f32[8,4096]{1,0:T(8,128)S(1)}, f32[8,4096]{1,0:T(8,128)S(1)}, u32[]{:S(2)}, u32[]{:S(2)}) collective-permute-start(f32[8,4096]{1,0:T(8,128)S(1)} %slice.80), channel_id=1, source_target_pairs={{0,8},{2,10},{4,12},{6,14},{8,0},{10,2},{12,4},{14,6},{1,9},{3,11}... | collective-permute-start | bytes 393224 | tf_op jit(solution)/shard_map/ppermute | solution.py:38
  133.5 54.2 %collective-permute-start.18 = (f32[2,256]{1,0:T(2,128)S(1)}, f32[2,256]{1,0:T(2,128)S(1)}, u32[]{:S(2)}, u32[]{:S(2)}) collective-permute-start(f32[2,256]{1,0:T(2,128)S(1)} %subtract_select_fusion), channel_id=1, source_target_pairs={{0,16},{16,0},{1,17},{17,1},{2,18},{18,2},{3,19},{19,3},{4,20},{20... | collective-permute-start | bytes 6152 | tf_op jit(solution)/shard_map/ppermute | solution.py:33
  136.3 138.1 %copy-start.11 = (f32[2,256]{1,0:T(2,128)S(1)}, f32[2,256]{1,0:T(2,128)}, u32[]{:S(2)}) copy-start(f32[2,256]{1,0:T(2,128)} %param.13) | copy-start | bytes 6148
  136.3 132.7 %collective-permute-start.13 = (f32[8,4096]{1,0:T(8,128)S(1)}, f32[8,4096]{1,0:T(8,128)S(1)}, u32[]{:S(2)}, u32[]{:S(2)}) collective-permute-start(f32[8,4096]{1,0:T(8,128)S(1)} %slice_add_fusion.2), channel_id=1, source_target_pairs={{0,16},{16,0},{1,17},{17,1},{2,18},{18,2},{3,19},{19,3},{4,20},{20... | collective-permute-start | bytes 393224 | tf_op jit(solution)/shard_map/ppermute | solution.py:33
  136.7 169.6 %slice-start = ((s8[8388608]{0:T(1024)(128)(4,1)}), s8[4194304]{0:T(1024)(128)(4,1)S(1)}, s32[]{:S(2)}) async-start(s8[8388608]{0:T(1024)(128)(4,1)} %bitcast.41), calls=%async_computation | async-start | bytes 8388608
  187.8 115.1 %collective-permute-start.2 = (f32[128,2048]{1,0:T(8,128)S(1)}, f32[128,2048]{1,0:T(8,128)S(1)}, u32[]{:S(2)}, u32[]{:S(2)}) collective-permute-start(f32[128,2048]{1,0:T(8,128)S(1)} %get-tuple-element.23), channel_id=1, source_target_pairs={{0,16},{16,0},{1,17},{17,1},{2,18},{18,2},{3,19},{19,3},{4,20},{20... | collective-permute-start | bytes 3145736 | tf_op jit(solution)/shard_map/ppermute | solution.py:33
  269.1 5.0 %collective-permute-start.14 = (f32[8,4096]{1,0:T(8,128)S(1)}, f32[8,4096]{1,0:T(8,128)S(1)}, u32[]{:S(2)}, u32[]{:S(2)}) collective-permute-start(f32[8,4096]{1,0:T(8,128)S(1)} %add_multiply_fusion), channel_id=1, source_target_pairs={{0,8},{2,10},{4,12},{6,14},{8,0},{10,2},{12,4},{14,6},{1,9},{3,11}... | collective-permute-start | bytes 393224 | tf_op jit(solution)/shard_map/ppermute | solution.py:38
  273.8 32.5 %slice-start.1 = ((s8[8388608]{0:T(1024)(128)(4,1)}), s8[4194304]{0:T(1024)(128)(4,1)S(1)}, s32[]{:S(2)}) async-start(s8[8388608]{0:T(1024)(128)(4,1)} %bitcast.41), calls=%async_computation.1 | async-start | bytes 8388608
  274.2 6.4 %collective-permute-start.15 = (f32[16,4096]{1,0:T(8,128)S(1)}, f32[16,4096]{1,0:T(8,128)S(1)}, u32[]{:S(2)}, u32[]{:S(2)}) collective-permute-start(f32[16,4096]{1,0:T(8,128)S(1)} %pad_maximum_fusion.2), channel_id=1, source_target_pairs={{0,4},{2,6},{4,0},{6,2},{8,12},{10,14},{12,8},{14,10},{1,5},{3,7},... | collective-permute-start | bytes 786440 | tf_op jit(solution)/shard_map/ppermute | solution.py:38
  280.6 25.6 %collective-permute-start.16 = (f32[32,4096]{1,0:T(8,128)S(1)}, f32[32,4096]{1,0:T(8,128)S(1)}, u32[]{:S(2)}, u32[]{:S(2)}) collective-permute-start(f32[32,4096]{1,0:T(8,128)S(1)} %pad_maximum_fusion.1), channel_id=1, source_target_pairs={{0,2},{2,0},{4,6},{6,4},{8,10},{10,8},{12,14},{14,12},{1,3},{3,1},... | collective-permute-start | bytes 1572872 | tf_op jit(solution)/shard_map/ppermute | solution.py:38
  280.7 40.1 %copy-start.1 = (f32[192,2048]{1,0:T(8,128)}, f32[192,2048]{1,0:T(8,128)S(1)}, u32[]{:S(2)}) copy-start(f32[192,2048]{1,0:T(8,128)S(1)} %collective-permute-done.8) | copy-start | bytes 4718596
  280.8 44.6 %collective-permute-start.9 = (f32[128,2048]{1,0:T(8,128)S(1)}, f32[128,2048]{1,0:T(8,128)S(1)}, u32[]{:S(2)}, u32[]{:S(2)}) collective-permute-start(f32[128,2048]{1,0:T(8,128)S(1)} %get-tuple-element.31), channel_id=1, source_target_pairs={{0,16},{16,0},{1,17},{17,1},{2,18},{18,2},{3,19},{19,3},{4,20},{20... | collective-permute-start | bytes 3145736 | tf_op jit(solution)/shard_map/ppermute | solution.py:33
  288.5 51.2 %collective-permute-start.6 = (f32[64,2048]{1,0:T(8,128)}, f32[64,2048]{1,0:T(8,128)}, u32[]{:S(2)}, u32[]{:S(2)}) collective-permute-start(f32[64,2048]{1,0:T(8,128)} %get-tuple-element.29), channel_id=1, source_target_pairs={{0,16},{16,0},{1,17},{17,1},{2,18},{18,2},{3,19},{19,3},{4,20},{20... | collective-permute-start | bytes 1572872 | tf_op jit(solution)/shard_map/ppermute | solution.py:33
  302.9 45.0 %collective-permute-start.3 = (f32[64,2048]{1,0:T(8,128)}, f32[64,2048]{1,0:T(8,128)}, u32[]{:S(2)}, u32[]{:S(2)}) collective-permute-start(f32[64,2048]{1,0:T(8,128)} %get-tuple-element.24), channel_id=1, source_target_pairs={{0,16},{16,0},{1,17},{17,1},{2,18},{18,2},{3,19},{19,3},{4,20},{20... | collective-permute-start | bytes 1572872 | tf_op jit(solution)/shard_map/ppermute | solution.py:33
  325.3 39.2 %collective-permute-start.17 = (f32[64,2048]{1,0:T(8,128)}, f32[64,2048]{1,0:T(8,128)}, u32[]{:S(2)}, u32[]{:S(2)}) collective-permute-start(f32[64,2048]{1,0:T(8,128)} %get-tuple-element.32), channel_id=1, source_target_pairs={{0,16},{16,0},{1,17},{17,1},{2,18},{18,2},{3,19},{19,3},{4,20},{20... | collective-permute-start | bytes 1572872 | tf_op jit(solution)/shard_map/ppermute | solution.py:33
  339.7 27.8 %collective-permute-start.7 = (f32[32,2048]{1,0:T(8,128)}, f32[32,2048]{1,0:T(8,128)S(1)}, u32[]{:S(2)}, u32[]{:S(2)}) collective-permute-start(f32[32,2048]{1,0:T(8,128)} %get-tuple-element.30), channel_id=1, source_target_pairs={{0,16},{16,0},{1,17},{17,1},{2,18},{18,2},{3,19},{19,3},{4,20},{20... | collective-permute-start | bytes 786440 | tf_op jit(solution)/shard_map/ppermute | solution.py:33
  351.5 19.4 %collective-permute-start.4 = (f32[32,2048]{1,0:T(8,128)}, f32[32,2048]{1,0:T(8,128)S(1)}, u32[]{:S(2)}, u32[]{:S(2)}) collective-permute-start(f32[32,2048]{1,0:T(8,128)} %get-tuple-element.25), channel_id=1, source_target_pairs={{0,16},{16,0},{1,17},{17,1},{2,18},{18,2},{3,19},{19,3},{4,20},{20... | collective-permute-start | bytes 786440 | tf_op jit(solution)/shard_map/ppermute | solution.py:33
  (9 other events, 51.1 us)

commit v7 on v6

--- a/solution.py
+++ b/solution.py
@@ -11,10 +11,11 @@
 momentum = 0.9
 rate = outer_rate * (1 + momentum)
 decay = outer_rate * momentum * momentum
-first_sizes = (1, 3, 6, 6)
-last_sizes = (4, 4, 2, 2, 2, 1, 1)
+first_sizes = (1, 7, 12, 12)
+last_sizes = (8, 8, 4, 4, 4, 2, 2)
 window = 3
-gate_before = 8
+gate_before = 6
+pinned = 4
 
 
 def advance(anchor, moment, delta):
@@ -79,11 +80,14 @@
     )(part, total)
 
 
-def sum_factors(value, bits):
+def scatter_factors(value, bits):
     for bit in bits:
         rest = value.shape[0] // 2
         value = value[:rest] + across(value[rest:], bit)
-    value = (value + swap(value)) / lax.axis_size("group")
+    return value
+
+
+def gather_factors(value, bits):
     for bit in reversed(bits):
         value = lax.concatenate([value, across(value, bit)], 0)
     return value
@@ -149,9 +153,8 @@
     partial_factors = lax.dot_general(
         basis, gate_diff, (((1,), (1,)), ((), ())), precision=lax.Precision.HIGHEST
     )
-    factors = sum_factors(partial_factors, bits)
-    gate = advance(gate_anchor, gate_moment, rebuild(factors, basis))
-    new_gate_anchor, new_gate_moment = gate
+    factor_piece = scatter_factors(partial_factors, bits)
+    factor_other = swap(factor_piece)
 
     parts = []
     cut = local
@@ -171,8 +174,13 @@
             anchor_next = (1 - rate) * after(down_anchor, parts[0]) + (rate / 2) * local
             norm_sent = after(norm_message(norm_local[0], norm_moment), parts[0])
             norm_received = swap(norm_sent)
+        if i == len(spans) - 1:
+            norm_received = after(norm_received, parts[i])
+            factor_piece = (factor_piece + after(factor_other, parts[i])) / groups
+            factors = gather_factors(factor_piece, bits)
+            gate = advance(gate_anchor, gate_moment, rebuild(factors, basis))
+            new_gate_anchor, new_gate_moment = gate
     received, mixed_received = parts[: len(spans)], parts[len(spans) :]
-    norm_received = after(norm_received, parts[1])
     new_norm_anchor, new_norm_moment = norm_finish(
         norm_anchor, norm_local[0], norm_moment, norm_received
     )
@@ -187,8 +195,12 @@
         )
         value = rows_of(anchor_next, own + start, size) + ((rate / 2) * part - decay * old)
         anchor_next = lax.dynamic_update_slice_in_dim(anchor_next, value, own + start, 0)
-    for (start, size), part in zip(mixed_spans, mixed_received):
-        anchor_next = add_rows(anchor_next, part, start, half)
+    for i, ((start, size), part) in enumerate(zip(mixed_spans, mixed_received)):
+        if i == pinned:
+            anchor_next = add_rows(anchor_next, part, start, half)
+        else:
+            value = rows_of(anchor_next, other + start, size) + part
+            anchor_next = lax.dynamic_update_slice_in_dim(anchor_next, value, other + start, 0)
     return (
         anchor_next,
         lax.concatenate(moment_next, 0),

time: 377 us -> 376 us (level)
  Pallas kernels: 21.1 us -> 2.93 us
  other arithmetic: 37.2 us -> 49.1 us
  waiting for transfers between devices: 234 us -> 242 us
    pallas_call x7 -> x1, Pallas kernels: 21.1 us -> 2.93 us  [add_rows(): pl.pallas_call(functools.partial(add_kernel, start, half), out_shape=jax....]
    dynamic_update_slice x0 -> x6, other arithmetic: none -> 12.4 us  [body(): lax.dynamic_update_slice_in_dim(anchor_next, value, other + start, 0)]
    ppermute x13, waiting for transfers between devices: 221 us -> 233 us  [swap(): return lax.ppermute(array, 'group', [(0, 1), (1, 0)])]
    ppermute x6, waiting for transfers between devices: 12.8 us -> 9.01 us  [across(): return lax.ppermute(array, 'shard', [(i, i ^ k) for i in range(shards)])]
    unnamed x35 -> x43, local copies, waits for them, and re-layouts: 8.42 us -> 7.11 us
  transfers between devices with their start and end apart: 19 -> 19, of which waited for: 10 -> 11; matrix products, arithmetic and copies ran while one was open for 21% -> 24% of each run, Pallas kernels for 5% -> 1%
where the time goes in v7:
time: 376 us; the launch traced here: 373 us
  waiting for transfers between devices  242 us (64%)
  other arithmetic  49.1 us (13%)
  starting transfers between devices  30.7 us (8%)
  matrix products  26.2 us (7%)
  local copies, waits for them, and re-layouts  20.7 us (6%)
    ppermute x13, waiting for transfers between devices, swap(): return lax.ppermute(array, 'group', [(0, 1), (1, 0)])  233 us
    ppermute x13, starting transfers between devices, swap(): return lax.ppermute(array, 'group', [(0, 1), (1, 0)])  26.3 us
    dot_general x1, matrix products, rebuild(): lax.dot_general(factors, factor_basis, (((0,), (0,)), ((), ())), precisio...  14.6 us
    dynamic_update_slice x6, other arithmetic, body(): lax.dynamic_update_slice_in_dim(anchor_next, value, other + start, 0)  12.4 us
    add x1, other arithmetic, body(): anchor_next = (1 - rate) * after(down_anchor, parts[0]) + rate / 2 * local  12.1 us
    sub x3, other arithmetic, body(): momentum * old + rows_of(down_anchor, own + start, size)  11.7 us
    dot_general x1, matrix products, body(): lax.dot_general(basis, gate_diff, (((1,), (1,)), ((), ())), precision=lax...  11.6 us
    ppermute x6, waiting for transfers between devices, across(): return lax.ppermute(array, 'shard', [(i, i ^ k) for i in range(shards)])  9.01 us
  transfers between devices with their start and end apart: 19, of which 11 were waited for; matrix products, arithmetic and copies ran while one was open for 24% of the time, Pallas kernels for 1%

profile of v7, /device:TPU:10, one launch (start us, length us, event | category | flops | bytes accessed | tf_op | source)
XLA Modules:
  0.0 372.7 jit_solution(12070665194867740636)
XLA Ops:
  1.6 2.7 collective-permute-start
  12.5 11.6 %fusion = f32[64,4096]{1,0:T(8,128)S(1)} fusion(f32[64,512]{1,0:T(8,128)S(1)} %constant_dynamic-update-slice_fusion, f32[4096,512]{1,0:T(8,128)} %param.16, f32[1,4096,512]{2,1,0:T(8,128)} %param.17), kind=kOutput, calls=%fused_computation.1 | convolution fusion | flops 1612709888 | bytes 17956864 | tf_op jit(solution)/shard_map/dot_general | solution.py:153
  26.0 2.7 constant_dynamic-slice_fusion.4
  31.2 2.7 constant_dynamic-slice_fusion.1
  37.0 4.4 %bitcast_subtract_fusion.2 = f32[512,2048]{1,0:T(8,128)S(1)} fusion(f32[512,2048]{1,0:T(8,128)} %param.12, f32[1,1024,2048]{2,1,0:T(8,128)} %param.11, s32[]{:T(128)S(6)} %select_n.93), kind=kLoop, calls=%fused_computation.6 | loop fusion | flops 3145728 | bytes 12582916 | tf_op jit(solution)/shard_map/sub | solution.py:173
  42.6 12.1 %multiply_add_fusion.1 = f32[1024,2048]{1,0:T(8,128)} fusion(f32[1024,2048]{1,0:T(8,128)} %param.10, f32[1,1024,2048]{2,1,0:T(8,128)} %param.11), kind=kLoop, calls=%fused_computation.4 | loop fusion | flops 6291456 | bytes 25165824 | tf_op jit(solution)/shard_map/add | solution.py:174
  59.5 6.5 %collective-permute-done.8 = f32[16,4096]{1,0:T(8,128)S(1)} collective-permute-done((f32[16,4096]{1,0:T(8,128)S(1)}, f32[16,4096]{1,0:T(8,128)S(1)}, u32[]{:S(2)}, u32[]{:S(2)}) %collective-permute-start.8) | collective-permute-done | bytes 262176 | tf_op jit(solution)/shard_map/ppermute | solution.py:39
  72.1 47.4 %collective-permute-done.4 = f32[112,2048]{1,0:T(8,128)S(1)} collective-permute-done((f32[112,2048]{1,0:T(8,128)}, f32[112,2048]{1,0:T(8,128)S(1)}, u32[]{:S(2)}, u32[]{:S(2)}) %collective-permute-start.4) | collective-permute-done | bytes 917536 | tf_op jit(solution)/shard_map/ppermute | solution.py:34
  119.5 3.3 collective-permute-start.6
  122.7 3.1 fusion.14
  125.8 49.8 %collective-permute-done.1 = f32[192,2048]{1,0:T(8,128)S(1)} collective-permute-done((f32[192,2048]{1,0:T(8,128)}, f32[192,2048]{1,0:T(8,128)S(1)}, u32[]{:S(2)}, u32[]{:S(2)}) %collective-permute-start.1) | collective-permute-done | bytes 1572896 | tf_op jit(solution)/shard_map/ppermute | solution.py:34
  175.6 3.3 collective-permute-start.2
  178.9 55.6 %collective-permute-done.10 = f32[8,4096]{1,0:T(8,128)S(1)} collective-permute-done((f32[8,4096]{1,0:T(8,128)S(1)}, f32[8,4096]{1,0:T(8,128)S(1)}, u32[]{:S(2)}, u32[]{:S(2)}) %collective-permute-start.10) | collective-permute-done | bytes 131104 | tf_op jit(solution)/shard_map/ppermute | solution.py:34
  236.2 3.0 add_dynamic-update-slice_fusion.1
  240.6 6.9 %fusion.4 = (f32[192,2048]{1,0:T(8,128)S(1)}, f32[192,2048]{1,0:T(8,128)S(1)}, f32[1024,2048]{1,0:T(8,128)}) fusion(f32[192,2048]{1,0:T(8,128)S(1)} %collective-permute-done.1, f32[1,1024,2048]{2,1,0:T(8,128)} %param.11, s32[]{:T(128)S(6)} %select_n.98, f32[1024,2048]{1,0:T(8,128)} %param.10, f32[512,2048]{1,0:T(8,128)S(1)} %copy-done, ...), kind=kLoop, calls=%fused_computation.12 | loop fusion | flops 5505024 | bytes 18874376 | tf_op jit(solution)/shard_map/sub | solution.py:192
  251.1 6.0 %collective-permute-done.6 = f32[128,2048]{1,0:T(8,128)} collective-permute-done((f32[128,2048]{1,0:T(8,128)}, f32[128,2048]{1,0:T(8,128)}, u32[]{:S(2)}, u32[]{:S(2)}) %collective-permute-start.6) | collective-permute-done | bytes 1048608 | tf_op jit(solution)/shard_map/ppermute | solution.py:34
  257.2 3.4 collective-permute-start.15
  260.6 14.6 %multiply_subtract_fusion = (f32[4096,512]{1,0:T(8,128)}, f32[4096,512]{1,0:T(8,128)}) fusion(f32[4096,512]{1,0:T(8,128)S(1)} %bitcast.42, f32[4096,512]{1,0:T(8,128)} %param.18, f32[64,512]{1,0:T(8,128)S(1)} %copy-done.3, f32[32,4096]{1,0:T(8,128)S(1)} %collective-permute-done.13, f32[16,4096]{1,0:T(8,128)S(1)} %collective-permute-done.12, ...), kind=kOutput, calls=%fused_computation.2 | convolution fusion | flops 1623982080 | bytes 34734080 | tf_op jit(solution)/shard_map/dot_general | solution.py:28
  278.0 35.2 %collective-permute-done.15 = f32[64,2048]{1,0:T(8,128)S(1)} collective-permute-done((f32[64,2048]{1,0:T(8,128)S(1)}, f32[64,2048]{1,0:T(8,128)S(1)}, u32[]{:S(2)}, u32[]{:S(2)}) %collective-permute-start.15) | collective-permute-done | bytes 524320 | tf_op jit(solution)/shard_map/ppermute | solution.py:34
  313.2 3.4 collective-permute-start.17
  319.3 22.0 %collective-permute-done.14 = f32[64,2048]{1,0:T(8,128)S(1)} collective-permute-done((f32[64,2048]{1,0:T(8,128)S(1)}, f32[64,2048]{1,0:T(8,128)S(1)}, u32[]{:S(2)}, u32[]{:S(2)}) %collective-permute-start.14) | collective-permute-done | bytes 524320 | tf_op jit(solution)/shard_map/ppermute | solution.py:34
  341.3 3.4 collective-permute-start.16
  348.5 15.3 %collective-permute-done.3.part = f32[64,2048]{1,0:T(8,128)S(1)} collective-permute-done((f32[64,2048]{1,0:T(8,128)S(1)}, f32[64,2048]{1,0:T(8,128)S(1)}, u32[]{:S(2)}, u32[]{:S(2)}) %collective-permute-start.3) | collective-permute-done | bytes 524320 | tf_op jit(solution)/shard_map/ppermute | solution.py:34
  364.6 2.9 shard_map.145
  (94 shorter events, 50.6 us)
Async XLA Ops:
  1.6 32.4 %collective-permute-start = (f32[16,2048]{1,0:T(8,128)S(1)}, f32[16,2048]{1,0:T(8,128)S(1)}, u32[]{:S(2)}, u32[]{:S(2)}) collective-permute-start(f32[16,2048]{1,0:T(8,128)S(1)} %dynamic-slice_bitcast_fusion), channel_id=1, source_target_pairs={{0,16},{16,0},{1,17},{17,1},{2,18},{18,2},{3,19},{19,3},{4,20},{20... | collective-permute-start | bytes 393224 | tf_op jit(solution)/shard_map/ppermute | solution.py:34
  6.4 113.1 %collective-permute-start.4 = (f32[112,2048]{1,0:T(8,128)}, f32[112,2048]{1,0:T(8,128)S(1)}, u32[]{:S(2)}, u32[]{:S(2)}) collective-permute-start(f32[112,2048]{1,0:T(8,128)} %constant_dynamic-slice_fusion.5), channel_id=1, source_target_pairs={{0,16},{16,0},{1,17},{17,1},{2,18},{18,2},{3,19},{19,3},{4,20},{20... | collective-permute-start | bytes 2752520 | tf_op jit(solution)/shard_map/ppermute | solution.py:34
  12.5 21.5 %copy-start.13 = (f32[1,2,256]{2,1,0:T(2,128)S(1)}, f32[1,2,256]{2,1,0:T(2,128)}, u32[]{:S(2)}) copy-start(f32[1,2,256]{2,1,0:T(2,128)} %param.14) | copy-start | bytes 6148
  12.5 21.5 %copy-start.14 = (f32[1,256]{1,0:T(1,128)S(1)}, f32[1,256]{1,0:T(1,128)}, u32[]{:S(2)}) copy-start(f32[1,256]{1,0:T(1,128)} %param.15) | copy-start | bytes 3076
  25.9 30.3 %collective-permute-start.7 = (f32[32,4096]{1,0:T(8,128)}, f32[32,4096]{1,0:T(8,128)}, u32[]{:S(2)}, u32[]{:S(2)}) collective-permute-start(f32[32,4096]{1,0:T(8,128)} %slice.73), channel_id=1, source_target_pairs={{0,2},{2,0},{4,6},{6,4},{8,10},{10,8},{12,14},{14,12},{1,3},{3,1},... | collective-permute-start | bytes 1572872 | tf_op jit(solution)/shard_map/ppermute | solution.py:39
  28.7 147.0 %collective-permute-start.1 = (f32[192,2048]{1,0:T(8,128)}, f32[192,2048]{1,0:T(8,128)S(1)}, u32[]{:S(2)}, u32[]{:S(2)}) collective-permute-start(f32[192,2048]{1,0:T(8,128)} %constant_dynamic-slice_fusion.4), channel_id=1, source_target_pairs={{0,16},{16,0},{1,17},{17,1},{2,18},{18,2},{3,19},{19,3},{4,20},{20... | collective-permute-start | bytes 4718600 | tf_op jit(solution)/shard_map/ppermute | solution.py:34
  34.0 213.5 %collective-permute-start.18 = (f32[2,256]{1,0:T(2,128)S(1)}, f32[2,256]{1,0:T(2,128)S(1)}, u32[]{:S(2)}, u32[]{:S(2)}) collective-permute-start(f32[2,256]{1,0:T(2,128)S(1)} %subtract_select_fusion), channel_id=1, source_target_pairs={{0,16},{16,0},{1,17},{17,1},{2,18},{18,2},{3,19},{19,3},{4,20},{20... | collective-permute-start | bytes 6152 | tf_op jit(solution)/shard_map/ppermute | solution.py:34
  34.6 199.9 %collective-permute-start.5 = (f32[192,2048]{1,0:T(8,128)}, f32[192,2048]{1,0:T(8,128)}, u32[]{:S(2)}, u32[]{:S(2)}) collective-permute-start(f32[192,2048]{1,0:T(8,128)} %constant_dynamic-slice_fusion.1), channel_id=1, source_target_pairs={{0,16},{16,0},{1,17},{17,1},{2,18},{18,2},{3,19},{19,3},{4,20},{20... | collective-permute-start | bytes 4718600 | tf_op jit(solution)/shard_map/ppermute | solution.py:34
  58.1 7.9 %collective-permute-start.8 = (f32[16,4096]{1,0:T(8,128)S(1)}, f32[16,4096]{1,0:T(8,128)S(1)}, u32[]{:S(2)}, u32[]{:S(2)}) collective-permute-start(f32[16,4096]{1,0:T(8,128)S(1)} %slice.75), channel_id=1, source_target_pairs={{0,4},{2,6},{4,0},{6,2},{8,12},{10,14},{12,8},{14,10},{1,5},{3,7},... | collective-permute-start | bytes 786440 | tf_op jit(solution)/shard_map/ppermute | solution.py:39
  66.1 5.0 %collective-permute-start.9 = (f32[8,4096]{1,0:T(8,128)S(1)}, f32[8,4096]{1,0:T(8,128)S(1)}, u32[]{:S(2)}, u32[]{:S(2)}) collective-permute-start(f32[8,4096]{1,0:T(8,128)S(1)} %slice.77), channel_id=1, source_target_pairs={{0,8},{2,10},{4,12},{6,14},{8,0},{10,2},{12,4},{14,6},{1,9},{3,11}... | collective-permute-start | bytes 393224 | tf_op jit(solution)/shard_map/ppermute | solution.py:39
  71.1 163.4 %collective-permute-start.10 = (f32[8,4096]{1,0:T(8,128)S(1)}, f32[8,4096]{1,0:T(8,128)S(1)}, u32[]{:S(2)}, u32[]{:S(2)}) collective-permute-start(f32[8,4096]{1,0:T(8,128)S(1)} %slice_add_fusion.2), channel_id=1, source_target_pairs={{0,16},{16,0},{1,17},{17,1},{2,18},{18,2},{3,19},{19,3},{4,20},{20... | collective-permute-start | bytes 393224 | tf_op jit(solution)/shard_map/ppermute | solution.py:34
  119.5 137.7 %collective-permute-start.6 = (f32[128,2048]{1,0:T(8,128)}, f32[128,2048]{1,0:T(8,128)}, u32[]{:S(2)}, u32[]{:S(2)}) collective-permute-start(f32[128,2048]{1,0:T(8,128)} %get-tuple-element.30), channel_id=1, source_target_pairs={{0,16},{16,0},{1,17},{17,1},{2,18},{18,2},{3,19},{19,3},{4,20},{20... | collective-permute-start | bytes 3145736 | tf_op jit(solution)/shard_map/ppermute | solution.py:34
  175.6 141.0 %collective-permute-start.2 = (f32[128,2048]{1,0:T(8,128)}, f32[128,2048]{1,0:T(8,128)}, u32[]{:S(2)}, u32[]{:S(2)}) collective-permute-start(f32[128,2048]{1,0:T(8,128)} %get-tuple-element.25), channel_id=1, source_target_pairs={{0,16},{16,0},{1,17},{17,1},{2,18},{18,2},{3,19},{19,3},{4,20},{20... | collective-permute-start | bytes 3145736 | tf_op jit(solution)/shard_map/ppermute | solution.py:34
  234.6 5.4 %collective-permute-start.11 = (f32[8,4096]{1,0:T(8,128)S(1)}, f32[8,4096]{1,0:T(8,128)S(1)}, u32[]{:S(2)}, u32[]{:S(2)}) collective-permute-start(f32[8,4096]{1,0:T(8,128)S(1)} %add_multiply_fusion), channel_id=1, source_target_pairs={{0,8},{2,10},{4,12},{6,14},{8,0},{10,2},{12,4},{14,6},{1,9},{3,11}... | collective-permute-start | bytes 393224 | tf_op jit(solution)/shard_map/ppermute | solution.py:39
  240.0 8.1 %collective-permute-start.12 = (f32[16,4096]{1,0:T(8,128)S(1)}, f32[16,4096]{1,0:T(8,128)S(1)}, u32[]{:S(2)}, u32[]{:S(2)}) collective-permute-start(f32[16,4096]{1,0:T(8,128)S(1)} %pad_maximum_fusion.2), channel_id=1, source_target_pairs={{0,4},{2,6},{4,0},{6,2},{8,12},{10,14},{12,8},{14,10},{1,5},{3,7},... | collective-permute-start | bytes 786440 | tf_op jit(solution)/shard_map/ppermute | solution.py:39
  248.1 12.5 %collective-permute-start.13 = (f32[32,4096]{1,0:T(8,128)S(1)}, f32[32,4096]{1,0:T(8,128)S(1)}, u32[]{:S(2)}, u32[]{:S(2)}) collective-permute-start(f32[32,4096]{1,0:T(8,128)S(1)} %pad_maximum_fusion.1), channel_id=1, source_target_pairs={{0,2},{2,0},{4,6},{6,4},{8,10},{10,8},{12,14},{14,12},{1,3},{3,1},... | collective-permute-start | bytes 1572872 | tf_op jit(solution)/shard_map/ppermute | solution.py:39
  257.1 56.1 %copy-start.9 = (f32[32,2048]{1,0:T(8,128)S(1)}, f32[32,2048]{1,0:T(8,128)}, u32[]{:S(2)}) copy-start(f32[32,2048]{1,0:T(8,128)} %get-tuple-element.35) | copy-start | bytes 786436
  257.1 59.5 %copy-start.6 = (f32[64,2048]{1,0:T(8,128)S(1)}, f32[64,2048]{1,0:T(8,128)}, u32[]{:S(2)}) copy-start(f32[64,2048]{1,0:T(8,128)} %get-tuple-element.26) | copy-start | bytes 1572868
  257.1 84.2 %copy-start.10 = (f32[32,2048]{1,0:T(8,128)S(1)}, f32[32,2048]{1,0:T(8,128)}, u32[]{:S(2)}) copy-start(f32[32,2048]{1,0:T(8,128)} %get-tuple-element.34) | copy-start | bytes 786436
  257.2 56.0 %collective-permute-start.15 = (f32[64,2048]{1,0:T(8,128)S(1)}, f32[64,2048]{1,0:T(8,128)S(1)}, u32[]{:S(2)}, u32[]{:S(2)}) collective-permute-start(f32[64,2048]{1,0:T(8,128)S(1)} %copy-done.8), channel_id=1, source_target_pairs={{0,16},{16,0},{1,17},{17,1},{2,18},{18,2},{3,19},{19,3},{4,20},{20... | collective-permute-start | bytes 1572872 | tf_op jit(solution)/shard_map/ppermute | solution.py:34
  275.2 66.1 %collective-permute-start.14 = (f32[64,2048]{1,0:T(8,128)S(1)}, f32[64,2048]{1,0:T(8,128)S(1)}, u32[]{:S(2)}, u32[]{:S(2)}) collective-permute-start(f32[64,2048]{1,0:T(8,128)S(1)} %copy-done.7), channel_id=1, source_target_pairs={{0,16},{16,0},{1,17},{17,1},{2,18},{18,2},{3,19},{19,3},{4,20},{20... | collective-permute-start | bytes 1572872 | tf_op jit(solution)/shard_map/ppermute | solution.py:34
  313.2 57.8 %collective-permute-start.17 = (f32[32,2048]{1,0:T(8,128)S(1)}, f32[32,2048]{1,0:T(8,128)S(1)}, u32[]{:S(2)}, u32[]{:S(2)}) collective-permute-start(f32[32,2048]{1,0:T(8,128)S(1)} %copy-done.9), channel_id=1, source_target_pairs={{0,16},{16,0},{1,17},{17,1},{2,18},{18,2},{3,19},{19,3},{4,20},{20... | collective-permute-start | bytes 786440 | tf_op jit(solution)/shard_map/ppermute | solution.py:34
  316.6 47.2 %collective-permute-start.3 = (f32[64,2048]{1,0:T(8,128)S(1)}, f32[64,2048]{1,0:T(8,128)S(1)}, u32[]{:S(2)}, u32[]{:S(2)}) collective-permute-start(f32[64,2048]{1,0:T(8,128)S(1)} %copy-done.6), channel_id=1, source_target_pairs={{0,16},{16,0},{1,17},{17,1},{2,18},{18,2},{3,19},{19,3},{4,20},{20... | collective-permute-start | bytes 1572872 | tf_op jit(solution)/shard_map/ppermute | solution.py:34
  341.3 28.0 %collective-permute-start.16 = (f32[32,2048]{1,0:T(8,128)S(1)}, f32[32,2048]{1,0:T(8,128)S(1)}, u32[]{:S(2)}, u32[]{:S(2)}) collective-permute-start(f32[32,2048]{1,0:T(8,128)S(1)} %copy-done.10), channel_id=1, source_target_pairs={{0,16},{16,0},{1,17},{17,1},{2,18},{18,2},{3,19},{19,3},{4,20},{20... | collective-permute-start | bytes 786440 | tf_op jit(solution)/shard_map/ppermute | solution.py:34
  (13 other events, 138.2 us)

commit v8 on v7

--- a/solution.py
+++ b/solution.py
@@ -12,7 +12,7 @@
 rate = outer_rate * (1 + momentum)
 decay = outer_rate * momentum * momentum
 first_sizes = (1, 7, 12, 12)
-last_sizes = (8, 8, 4, 4, 4, 2, 2)
+last_sizes = (8, 8, 5, 5, 4, 2)
 window = 3
 gate_before = 6
 pinned = 4
@@ -185,6 +185,8 @@
         norm_anchor, norm_local[0], norm_moment, norm_received
     )
 
+    start, size = mixed_spans[-1]
+    last_base = after(rows_of(anchor_next, other + start, size), parts[-3])
     moment_next = []
     for (start, size), part in zip(spans, received):
         old = down_moment[start : start + size]
@@ -199,7 +201,8 @@
         if i == pinned:
             anchor_next = add_rows(anchor_next, part, start, half)
         else:
-            value = rows_of(anchor_next, other + start, size) + part
+            value = last_base if i == len(mixed_spans) - 1 else rows_of(anchor_next, other + start, size)
+            value = value + part
             anchor_next = lax.dynamic_update_slice_in_dim(anchor_next, value, other + start, 0)
     return (
         anchor_next,

time: 376 us -> 373 us (level)
  waiting for transfers between devices: 242 us -> 238 us
  local copies, waits for them, and re-layouts: 20.7 us -> 24.5 us
    ppermute x6, waiting for transfers between devices: 9.01 us -> 0.84 us  [across(): return lax.ppermute(array, 'shard', [(i, i ^ k) for i in range(shards)])]
    ppermute x13 -> x12, waiting for transfers between devices: 233 us -> 237 us  [swap(): return lax.ppermute(array, 'group', [(0, 1), (1, 0)])]
    dynamic_update_slice x6 -> x5, other arithmetic: 12.4 us -> 10 us  [body(): lax.dynamic_update_slice_in_dim(anchor_next, value, other + start, 0)]
    dynamic_slice x4 -> x5, local copies, waits for them, and re-layouts: 8.51 us -> 9.5 us  [rows_of(): return lax.dynamic_slice_in_dim(array, start, size, 0)]
    ppermute x13 -> x12, starting transfers between devices: 26.3 us -> 26 us  [swap(): return lax.ppermute(array, 'group', [(0, 1), (1, 0)])]
  transfers between devices with their start and end apart: 19 -> 18, of which waited for: 11 -> 10; matrix products, arithmetic and copies ran while one was open for 24% -> 26% of each run, Pallas kernels for 1% -> 1%
where the time goes in v8:
time: 373 us; the launch traced here: 370 us
  waiting for transfers between devices  238 us (64%)
  other arithmetic  47.5 us (13%)
  starting transfers between devices  30.4 us (8%)
  matrix products  26.1 us (7%)
  local copies, waits for them, and re-layouts  24.5 us (7%)
    ppermute x12, waiting for transfers between devices, swap(): return lax.ppermute(array, 'group', [(0, 1), (1, 0)])  237 us
    ppermute x12, starting transfers between devices, swap(): return lax.ppermute(array, 'group', [(0, 1), (1, 0)])  26 us
    dot_general x1, matrix products, rebuild(): lax.dot_general(factors, factor_basis, (((0,), (0,)), ((), ())), precisio...  14.6 us
    add x1, other arithmetic, body(): anchor_next = (1 - rate) * after(down_anchor, parts[0]) + rate / 2 * local  12.4 us
    sub x3, other arithmetic, body(): momentum * old + rows_of(down_anchor, own + start, size)  12.3 us
    dot_general x1, matrix products, body(): lax.dot_general(basis, gate_diff, (((1,), (1,)), ((), ())), precision=lax...  11.6 us
    dynamic_update_slice x5, other arithmetic, body(): lax.dynamic_update_slice_in_dim(anchor_next, value, other + start, 0)  10 us
    dynamic_slice x5, local copies, waits for them, and re-layouts, rows_of(): return lax.dynamic_slice_in_dim(array, start, size, 0)  9.5 us
  transfers between devices with their start and end apart: 18, of which 10 were waited for; matrix products, arithmetic and copies ran while one was open for 26% of the time, Pallas kernels for 1%

profile of v8, /device:TPU:10, one launch (start us, length us, event | category | flops | bytes accessed | tf_op | source)
XLA Modules:
  0.0 370.0 jit_solution(16614732507073688932)
XLA Ops:
  1.6 2.7 collective-permute-start
  12.5 11.6 %fusion = f32[64,4096]{1,0:T(8,128)S(1)} fusion(f32[64,512]{1,0:T(8,128)S(1)} %constant_dynamic-update-slice_fusion, f32[4096,512]{1,0:T(8,128)} %param.16, f32[1,4096,512]{2,1,0:T(8,128)} %param.17), kind=kOutput, calls=%fused_computation.1 | convolution fusion | flops 1612709888 | bytes 17956864 | tf_op jit(solution)/shard_map/dot_general | solution.py:153
  25.2 2.7 constant_dynamic-slice_fusion.5
  30.5 2.7 constant_dynamic-slice_fusion.2
  36.2 4.4 %bitcast_subtract_fusion.2 = f32[512,2048]{1,0:T(8,128)S(1)} fusion(f32[512,2048]{1,0:T(8,128)} %param.12, f32[1,1024,2048]{2,1,0:T(8,128)} %param.11, s32[]{:T(128)S(6)} %select_n.91), kind=kLoop, calls=%fused_computation.6 | loop fusion | flops 3145728 | bytes 12582916 | tf_op jit(solution)/shard_map/sub | solution.py:173
  45.1 12.4 %multiply_add_fusion.1 = f32[1024,2048]{1,0:T(8,128)} fusion(f32[1024,2048]{1,0:T(8,128)} %param.10, f32[1,1024,2048]{2,1,0:T(8,128)} %param.11), kind=kLoop, calls=%fused_computation.4 | loop fusion | flops 6291456 | bytes 25165824 | tf_op jit(solution)/shard_map/add | solution.py:174
  66.9 52.6 %collective-permute-done.4 = f32[112,2048]{1,0:T(8,128)} collective-permute-done((f32[112,2048]{1,0:T(8,128)}, f32[112,2048]{1,0:T(8,128)}, u32[]{:S(2)}, u32[]{:S(2)}) %collective-permute-start.4) | collective-permute-done | bytes 917536 | tf_op jit(solution)/shard_map/ppermute | solution.py:34
  119.5 3.4 collective-permute-start.6
  122.8 3.4 fusion.14
  126.2 49.4 %collective-permute-done.1 = f32[192,2048]{1,0:T(8,128)S(1)} collective-permute-done((f32[192,2048]{1,0:T(8,128)}, f32[192,2048]{1,0:T(8,128)S(1)}, u32[]{:S(2)}, u32[]{:S(2)}) %collective-permute-start.1) | collective-permute-done | bytes 1572896 | tf_op jit(solution)/shard_map/ppermute | solution.py:34
  175.6 3.3 collective-permute-start.2
  178.9 55.6 %collective-permute-done.10 = f32[8,4096]{1,0:T(8,128)S(1)} collective-permute-done((f32[8,4096]{1,0:T(8,128)S(1)}, f32[8,4096]{1,0:T(8,128)S(1)}, u32[]{:S(2)}, u32[]{:S(2)}) %collective-permute-start.10) | collective-permute-done | bytes 131104 | tf_op jit(solution)/shard_map/ppermute | solution.py:34
  236.2 3.0 add_dynamic-update-slice_fusion.1
  241.2 7.2 %fusion.4 = (f32[192,2048]{1,0:T(8,128)S(1)}, f32[192,2048]{1,0:T(8,128)S(1)}, f32[1024,2048]{1,0:T(8,128)}) fusion(f32[192,2048]{1,0:T(8,128)S(1)} %collective-permute-done.1, f32[1,1024,2048]{2,1,0:T(8,128)} %param.11, s32[]{:T(128)S(6)} %select_n.96, f32[1024,2048]{1,0:T(8,128)} %param.10, f32[512,2048]{1,0:T(8,128)S(1)} %copy-done, ...), kind=kLoop, calls=%fused_computation.12 | loop fusion | flops 5505024 | bytes 18874376 | tf_op jit(solution)/shard_map/sub | solution.py:194
  252.0 5.1 %collective-permute-done.6 = f32[128,2048]{1,0:T(8,128)} collective-permute-done((f32[128,2048]{1,0:T(8,128)}, f32[128,2048]{1,0:T(8,128)}, u32[]{:S(2)}, u32[]{:S(2)}) %collective-permute-start.6) | collective-permute-done | bytes 1048608 | tf_op jit(solution)/shard_map/ppermute | solution.py:34
  257.1 3.4 collective-permute-start.15
  260.6 14.6 %multiply_subtract_fusion = (f32[4096,512]{1,0:T(8,128)}, f32[4096,512]{1,0:T(8,128)}) fusion(f32[4096,512]{1,0:T(8,128)S(1)} %bitcast.42, f32[4096,512]{1,0:T(8,128)} %param.18, f32[64,512]{1,0:T(8,128)S(1)} %constant_dynamic-update-slice_fusion, f32[32,4096]{1,0:T(8,128)S(1)} %collective-permute-done.13, f32[16,4096]{1,0:T(8,128)S(1)} %collective-permute-done.12, ...), kind=kOutput, calls=%fused_computation.2 | convolution fusion | flops 1623982080 | bytes 34734080 | tf_op jit(solution)/shard_map/dot_general | solution.py:28
  278.0 29.7 %collective-permute-done.2 = f32[128,2048]{1,0:T(8,128)} collective-permute-done((f32[128,2048]{1,0:T(8,128)}, f32[128,2048]{1,0:T(8,128)}, u32[]{:S(2)}, u32[]{:S(2)}) %collective-permute-start.2) | collective-permute-done | bytes 1048608 | tf_op jit(solution)/shard_map/ppermute | solution.py:34
  307.7 3.4 collective-permute-start.3
  311.1 21.8 %collective-permute-done.15 = f32[80,2048]{1,0:T(8,128)S(1)} collective-permute-done((f32[80,2048]{1,0:T(8,128)S(1)}, f32[80,2048]{1,0:T(8,128)S(1)}, u32[]{:S(2)}, u32[]{:S(2)}) %collective-permute-start.15) | collective-permute-done | bytes 655392 | tf_op jit(solution)/shard_map/ppermute | solution.py:34
  335.5 11.4 %collective-permute-done.14 = f32[80,2048]{1,0:T(8,128)S(1)} collective-permute-done((f32[80,2048]{1,0:T(8,128)S(1)}, f32[80,2048]{1,0:T(8,128)S(1)}, u32[]{:S(2)}, u32[]{:S(2)}) %collective-permute-start.14) | collective-permute-done | bytes 655392 | tf_op jit(solution)/shard_map/ppermute | solution.py:34
  346.9 3.4 collective-permute-start.16
  354.3 9.5 %collective-permute-done.3.part = f32[64,2048]{1,0:T(8,128)S(1)} collective-permute-done((f32[64,2048]{1,0:T(8,128)S(1)}, f32[64,2048]{1,0:T(8,128)S(1)}, u32[]{:S(2)}, u32[]{:S(2)}) %collective-permute-start.3) | collective-permute-done | bytes 524320 | tf_op jit(solution)/shard_map/ppermute | solution.py:34
  364.6 2.9 shard_map.145
  (87 shorter events, 49.7 us)
Async XLA Ops:
  1.6 31.7 %collective-permute-start = (f32[16,2048]{1,0:T(8,128)S(1)}, f32[16,2048]{1,0:T(8,128)S(1)}, u32[]{:S(2)}, u32[]{:S(2)}) collective-permute-start(f32[16,2048]{1,0:T(8,128)S(1)} %dynamic-slice_bitcast_fusion), channel_id=1, source_target_pairs={{0,16},{16,0},{1,17},{17,1},{2,18},{18,2},{3,19},{19,3},{4,20},{20... | collective-permute-start | bytes 393224 | tf_op jit(solution)/shard_map/ppermute | solution.py:34
  6.4 113.0 %collective-permute-start.4 = (f32[112,2048]{1,0:T(8,128)}, f32[112,2048]{1,0:T(8,128)}, u32[]{:S(2)}, u32[]{:S(2)}) collective-permute-start(f32[112,2048]{1,0:T(8,128)} %constant_dynamic-slice_fusion.6), channel_id=1, source_target_pairs={{0,16},{16,0},{1,17},{17,1},{2,18},{18,2},{3,19},{19,3},{4,20},{20... | collective-permute-start | bytes 2752520 | tf_op jit(solution)/shard_map/ppermute | solution.py:34
  12.5 20.7 %copy-start.10 = (f32[1,2,256]{2,1,0:T(2,128)S(1)}, f32[1,2,256]{2,1,0:T(2,128)}, u32[]{:S(2)}) copy-start(f32[1,2,256]{2,1,0:T(2,128)} %param.14) | copy-start | bytes 6148
  12.5 20.7 %copy-start.11 = (f32[1,256]{1,0:T(1,128)S(1)}, f32[1,256]{1,0:T(1,128)}, u32[]{:S(2)}) copy-start(f32[1,256]{1,0:T(1,128)} %param.15) | copy-start | bytes 3076
  25.1 18.6 %collective-permute-start.7 = (f32[32,4096]{1,0:T(8,128)S(1)}, f32[32,4096]{1,0:T(8,128)S(1)}, u32[]{:S(2)}, u32[]{:S(2)}) collective-permute-start(f32[32,4096]{1,0:T(8,128)S(1)} %slice.69), channel_id=1, source_target_pairs={{0,2},{2,0},{4,6},{6,4},{8,10},{10,8},{12,14},{14,12},{1,3},{3,1},... | collective-permute-start | bytes 1572872 | tf_op jit(solution)/shard_map/ppermute | solution.py:39
  27.9 147.7 %collective-permute-start.1 = (f32[192,2048]{1,0:T(8,128)}, f32[192,2048]{1,0:T(8,128)S(1)}, u32[]{:S(2)}, u32[]{:S(2)}) collective-permute-start(f32[192,2048]{1,0:T(8,128)} %constant_dynamic-slice_fusion.5), channel_id=1, source_target_pairs={{0,16},{16,0},{1,17},{17,1},{2,18},{18,2},{3,19},{19,3},{4,20},{20... | collective-permute-start | bytes 4718600 | tf_op jit(solution)/shard_map/ppermute | solution.py:34
  33.2 215.2 %collective-permute-start.17 = (f32[2,256]{1,0:T(2,128)S(1)}, f32[2,256]{1,0:T(2,128)S(1)}, u32[]{:S(2)}, u32[]{:S(2)}) collective-permute-start(f32[2,256]{1,0:T(2,128)S(1)} %subtract_select_fusion), channel_id=1, source_target_pairs={{0,16},{16,0},{1,17},{17,1},{2,18},{18,2},{3,19},{19,3},{4,20},{20... | collective-permute-start | bytes 6152 | tf_op jit(solution)/shard_map/ppermute | solution.py:34
  33.6 200.9 %collective-permute-start.5 = (f32[192,2048]{1,0:T(8,128)}, f32[192,2048]{1,0:T(8,128)}, u32[]{:S(2)}, u32[]{:S(2)}) collective-permute-start(f32[192,2048]{1,0:T(8,128)} %constant_dynamic-slice_fusion.2), channel_id=1, source_target_pairs={{0,16},{16,0},{1,17},{17,1},{2,18},{18,2},{3,19},{19,3},{4,20},{20... | collective-permute-start | bytes 4718600 | tf_op jit(solution)/shard_map/ppermute | solution.py:34
  44.5 13.9 %collective-permute-start.8 = (f32[16,4096]{1,0:T(8,128)}, f32[16,4096]{1,0:T(8,128)}, u32[]{:S(2)}, u32[]{:S(2)}) collective-permute-start(f32[16,4096]{1,0:T(8,128)} %slice.71), channel_id=1, source_target_pairs={{0,4},{2,6},{4,0},{6,2},{8,12},{10,14},{12,8},{14,10},{1,5},{3,7},... | collective-permute-start | bytes 786440 | tf_op jit(solution)/shard_map/ppermute | solution.py:39
  59.4 7.0 %collective-permute-start.9 = (f32[8,4096]{1,0:T(8,128)S(1)}, f32[8,4096]{1,0:T(8,128)S(1)}, u32[]{:S(2)}, u32[]{:S(2)}) collective-permute-start(f32[8,4096]{1,0:T(8,128)S(1)} %slice.73), channel_id=1, source_target_pairs={{0,8},{2,10},{4,12},{6,14},{8,0},{10,2},{12,4},{14,6},{1,9},{3,11}... | collective-permute-start | bytes 393224 | tf_op jit(solution)/shard_map/ppermute | solution.py:39
  66.5 168.1 %collective-permute-start.10 = (f32[8,4096]{1,0:T(8,128)S(1)}, f32[8,4096]{1,0:T(8,128)S(1)}, u32[]{:S(2)}, u32[]{:S(2)}) collective-permute-start(f32[8,4096]{1,0:T(8,128)S(1)} %slice_add_fusion.2), channel_id=1, source_target_pairs={{0,16},{16,0},{1,17},{17,1},{2,18},{18,2},{3,19},{19,3},{4,20},{20... | collective-permute-start | bytes 393224 | tf_op jit(solution)/shard_map/ppermute | solution.py:34
  119.5 137.7 %collective-permute-start.6 = (f32[128,2048]{1,0:T(8,128)}, f32[128,2048]{1,0:T(8,128)}, u32[]{:S(2)}, u32[]{:S(2)}) collective-permute-start(f32[128,2048]{1,0:T(8,128)} %get-tuple-element.30), channel_id=1, source_target_pairs={{0,16},{16,0},{1,17},{17,1},{2,18},{18,2},{3,19},{19,3},{4,20},{20... | collective-permute-start | bytes 3145736 | tf_op jit(solution)/shard_map/ppermute | solution.py:34
  175.6 132.1 %collective-permute-start.2 = (f32[128,2048]{1,0:T(8,128)}, f32[128,2048]{1,0:T(8,128)}, u32[]{:S(2)}, u32[]{:S(2)}) collective-permute-start(f32[128,2048]{1,0:T(8,128)} %get-tuple-element.25), channel_id=1, source_target_pairs={{0,16},{16,0},{1,17},{17,1},{2,18},{18,2},{3,19},{19,3},{4,20},{20... | collective-permute-start | bytes 3145736 | tf_op jit(solution)/shard_map/ppermute | solution.py:34
  234.6 5.4 %collective-permute-start.11 = (f32[8,4096]{1,0:T(8,128)S(1)}, f32[8,4096]{1,0:T(8,128)S(1)}, u32[]{:S(2)}, u32[]{:S(2)}) collective-permute-start(f32[8,4096]{1,0:T(8,128)S(1)} %add_multiply_fusion), channel_id=1, source_target_pairs={{0,8},{2,10},{4,12},{6,14},{8,0},{10,2},{12,4},{14,6},{1,9},{3,11}... | collective-permute-start | bytes 393224 | tf_op jit(solution)/shard_map/ppermute | solution.py:39
  240.0 20.6 %slice-start = ((s8[8388608]{0:T(1024)(128)(4,1)}), s8[4194304]{0:T(1024)(128)(4,1)S(1)}, s32[]{:S(2)}) async-start(s8[8388608]{0:T(1024)(128)(4,1)} %bitcast.41), calls=%async_computation | async-start | bytes 8388608
  240.7 19.9 %slice-start.1 = ((s8[8388608]{0:T(1024)(128)(4,1)}), s8[4194304]{0:T(1024)(128)(4,1)S(1)}, s32[]{:S(2)}) async-start(s8[8388608]{0:T(1024)(128)(4,1)} %bitcast.41), calls=%async_computation.1 | async-start | bytes 8388608
  240.7 8.3 %collective-permute-start.12 = (f32[16,4096]{1,0:T(8,128)}, f32[16,4096]{1,0:T(8,128)S(1)}, u32[]{:S(2)}, u32[]{:S(2)}) collective-permute-start(f32[16,4096]{1,0:T(8,128)} %pad_maximum_fusion.2), channel_id=1, source_target_pairs={{0,4},{2,6},{4,0},{6,2},{8,12},{10,14},{12,8},{14,10},{1,5},{3,7},... | collective-permute-start | bytes 786440 | tf_op jit(solution)/shard_map/ppermute | solution.py:39
  249.1 11.5 %collective-permute-start.13 = (f32[32,4096]{1,0:T(8,128)S(1)}, f32[32,4096]{1,0:T(8,128)S(1)}, u32[]{:S(2)}, u32[]{:S(2)}) collective-permute-start(f32[32,4096]{1,0:T(8,128)S(1)} %pad_maximum_fusion.1), channel_id=1, source_target_pairs={{0,2},{2,0},{4,6},{6,4},{8,10},{10,8},{12,14},{14,12},{1,3},{3,1},... | collective-permute-start | bytes 1572872 | tf_op jit(solution)/shard_map/ppermute | solution.py:39
  257.1 50.6 %copy-start.7 = (f32[64,2048]{1,0:T(8,128)S(1)}, f32[64,2048]{1,0:T(8,128)}, u32[]{:S(2)}) copy-start(f32[64,2048]{1,0:T(8,128)} %slice.64) | copy-start | bytes 1572868
  257.1 89.8 %copy-start.8 = (f32[32,2048]{1,0:T(8,128)S(1)}, f32[32,2048]{1,0:T(8,128)}, u32[]{:S(2)}) copy-start(f32[32,2048]{1,0:T(8,128)} %slice.75) | copy-start | bytes 786436
  257.1 75.7 %collective-permute-start.15 = (f32[80,2048]{1,0:T(8,128)S(1)}, f32[80,2048]{1,0:T(8,128)S(1)}, u32[]{:S(2)}, u32[]{:S(2)}) collective-permute-start(f32[80,2048]{1,0:T(8,128)S(1)} %copy-done.5), channel_id=1, source_target_pairs={{0,16},{16,0},{1,17},{17,1},{2,18},{18,2},{3,19},{19,3},{4,20},{20... | collective-permute-start | bytes 1966088 | tf_op jit(solution)/shard_map/ppermute | solution.py:34
  275.2 71.7 %collective-permute-start.14 = (f32[80,2048]{1,0:T(8,128)S(1)}, f32[80,2048]{1,0:T(8,128)S(1)}, u32[]{:S(2)}, u32[]{:S(2)}) collective-permute-start(f32[80,2048]{1,0:T(8,128)S(1)} %copy-done.4), channel_id=1, source_target_pairs={{0,16},{16,0},{1,17},{17,1},{2,18},{18,2},{3,19},{19,3},{4,20},{20... | collective-permute-start | bytes 1966088 | tf_op jit(solution)/shard_map/ppermute | solution.py:34
  307.7 56.1 %collective-permute-start.3 = (f32[64,2048]{1,0:T(8,128)S(1)}, f32[64,2048]{1,0:T(8,128)S(1)}, u32[]{:S(2)}, u32[]{:S(2)}) collective-permute-start(f32[64,2048]{1,0:T(8,128)S(1)} %copy-done.7), channel_id=1, source_target_pairs={{0,16},{16,0},{1,17},{17,1},{2,18},{18,2},{3,19},{19,3},{4,20},{20... | collective-permute-start | bytes 1572872 | tf_op jit(solution)/shard_map/ppermute | solution.py:34
  346.9 22.4 %collective-permute-start.16 = (f32[32,2048]{1,0:T(8,128)S(1)}, f32[32,2048]{1,0:T(8,128)S(1)}, u32[]{:S(2)}, u32[]{:S(2)}) collective-permute-start(f32[32,2048]{1,0:T(8,128)S(1)} %copy-done.8), channel_id=1, source_target_pairs={{0,16},{16,0},{1,17},{17,1},{2,18},{18,2},{3,19},{19,3},{4,20},{20... | collective-permute-start | bytes 786440 | tf_op jit(solution)/shard_map/ppermute | solution.py:34
  (9 other events, 76.9 us)

commit v9 on v8

--- a/solution.py
+++ b/solution.py
@@ -11,7 +11,7 @@
 momentum = 0.9
 rate = outer_rate * (1 + momentum)
 decay = outer_rate * momentum * momentum
-first_sizes = (1, 7, 12, 12)
+first_sizes = (1, 5, 13, 13)
 last_sizes = (8, 8, 5, 5, 4, 2)
 window = 3
 gate_before = 6

time: 373 us -> 373 us (level)
  waiting for transfers between devices: 238 us -> 232 us
    ppermute x12, waiting for transfers between devices: 237 us -> 229 us  [swap(): return lax.ppermute(array, 'group', [(0, 1), (1, 0)])]
    unnamed x37 -> x29, local copies, waits for them, and re-layouts: 6.85 us -> 8.04 us
where the time goes in v9:
time: 373 us; the launch traced here: 370 us
  waiting for transfers between devices  232 us (62%)
  other arithmetic  49.8 us (13%)
  starting transfers between devices  33.6 us (9%)
  matrix products  26.4 us (7%)
  local copies, waits for them, and re-layouts  24 us (6%)
    ppermute x12, waiting for transfers between devices, swap(): return lax.ppermute(array, 'group', [(0, 1), (1, 0)])  229 us
    ppermute x12, starting transfers between devices, swap(): return lax.ppermute(array, 'group', [(0, 1), (1, 0)])  29.1 us
    dot_general x1, matrix products, rebuild(): lax.dot_general(factors, factor_basis, (((0,), (0,)), ((), ())), precisio...  14.8 us
    sub x3, other arithmetic, body(): momentum * old + rows_of(down_anchor, own + start, size)  12.9 us
    add x1, other arithmetic, body(): anchor_next = (1 - rate) * after(down_anchor, parts[0]) + rate / 2 * local  12.1 us
    dot_general x1, matrix products, body(): lax.dot_general(basis, gate_diff, (((1,), (1,)), ((), ())), precision=lax...  11.6 us
    dynamic_update_slice x5, other arithmetic, body(): lax.dynamic_update_slice_in_dim(anchor_next, value, other + start, 0)  10.2 us
    dynamic_slice x5, local copies, waits for them, and re-layouts, rows_of(): return lax.dynamic_slice_in_dim(array, start, size, 0)  9.51 us
  transfers between devices with their start and end apart: 18, of which 10 were waited for; matrix products, arithmetic and copies ran while one was open for 26% of the time, Pallas kernels for 1%

profile of v9, /device:TPU:10, one launch (start us, length us, event | category | flops | bytes accessed | tf_op | source)
XLA Modules:
  0.0 370.0 jit_solution(5661742617373484498)
XLA Ops:
  12.3 11.6 %fusion = f32[64,4096]{1,0:T(8,128)S(1)} fusion(f32[64,512]{1,0:T(8,128)S(1)} %constant_dynamic-update-slice_fusion, f32[4096,512]{1,0:T(8,128)} %param.16, f32[1,4096,512]{2,1,0:T(8,128)} %param.17), kind=kOutput, calls=%fused_computation.1 | convolution fusion | flops 1612709888 | bytes 17956864 | tf_op jit(solution)/shard_map/dot_general | solution.py:153
  25.8 2.8 constant_dynamic-slice_fusion.5
  31.2 2.8 constant_dynamic-slice_fusion.3
  34.0 4.4 %bitcast_subtract_fusion.2 = f32[512,2048]{1,0:T(8,128)S(1)} fusion(f32[512,2048]{1,0:T(8,128)} %param.12, f32[1,1024,2048]{2,1,0:T(8,128)} %param.11, s32[]{:T(128)S(6)} %select_n.93), kind=kLoop, calls=%fused_computation.6 | loop fusion | flops 3145728 | bytes 12582916 | tf_op jit(solution)/shard_map/sub | solution.py:173
  44.7 12.1 %multiply_add_fusion.1 = f32[1024,2048]{1,0:T(8,128)} fusion(f32[1024,2048]{1,0:T(8,128)} %param.10, f32[1,1024,2048]{2,1,0:T(8,128)} %param.11), kind=kLoop, calls=%fused_computation.4 | loop fusion | flops 6291456 | bytes 25165824 | tf_op jit(solution)/shard_map/add | solution.py:174
  64.1 46.9 %collective-permute-done.4 = f32[80,2048]{1,0:T(8,128)} collective-permute-done((f32[80,2048]{1,0:T(8,128)}, f32[80,2048]{1,0:T(8,128)}, u32[]{:S(2)}, u32[]{:S(2)}) %collective-permute-start.4) | collective-permute-done | bytes 655392 | tf_op jit(solution)/shard_map/ppermute | solution.py:34
  111.0 3.4 collective-permute-start.6
  116.0 2.8 fusion.14
  119.9 52.9 %collective-permute-done.1 = f32[208,2048]{1,0:T(8,128)S(1)} collective-permute-done((f32[208,2048]{1,0:T(8,128)}, f32[208,2048]{1,0:T(8,128)S(1)}, u32[]{:S(2)}, u32[]{:S(2)}) %collective-permute-start.1) | collective-permute-done | bytes 1703968 | tf_op jit(solution)/shard_map/ppermute | solution.py:34
  172.8 3.3 collective-permute-start.2
  176.1 78.1 %collective-permute-done.6 = f32[128,2048]{1,0:T(8,128)} collective-permute-done((f32[128,2048]{1,0:T(8,128)S(1)}, f32[128,2048]{1,0:T(8,128)}, u32[]{:S(2)}, u32[]{:S(2)}) %collective-permute-start.6) | collective-permute-done | bytes 1048608 | tf_op jit(solution)/shard_map/ppermute | solution.py:34
  254.2 3.5 collective-permute-start.15
  257.7 3.1 add_dynamic-update-slice_fusion.1
  260.8 10.3 %collective-permute-done.10 = f32[8,4096]{1,0:T(8,128)S(1)} collective-permute-done((f32[8,4096]{1,0:T(8,128)S(1)}, f32[8,4096]{1,0:T(8,128)S(1)}, u32[]{:S(2)}, u32[]{:S(2)}) %collective-permute-start.10) | collective-permute-done | bytes 131104 | tf_op jit(solution)/shard_map/ppermute | solution.py:34
  272.7 8.4 %fusion.4 = (f32[208,2048]{1,0:T(8,128)}, f32[208,2048]{1,0:T(8,128)}, f32[1024,2048]{1,0:T(8,128)}) fusion(f32[208,2048]{1,0:T(8,128)S(1)} %collective-permute-done.1, f32[1,1024,2048]{2,1,0:T(8,128)} %param.11, s32[]{:T(128)S(6)} %select_n.98, f32[1024,2048]{1,0:T(8,128)} %param.10, f32[512,2048]{1,0:T(8,128)S(1)} %copy-done, ...), kind=kLoop, calls=%fused_computation.12 | loop fusion | flops 5963776 | bytes 20447240 | tf_op jit(solution)/shard_map/sub | solution.py:194
  281.7 4.5 %pad_maximum_fusion = f32[512,2048]{1,0:T(8,128)} fusion(f32[208,2048]{1,0:T(8,128)} %get-tuple-element.41, f32[208,2048]{1,0:T(8,128)} %get-tuple-element.40, f32[80,2048]{1,0:T(8,128)S(1)} %get-tuple-element.43, f32[16,2048]{1,0:T(8,128)S(1)} %get-tuple-element.45), kind=kLoop, calls=%fused_computation.5 | loop fusion | flops 3145728 | bytes 8388608 | tf_op jit(solution)/shard_map/concatenate | solution.py:209
  292.3 14.8 %multiply_subtract_fusion = (f32[4096,512]{1,0:T(8,128)}, f32[4096,512]{1,0:T(8,128)}) fusion(f32[4096,512]{1,0:T(8,128)S(1)} %bitcast.42, f32[4096,512]{1,0:T(8,128)} %param.18, f32[64,512]{1,0:T(8,128)S(1)} %constant_dynamic-update-slice_fusion, f32[32,4096]{1,0:T(8,128)S(1)} %collective-permute-done.13, f32[16,4096]{1,0:T(8,128)S(1)} %collective-permute-done.12, ...), kind=kOutput, calls=%fused_computation.2 | convolution fusion | flops 1623982080 | bytes 34734080 | tf_op jit(solution)/shard_map/dot_general | solution.py:28
  307.2 3.4 collective-permute-start.14
  311.1 21.9 %collective-permute-done.15 = f32[80,2048]{1,0:T(8,128)} collective-permute-done((f32[80,2048]{1,0:T(8,128)}, f32[80,2048]{1,0:T(8,128)}, u32[]{:S(2)}, u32[]{:S(2)}) %collective-permute-start.15) | collective-permute-done | bytes 655392 | tf_op jit(solution)/shard_map/ppermute | solution.py:34
  333.0 3.4 collective-permute-start.3
  339.0 13.5 %collective-permute-done.14 = f32[80,2048]{1,0:T(8,128)S(1)} collective-permute-done((f32[80,2048]{1,0:T(8,128)S(1)}, f32[80,2048]{1,0:T(8,128)S(1)}, u32[]{:S(2)}, u32[]{:S(2)}) %collective-permute-start.14) | collective-permute-done | bytes 655392 | tf_op jit(solution)/shard_map/ppermute | solution.py:34
  352.5 3.4 collective-permute-start.16
  360.1 3.6 collective-permute-done.3.part
  364.6 2.9 shard_map.145
  (79 shorter events, 51.5 us)
Async XLA Ops:
  1.6 32.4 %collective-permute-start = (f32[16,2048]{1,0:T(8,128)S(1)}, f32[16,2048]{1,0:T(8,128)S(1)}, u32[]{:S(2)}, u32[]{:S(2)}) collective-permute-start(f32[16,2048]{1,0:T(8,128)S(1)} %dynamic-slice_bitcast_fusion), channel_id=1, source_target_pairs={{0,16},{16,0},{1,17},{17,1},{2,18},{18,2},{3,19},{19,3},{4,20},{20... | collective-permute-start | bytes 393224 | tf_op jit(solution)/shard_map/ppermute | solution.py:34
  6.2 104.8 %collective-permute-start.4 = (f32[80,2048]{1,0:T(8,128)}, f32[80,2048]{1,0:T(8,128)}, u32[]{:S(2)}, u32[]{:S(2)}) collective-permute-start(f32[80,2048]{1,0:T(8,128)} %constant_dynamic-slice_fusion.6), channel_id=1, source_target_pairs={{0,16},{16,0},{1,17},{17,1},{2,18},{18,2},{3,19},{19,3},{4,20},{20... | collective-permute-start | bytes 1966088 | tf_op jit(solution)/shard_map/ppermute | solution.py:34
  12.3 21.7 %copy-start.6 = (f32[1,2,256]{2,1,0:T(2,128)S(1)}, f32[1,2,256]{2,1,0:T(2,128)}, u32[]{:S(2)}) copy-start(f32[1,2,256]{2,1,0:T(2,128)} %param.14) | copy-start | bytes 6148
  12.3 21.7 %copy-start.7 = (f32[1,256]{1,0:T(1,128)S(1)}, f32[1,256]{1,0:T(1,128)}, u32[]{:S(2)}) copy-start(f32[1,256]{1,0:T(1,128)} %param.15) | copy-start | bytes 3076
  25.8 34.7 %collective-permute-start.7 = (f32[32,4096]{1,0:T(8,128)}, f32[32,4096]{1,0:T(8,128)}, u32[]{:S(2)}, u32[]{:S(2)}) collective-permute-start(f32[32,4096]{1,0:T(8,128)} %slice.69), channel_id=1, source_target_pairs={{0,2},{2,0},{4,6},{6,4},{8,10},{10,8},{12,14},{14,12},{1,3},{3,1},... | collective-permute-start | bytes 1572872 | tf_op jit(solution)/shard_map/ppermute | solution.py:39
  28.6 144.2 %collective-permute-start.1 = (f32[208,2048]{1,0:T(8,128)}, f32[208,2048]{1,0:T(8,128)S(1)}, u32[]{:S(2)}, u32[]{:S(2)}) collective-permute-start(f32[208,2048]{1,0:T(8,128)} %constant_dynamic-slice_fusion.5), channel_id=1, source_target_pairs={{0,16},{16,0},{1,17},{17,1},{2,18},{18,2},{3,19},{19,3},{4,20},{20... | collective-permute-start | bytes 5111816 | tf_op jit(solution)/shard_map/ppermute | solution.py:34
  41.7 20.6 %copy-start = (f32[512,2048]{1,0:T(8,128)S(1)}, f32[512,2048]{1,0:T(8,128)}, u32[]{:S(2)}) copy-start(f32[512,2048]{1,0:T(8,128)} %param.12) | copy-start | bytes 12582916
  41.7 239.3 %collective-permute-start.17 = (f32[2,256]{1,0:T(2,128)S(1)}, f32[2,256]{1,0:T(2,128)S(1)}, u32[]{:S(2)}, u32[]{:S(2)}) collective-permute-start(f32[2,256]{1,0:T(2,128)S(1)} %subtract_select_fusion), channel_id=1, source_target_pairs={{0,16},{16,0},{1,17},{17,1},{2,18},{18,2},{3,19},{19,3},{4,20},{20... | collective-permute-start | bytes 6152 | tf_op jit(solution)/shard_map/ppermute | solution.py:34
  42.1 229.0 %collective-permute-start.5 = (f32[208,2048]{1,0:T(8,128)}, f32[208,2048]{1,0:T(8,128)}, u32[]{:S(2)}, u32[]{:S(2)}) collective-permute-start(f32[208,2048]{1,0:T(8,128)} %constant_dynamic-slice_fusion.3), channel_id=1, source_target_pairs={{0,16},{16,0},{1,17},{17,1},{2,18},{18,2},{3,19},{19,3},{4,20},{20... | collective-permute-start | bytes 5111816 | tf_op jit(solution)/shard_map/ppermute | solution.py:34
  61.8 52.7 %collective-permute-start.8 = (f32[16,4096]{1,0:T(8,128)S(1)}, f32[16,4096]{1,0:T(8,128)S(1)}, u32[]{:S(2)}, u32[]{:S(2)}) collective-permute-start(f32[16,4096]{1,0:T(8,128)S(1)} %slice.71), channel_id=1, source_target_pairs={{0,4},{2,6},{4,0},{6,2},{8,12},{10,14},{12,8},{14,10},{1,5},{3,7},... | collective-permute-start | bytes 786440 | tf_op jit(solution)/shard_map/ppermute | solution.py:39
  111.0 143.2 %collective-permute-start.6 = (f32[128,2048]{1,0:T(8,128)S(1)}, f32[128,2048]{1,0:T(8,128)}, u32[]{:S(2)}, u32[]{:S(2)}) collective-permute-start(f32[128,2048]{1,0:T(8,128)S(1)} %get-tuple-element.30), channel_id=1, source_target_pairs={{0,16},{16,0},{1,17},{17,1},{2,18},{18,2},{3,19},{19,3},{4,20},{20... | collective-permute-start | bytes 3145736 | tf_op jit(solution)/shard_map/ppermute | solution.py:34
  114.5 5.1 %collective-permute-start.9 = (f32[8,4096]{1,0:T(8,128)S(1)}, f32[8,4096]{1,0:T(8,128)S(1)}, u32[]{:S(2)}, u32[]{:S(2)}) collective-permute-start(f32[8,4096]{1,0:T(8,128)S(1)} %slice.73), channel_id=1, source_target_pairs={{0,8},{2,10},{4,12},{6,14},{8,0},{10,2},{12,4},{14,6},{1,9},{3,11}... | collective-permute-start | bytes 393224 | tf_op jit(solution)/shard_map/ppermute | solution.py:39
  119.6 151.5 %collective-permute-start.10 = (f32[8,4096]{1,0:T(8,128)S(1)}, f32[8,4096]{1,0:T(8,128)S(1)}, u32[]{:S(2)}, u32[]{:S(2)}) collective-permute-start(f32[8,4096]{1,0:T(8,128)S(1)} %slice_add_fusion.2), channel_id=1, source_target_pairs={{0,16},{16,0},{1,17},{17,1},{2,18},{18,2},{3,19},{19,3},{4,20},{20... | collective-permute-start | bytes 393224 | tf_op jit(solution)/shard_map/ppermute | solution.py:34
  172.8 160.2 %collective-permute-start.2 = (f32[128,2048]{1,0:T(8,128)}, f32[128,2048]{1,0:T(8,128)}, u32[]{:S(2)}, u32[]{:S(2)}) collective-permute-start(f32[128,2048]{1,0:T(8,128)} %get-tuple-element.25), channel_id=1, source_target_pairs={{0,16},{16,0},{1,17},{17,1},{2,18},{18,2},{3,19},{19,3},{4,20},{20... | collective-permute-start | bytes 3145736 | tf_op jit(solution)/shard_map/ppermute | solution.py:34
  254.2 78.8 %collective-permute-start.15 = (f32[80,2048]{1,0:T(8,128)}, f32[80,2048]{1,0:T(8,128)}, u32[]{:S(2)}, u32[]{:S(2)}) collective-permute-start(f32[80,2048]{1,0:T(8,128)} %get-tuple-element.33), channel_id=1, source_target_pairs={{0,16},{16,0},{1,17},{17,1},{2,18},{18,2},{3,19},{19,3},{4,20},{20... | collective-permute-start | bytes 1966088 | tf_op jit(solution)/shard_map/ppermute | solution.py:34
  271.1 21.2 %slice-start = ((s8[8388608]{0:T(1024)(128)(4,1)}), s8[4194304]{0:T(1024)(128)(4,1)S(1)}, s32[]{:S(2)}) async-start(s8[8388608]{0:T(1024)(128)(4,1)} %bitcast.41), calls=%async_computation | async-start | bytes 8388608
  271.1 21.2 %slice-start.1 = ((s8[8388608]{0:T(1024)(128)(4,1)}), s8[4194304]{0:T(1024)(128)(4,1)S(1)}, s32[]{:S(2)}) async-start(s8[8388608]{0:T(1024)(128)(4,1)} %bitcast.41), calls=%async_computation.1 | async-start | bytes 8388608
  271.1 10.0 %collective-permute-start.11 = (f32[8,4096]{1,0:T(8,128)S(1)}, f32[8,4096]{1,0:T(8,128)S(1)}, u32[]{:S(2)}, u32[]{:S(2)}) collective-permute-start(f32[8,4096]{1,0:T(8,128)S(1)} %add_multiply_fusion), channel_id=1, source_target_pairs={{0,8},{2,10},{4,12},{6,14},{8,0},{10,2},{12,4},{14,6},{1,9},{3,11}... | collective-permute-start | bytes 393224 | tf_op jit(solution)/shard_map/ppermute | solution.py:39
  281.1 7.8 %collective-permute-start.12 = (f32[16,4096]{1,0:T(8,128)S(1)}, f32[16,4096]{1,0:T(8,128)S(1)}, u32[]{:S(2)}, u32[]{:S(2)}) collective-permute-start(f32[16,4096]{1,0:T(8,128)S(1)} %pad_maximum_fusion.2), channel_id=1, source_target_pairs={{0,4},{2,6},{4,0},{6,2},{8,12},{10,14},{12,8},{14,10},{1,5},{3,7},... | collective-permute-start | bytes 786440 | tf_op jit(solution)/shard_map/ppermute | solution.py:39
  289.0 3.3 collective-permute-start.13
  292.3 40.7 %copy-start.5 = (f32[64,2048]{1,0:T(8,128)S(1)}, f32[64,2048]{1,0:T(8,128)}, u32[]{:S(2)}) copy-start(f32[64,2048]{1,0:T(8,128)} %slice.64) | copy-start | bytes 1572868
  307.2 45.4 %collective-permute-start.14 = (f32[80,2048]{1,0:T(8,128)S(1)}, f32[80,2048]{1,0:T(8,128)S(1)}, u32[]{:S(2)}, u32[]{:S(2)}) collective-permute-start(f32[80,2048]{1,0:T(8,128)S(1)} %copy-done.3), channel_id=1, source_target_pairs={{0,16},{16,0},{1,17},{17,1},{2,18},{18,2},{3,19},{19,3},{4,20},{20... | collective-permute-start | bytes 1966088 | tf_op jit(solution)/shard_map/ppermute | solution.py:34
  333.0 30.8 %collective-permute-start.3 = (f32[64,2048]{1,0:T(8,128)S(1)}, f32[64,2048]{1,0:T(8,128)S(1)}, u32[]{:S(2)}, u32[]{:S(2)}) collective-permute-start(f32[64,2048]{1,0:T(8,128)S(1)} %copy-done.5), channel_id=1, source_target_pairs={{0,16},{16,0},{1,17},{17,1},{2,18},{18,2},{3,19},{19,3},{4,20},{20... | collective-permute-start | bytes 1572872 | tf_op jit(solution)/shard_map/ppermute | solution.py:34
  352.5 16.8 %collective-permute-start.16 = (f32[32,2048]{1,0:T(8,128)S(1)}, f32[32,2048]{1,0:T(8,128)S(1)}, u32[]{:S(2)}, u32[]{:S(2)}) collective-permute-start(f32[32,2048]{1,0:T(8,128)S(1)} %slice.75), channel_id=1, source_target_pairs={{0,16},{16,0},{1,17},{17,1},{2,18},{18,2},{3,19},{19,3},{4,20},{20... | collective-permute-start | bytes 786440 | tf_op jit(solution)/shard_map/ppermute | solution.py:34
  (5 other events, 26.8 us)

commit v10 on v9

--- a/solution.py
+++ b/solution.py
@@ -11,7 +11,7 @@
 momentum = 0.9
 rate = outer_rate * (1 + momentum)
 decay = outer_rate * momentum * momentum
-first_sizes = (1, 5, 13, 13)
+first_sizes = (1, 6, 12, 13)
 last_sizes = (8, 8, 5, 5, 4, 2)
 window = 3
 gate_before = 6

time: 373 us -> 373 us (level)
  waiting for transfers between devices: 232 us -> 246 us
  local copies, waits for them, and re-layouts: 24 us -> 20 us
  other arithmetic: 49.8 us -> 46 us
    ppermute x12, waiting for transfers between devices: 229 us -> 236 us  [swap(): return lax.ppermute(array, 'group', [(0, 1), (1, 0)])]
    ppermute x6, waiting for transfers between devices: 3.49 us -> 10.1 us  [across(): return lax.ppermute(array, 'shard', [(i, i ^ k) for i in range(shards)])]
    unnamed x29 -> x27, local copies, waits for them, and re-layouts: 8.04 us -> 5.86 us
    sub x3 -> x4, other arithmetic: 12.9 us -> 15 us  [body(): momentum * old + rows_of(down_anchor, own + start, size)]
  transfers between devices with their start and end apart: 18 -> 18, of which waited for: 10 -> 9; matrix products, arithmetic and copies ran while one was open for 26% -> 24% of each run, Pallas kernels for 1% -> 1%
where the time goes in v10:
time: 373 us; the launch traced here: 370 us
  waiting for transfers between devices  246 us (66%)
  other arithmetic  46 us (12%)
  starting transfers between devices  30.2 us (8%)
  matrix products  24.1 us (6%)
  local copies, waits for them, and re-layouts  20 us (5%)
    ppermute x12, waiting for transfers between devices, swap(): return lax.ppermute(array, 'group', [(0, 1), (1, 0)])  236 us
    ppermute x12, starting transfers between devices, swap(): return lax.ppermute(array, 'group', [(0, 1), (1, 0)])  25.8 us
    sub x4, other arithmetic, body(): momentum * old + rows_of(down_anchor, own + start, size)  15 us
    dot_general x1, matrix products, rebuild(): lax.dot_general(factors, factor_basis, (((0,), (0,)), ((), ())), precisio...  12.5 us
    add x1, other arithmetic, body(): anchor_next = (1 - rate) * after(down_anchor, parts[0]) + rate / 2 * local  12.1 us
    dot_general x1, matrix products, body(): lax.dot_general(basis, gate_diff, (((1,), (1,)), ((), ())), precision=lax...  11.6 us
    ppermute x6, waiting for transfers between devices, across(): return lax.ppermute(array, 'shard', [(i, i ^ k) for i in range(shards)])  10.1 us
    dynamic_slice x5, local copies, waits for them, and re-layouts, rows_of(): return lax.dynamic_slice_in_dim(array, start, size, 0)  9.61 us
  transfers between devices with their start and end apart: 18, of which 9 were waited for; matrix products, arithmetic and copies ran while one was open for 24% of the time, Pallas kernels for 1%

profile of v10, /device:TPU:10, one launch (start us, length us, event | category | flops | bytes accessed | tf_op | source)
XLA Modules:
  0.0 370.1 jit_solution(2569541778438986238)
XLA Ops:
  1.6 2.7 collective-permute-start
  12.4 11.6 %fusion = f32[64,4096]{1,0:T(8,128)S(1)} fusion(f32[64,512]{1,0:T(8,128)S(1)} %constant_dynamic-update-slice_fusion, f32[4096,512]{1,0:T(8,128)} %param.16, f32[1,4096,512]{2,1,0:T(8,128)} %param.17), kind=kOutput, calls=%fused_computation.1 | convolution fusion | flops 1612709888 | bytes 17956864 | tf_op jit(solution)/shard_map/dot_general | solution.py:153
  24.8 2.7 constant_dynamic-slice_fusion.5
  30.1 2.8 constant_dynamic-slice_fusion.2
  32.9 4.4 %bitcast_subtract_fusion.2 = f32[512,2048]{1,0:T(8,128)S(1)} fusion(f32[512,2048]{1,0:T(8,128)} %param.12, f32[1,1024,2048]{2,1,0:T(8,128)} %param.11, s32[]{:T(128)S(6)} %select_n.93), kind=kLoop, calls=%fused_computation.6 | loop fusion | flops 3145728 | bytes 12582916 | tf_op jit(solution)/shard_map/sub | solution.py:173
  43.0 12.1 %multiply_add_fusion.1 = f32[1024,2048]{1,0:T(8,128)} fusion(f32[1024,2048]{1,0:T(8,128)} %param.10, f32[1,1024,2048]{2,1,0:T(8,128)} %param.11), kind=kLoop, calls=%fused_computation.4 | loop fusion | flops 6291456 | bytes 25165824 | tf_op jit(solution)/shard_map/add | solution.py:174
  60.1 5.5 %collective-permute-done.8 = f32[16,4096]{1,0:T(8,128)S(1)} collective-permute-done((f32[16,4096]{1,0:T(8,128)S(1)}, f32[16,4096]{1,0:T(8,128)S(1)}, u32[]{:S(2)}, u32[]{:S(2)}) %collective-permute-start.8) | collective-permute-done | bytes 262176 | tf_op jit(solution)/shard_map/ppermute | solution.py:39
  67.3 46.6 %collective-permute-done.4 = f32[96,2048]{1,0:T(8,128)} collective-permute-done((f32[96,2048]{1,0:T(8,128)}, f32[96,2048]{1,0:T(8,128)}, u32[]{:S(2)}, u32[]{:S(2)}) %collective-permute-start.4) | collective-permute-done | bytes 786464 | tf_op jit(solution)/shard_map/ppermute | solution.py:34
  113.8 3.4 collective-permute-start.6
  117.2 3.1 fusion.14
  120.4 52.4 %collective-permute-done.1 = f32[192,2048]{1,0:T(8,128)} collective-permute-done((f32[192,2048]{1,0:T(8,128)}, f32[192,2048]{1,0:T(8,128)}, u32[]{:S(2)}, u32[]{:S(2)}) %collective-permute-start.1) | collective-permute-done | bytes 1572896 | tf_op jit(solution)/shard_map/ppermute | solution.py:34
  172.8 3.4 collective-permute-start.2
  176.2 4.8 %fusion.4 = (f32[192,2048]{1,0:T(8,128)S(1)}, f32[1024,2048]{1,0:T(8,128)}) fusion(f32[192,2048]{1,0:T(8,128)} %collective-permute-done.1, f32[1,1024,2048]{2,1,0:T(8,128)} %param.11, s32[]{:T(128)S(6)} %select_n.98, f32[1024,2048]{1,0:T(8,128)} %param.10, f32[512,2048]{1,0:T(8,128)S(1)} %copy-done, f32[1024,2048]{1,0:T(8,128)} %get-tuple-element.45), kind=kLoop, calls=%fused_computation.13 | loop fusion | flops 3538944 | bytes 11010052 | tf_op jit(solution)/shard_map/sub | solution.py:194
  181.0 76.0 %collective-permute-done.10 = f32[8,4096]{1,0:T(8,128)S(1)} collective-permute-done((f32[8,4096]{1,0:T(8,128)S(1)}, f32[8,4096]{1,0:T(8,128)S(1)}, u32[]{:S(2)}, u32[]{:S(2)}) %collective-permute-start.10) | collective-permute-done | bytes 131104 | tf_op jit(solution)/shard_map/ppermute | solution.py:34
  258.6 3.4 collective-permute-start.15
  262.0 5.3 %fusion.2 = (f32[208,2048]{1,0:T(8,128)S(1)}, f32[1024,2048]{1,0:T(8,128)}) fusion(f32[208,2048]{1,0:T(8,128)} %collective-permute-done.5, f32[1,1024,2048]{2,1,0:T(8,128)} %param.11, s32[]{:T(128)S(6)} %select_n.99, f32[1024,2048]{1,0:T(8,128)} %param.10, f32[512,2048]{1,0:T(8,128)S(1)} %copy-done, f32[1024,2048]{1,0:T(8,128)} %get-tuple-element.43), kind=kLoop, calls=%fused_computation.9 | loop fusion | flops 3833856 | bytes 11927556 | tf_op jit(solution)/shard_map/sub | solution.py:194
  270.3 4.6 %collective-permute-done.12 = f32[16,4096]{1,0:T(8,128)S(1)} collective-permute-done((f32[16,4096]{1,0:T(8,128)S(1)}, f32[16,4096]{1,0:T(8,128)S(1)}, u32[]{:S(2)}, u32[]{:S(2)}) %collective-permute-start.12) | collective-permute-done | bytes 262176 | tf_op jit(solution)/shard_map/ppermute | solution.py:39
  278.1 12.5 %multiply_subtract_fusion = (f32[4096,512]{1,0:T(8,128)}, f32[4096,512]{1,0:T(8,128)}) fusion(f32[4096,512]{1,0:T(8,128)S(1)} %bitcast.42, f32[4096,512]{1,0:T(8,128)S(1)} %bitcast.44, f32[64,512]{1,0:T(8,128)S(1)} %constant_dynamic-update-slice_fusion, f32[32,4096]{1,0:T(8,128)S(1)} %collective-permute-done.13, f32[16,4096]{1,0:T(8,128)S(1)} %collective-permute-done.12, ...), kind=kOutput, calls=%fused_computation.2 | convolution fusion | flops 1623982080 | bytes 34734080 | tf_op jit(solution)/shard_map/dot_general | solution.py:28
  291.5 30.3 %collective-permute-done.15 = f32[80,2048]{1,0:T(8,128)} collective-permute-done((f32[80,2048]{1,0:T(8,128)}, f32[80,2048]{1,0:T(8,128)}, u32[]{:S(2)}, u32[]{:S(2)}) %collective-permute-start.15) | collective-permute-done | bytes 655392 | tf_op jit(solution)/shard_map/ppermute | solution.py:34
  321.7 3.4 collective-permute-start.3
  327.5 19.5 %collective-permute-done.14 = f32[80,2048]{1,0:T(8,128)S(1)} collective-permute-done((f32[80,2048]{1,0:T(8,128)S(1)}, f32[80,2048]{1,0:T(8,128)S(1)}, u32[]{:S(2)}, u32[]{:S(2)}) %collective-permute-start.14) | collective-permute-done | bytes 655392 | tf_op jit(solution)/shard_map/ppermute | solution.py:34
  346.9 3.4 collective-permute-start.16
  354.5 9.4 %collective-permute-done.3.part = f32[64,2048]{1,0:T(8,128)S(1)} collective-permute-done((f32[64,2048]{1,0:T(8,128)}, f32[64,2048]{1,0:T(8,128)S(1)}, u32[]{:S(2)}, u32[]{:S(2)}) %collective-permute-start.3) | collective-permute-done | bytes 524320 | tf_op jit(solution)/shard_map/ppermute | solution.py:34
  364.7 2.9 shard_map.145
  (78 shorter events, 43.3 us)
Async XLA Ops:
  1.6 31.4 %collective-permute-start = (f32[16,2048]{1,0:T(8,128)S(1)}, f32[16,2048]{1,0:T(8,128)}, u32[]{:S(2)}, u32[]{:S(2)}) collective-permute-start(f32[16,2048]{1,0:T(8,128)S(1)} %dynamic-slice_bitcast_fusion), channel_id=1, source_target_pairs={{0,16},{16,0},{1,17},{17,1},{2,18},{18,2},{3,19},{19,3},{4,20},{20... | collective-permute-start | bytes 393224 | tf_op jit(solution)/shard_map/ppermute | solution.py:34
  6.3 107.6 %collective-permute-start.4 = (f32[96,2048]{1,0:T(8,128)}, f32[96,2048]{1,0:T(8,128)}, u32[]{:S(2)}, u32[]{:S(2)}) collective-permute-start(f32[96,2048]{1,0:T(8,128)} %constant_dynamic-slice_fusion.6), channel_id=1, source_target_pairs={{0,16},{16,0},{1,17},{17,1},{2,18},{18,2},{3,19},{19,3},{4,20},{20... | collective-permute-start | bytes 2359304 | tf_op jit(solution)/shard_map/ppermute | solution.py:34
  12.4 20.5 %copy-start.3 = (f32[1,2,256]{2,1,0:T(2,128)S(1)}, f32[1,2,256]{2,1,0:T(2,128)}, u32[]{:S(2)}) copy-start(f32[1,2,256]{2,1,0:T(2,128)} %param.14) | copy-start | bytes 6148
  12.4 20.5 %copy-start.4 = (f32[1,256]{1,0:T(1,128)S(1)}, f32[1,256]{1,0:T(1,128)}, u32[]{:S(2)}) copy-start(f32[1,256]{1,0:T(1,128)} %param.15) | copy-start | bytes 3076
  24.8 31.7 %collective-permute-start.7 = (f32[32,4096]{1,0:T(8,128)}, f32[32,4096]{1,0:T(8,128)}, u32[]{:S(2)}, u32[]{:S(2)}) collective-permute-start(f32[32,4096]{1,0:T(8,128)} %slice.69), channel_id=1, source_target_pairs={{0,2},{2,0},{4,6},{6,4},{8,10},{10,8},{12,14},{14,12},{1,3},{3,1},... | collective-permute-start | bytes 1572872 | tf_op jit(solution)/shard_map/ppermute | solution.py:39
  27.5 145.3 %collective-permute-start.1 = (f32[192,2048]{1,0:T(8,128)}, f32[192,2048]{1,0:T(8,128)}, u32[]{:S(2)}, u32[]{:S(2)}) collective-permute-start(f32[192,2048]{1,0:T(8,128)} %constant_dynamic-slice_fusion.5), channel_id=1, source_target_pairs={{0,16},{16,0},{1,17},{17,1},{2,18},{18,2},{3,19},{19,3},{4,20},{20... | collective-permute-start | bytes 4718600 | tf_op jit(solution)/shard_map/ppermute | solution.py:34
  40.1 227.2 %collective-permute-start.17 = (f32[2,256]{1,0:T(2,128)S(1)}, f32[2,256]{1,0:T(2,128)S(1)}, u32[]{:S(2)}, u32[]{:S(2)}) collective-permute-start(f32[2,256]{1,0:T(2,128)S(1)} %subtract_select_fusion), channel_id=1, source_target_pairs={{0,16},{16,0},{1,17},{17,1},{2,18},{18,2},{3,19},{19,3},{4,20},{20... | collective-permute-start | bytes 6152 | tf_op jit(solution)/shard_map/ppermute | solution.py:34
  40.5 216.6 %collective-permute-start.5 = (f32[208,2048]{1,0:T(8,128)}, f32[208,2048]{1,0:T(8,128)}, u32[]{:S(2)}, u32[]{:S(2)}) collective-permute-start(f32[208,2048]{1,0:T(8,128)} %constant_dynamic-slice_fusion.2), channel_id=1, source_target_pairs={{0,16},{16,0},{1,17},{17,1},{2,18},{18,2},{3,19},{19,3},{4,20},{20... | collective-permute-start | bytes 5111816 | tf_op jit(solution)/shard_map/ppermute | solution.py:34
  55.2 62.0 %copy-start = (f32[512,2048]{1,0:T(8,128)S(1)}, f32[512,2048]{1,0:T(8,128)}, u32[]{:S(2)}) copy-start(f32[512,2048]{1,0:T(8,128)} %param.12) | copy-start | bytes 12582916
  57.7 7.9 %collective-permute-start.8 = (f32[16,4096]{1,0:T(8,128)S(1)}, f32[16,4096]{1,0:T(8,128)S(1)}, u32[]{:S(2)}, u32[]{:S(2)}) collective-permute-start(f32[16,4096]{1,0:T(8,128)S(1)} %slice.71), channel_id=1, source_target_pairs={{0,4},{2,6},{4,0},{6,2},{8,12},{10,14},{12,8},{14,10},{1,5},{3,7},... | collective-permute-start | bytes 786440 | tf_op jit(solution)/shard_map/ppermute | solution.py:39
  65.7 54.6 %collective-permute-start.9 = (f32[8,4096]{1,0:T(8,128)S(1)}, f32[8,4096]{1,0:T(8,128)S(1)}, u32[]{:S(2)}, u32[]{:S(2)}) collective-permute-start(f32[8,4096]{1,0:T(8,128)S(1)} %slice.73), channel_id=1, source_target_pairs={{0,8},{2,10},{4,12},{6,14},{8,0},{10,2},{12,4},{14,6},{1,9},{3,11}... | collective-permute-start | bytes 393224 | tf_op jit(solution)/shard_map/ppermute | solution.py:39
  113.8 144.8 %collective-permute-start.6 = (f32[128,2048]{1,0:T(8,128)S(1)}, f32[128,2048]{1,0:T(8,128)S(1)}, u32[]{:S(2)}, u32[]{:S(2)}) collective-permute-start(f32[128,2048]{1,0:T(8,128)S(1)} %get-tuple-element.30), channel_id=1, source_target_pairs={{0,16},{16,0},{1,17},{17,1},{2,18},{18,2},{3,19},{19,3},{4,20},{20... | collective-permute-start | bytes 3145736 | tf_op jit(solution)/shard_map/ppermute | solution.py:34
  120.3 136.7 %collective-permute-start.10 = (f32[8,4096]{1,0:T(8,128)S(1)}, f32[8,4096]{1,0:T(8,128)S(1)}, u32[]{:S(2)}, u32[]{:S(2)}) collective-permute-start(f32[8,4096]{1,0:T(8,128)S(1)} %slice_add_fusion.2), channel_id=1, source_target_pairs={{0,16},{16,0},{1,17},{17,1},{2,18},{18,2},{3,19},{19,3},{4,20},{20... | collective-permute-start | bytes 393224 | tf_op jit(solution)/shard_map/ppermute | solution.py:34
  172.8 148.9 %collective-permute-start.2 = (f32[128,2048]{1,0:T(8,128)S(1)}, f32[128,2048]{1,0:T(8,128)S(1)}, u32[]{:S(2)}, u32[]{:S(2)}) collective-permute-start(f32[128,2048]{1,0:T(8,128)S(1)} %get-tuple-element.25), channel_id=1, source_target_pairs={{0,16},{16,0},{1,17},{17,1},{2,18},{18,2},{3,19},{19,3},{4,20},{20... | collective-permute-start | bytes 3145736 | tf_op jit(solution)/shard_map/ppermute | solution.py:34
  257.0 10.2 %collective-permute-start.11 = (f32[8,4096]{1,0:T(8,128)S(1)}, f32[8,4096]{1,0:T(8,128)S(1)}, u32[]{:S(2)}, u32[]{:S(2)}) collective-permute-start(f32[8,4096]{1,0:T(8,128)S(1)} %add_multiply_fusion), channel_id=1, source_target_pairs={{0,8},{2,10},{4,12},{6,14},{8,0},{10,2},{12,4},{14,6},{1,9},{3,11}... | collective-permute-start | bytes 393224 | tf_op jit(solution)/shard_map/ppermute | solution.py:39
  258.6 63.1 %collective-permute-start.15 = (f32[80,2048]{1,0:T(8,128)}, f32[80,2048]{1,0:T(8,128)}, u32[]{:S(2)}, u32[]{:S(2)}) collective-permute-start(f32[80,2048]{1,0:T(8,128)} %get-tuple-element.33), channel_id=1, source_target_pairs={{0,16},{16,0},{1,17},{17,1},{2,18},{18,2},{3,19},{19,3},{4,20},{20... | collective-permute-start | bytes 1966088 | tf_op jit(solution)/shard_map/ppermute | solution.py:34
  262.0 13.1 %copy-start.5 = (f32[2,256]{1,0:T(2,128)S(1)}, f32[2,256]{1,0:T(2,128)}, u32[]{:S(2)}) copy-start(f32[2,256]{1,0:T(2,128)} %param.13) | copy-start | bytes 6148
  262.0 16.0 %slice-start = ((s8[8388608]{0:T(1024)(128)(4,1)}), s8[4194304]{0:T(1024)(128)(4,1)S(1)}, s32[]{:S(2)}) async-start(s8[8388608]{0:T(1024)(128)(4,1)} %bitcast.41), calls=%async_computation | async-start | bytes 8388608
  262.0 16.0 %slice-start.2 = ((s8[8388608]{0:T(1024)(128)(4,1)}), s8[4194304]{0:T(1024)(128)(4,1)S(1)}, s32[]{:S(2)}) async-start(s8[8388608]{0:T(1024)(128)(4,1)} %bitcast.43), calls=%async_computation.2 | async-start | bytes 8388608
  267.3 7.6 %collective-permute-start.12 = (f32[16,4096]{1,0:T(8,128)S(1)}, f32[16,4096]{1,0:T(8,128)S(1)}, u32[]{:S(2)}, u32[]{:S(2)}) collective-permute-start(f32[16,4096]{1,0:T(8,128)S(1)} %pad_maximum_fusion.2), channel_id=1, source_target_pairs={{0,4},{2,6},{4,0},{6,2},{8,12},{10,14},{12,8},{14,10},{1,5},{3,7},... | collective-permute-start | bytes 786440 | tf_op jit(solution)/shard_map/ppermute | solution.py:39
  275.0 3.0 collective-permute-start.13
  290.6 56.3 %collective-permute-start.14 = (f32[80,2048]{1,0:T(8,128)S(1)}, f32[80,2048]{1,0:T(8,128)S(1)}, u32[]{:S(2)}, u32[]{:S(2)}) collective-permute-start(f32[80,2048]{1,0:T(8,128)S(1)} %copy-done.1), channel_id=1, source_target_pairs={{0,16},{16,0},{1,17},{17,1},{2,18},{18,2},{3,19},{19,3},{4,20},{20... | collective-permute-start | bytes 1966088 | tf_op jit(solution)/shard_map/ppermute | solution.py:34
  321.7 42.1 %collective-permute-start.3 = (f32[64,2048]{1,0:T(8,128)}, f32[64,2048]{1,0:T(8,128)S(1)}, u32[]{:S(2)}, u32[]{:S(2)}) collective-permute-start(f32[64,2048]{1,0:T(8,128)} %slice.64), channel_id=1, source_target_pairs={{0,16},{16,0},{1,17},{17,1},{2,18},{18,2},{3,19},{19,3},{4,20},{20... | collective-permute-start | bytes 1572872 | tf_op jit(solution)/shard_map/ppermute | solution.py:34
  346.9 22.5 %collective-permute-start.16 = (f32[32,2048]{1,0:T(8,128)}, f32[32,2048]{1,0:T(8,128)S(1)}, u32[]{:S(2)}, u32[]{:S(2)}) collective-permute-start(f32[32,2048]{1,0:T(8,128)} %slice.75), channel_id=1, source_target_pairs={{0,16},{16,0},{1,17},{17,1},{2,18},{18,2},{3,19},{19,3},{4,20},{20... | collective-permute-start | bytes 786440 | tf_op jit(solution)/shard_map/ppermute | solution.py:34
  (4 other events, 33.6 us)

commit v11 on v10

--- a/solution.py
+++ b/solution.py
@@ -165,6 +165,8 @@
                 cut = after(local, part)
         else:
             part = mixed[start : start + size]
+        if i == len(spans) + len(mixed_spans) - 1:
+            part = settled[start - settled_from :]
         ties = [parts[i - window]] if i >= window else []
         if i == gate_before:
             ties += gate
@@ -176,6 +178,9 @@
             norm_received = swap(norm_sent)
         if i == len(spans) - 1:
             norm_received = after(norm_received, parts[i])
+            settled_from = start
+            settled = rows_of(anchor_next, own + start, size)
+            settled += (rate / 2) * parts[i] - decay * down_moment[start:]
             factor_piece = (factor_piece + after(factor_other, parts[i])) / groups
             factors = gather_factors(factor_piece, bits)
             gate = advance(gate_anchor, gate_moment, rebuild(factors, basis))
@@ -185,8 +190,6 @@
         norm_anchor, norm_local[0], norm_moment, norm_received
     )
 
-    start, size = mixed_spans[-1]
-    last_base = after(rows_of(anchor_next, other + start, size), parts[-3])
     moment_next = []
     for (start, size), part in zip(spans, received):
         old = down_moment[start : start + size]
@@ -201,8 +204,9 @@
         if i == pinned:
             anchor_next = add_rows(anchor_next, part, start, half)
         else:
-            value = last_base if i == len(mixed_spans) - 1 else rows_of(anchor_next, other + start, size)
-            value = value + part
+            value = part
+            if i < len(mixed_spans) - 1:
+                value = value + rows_of(anchor_next, other + start, size)
             anchor_next = lax.dynamic_update_slice_in_dim(anchor_next, value, other + start, 0)
     return (
         anchor_next,

time: 373 us -> 373 us (level)
  waiting for transfers between devices: 246 us -> 239 us
  local copies, waits for them, and re-layouts: 20 us -> 26.9 us
    unnamed x27 -> x28, local copies, waits for them, and re-layouts: 5.86 us -> 13.9 us
    ppermute x12, waiting for transfers between devices: 236 us -> 229 us  [swap(): return lax.ppermute(array, 'group', [(0, 1), (1, 0)])]
    sub x4 -> x3, other arithmetic: 15 us -> 9.7 us  [body(): momentum * old + rows_of(down_anchor, own + start, size)]
    dynamic_update_slice x0 -> x1, other arithmetic: none -> 5.25 us  [body(): lax.dynamic_update_slice_in_dim(anchor_next, value, own + start, 0)]
    dynamic_slice x5 -> x4, local copies, waits for them, and re-layouts: 9.61 us -> 8.5 us  [rows_of(): return lax.dynamic_slice_in_dim(array, start, size, 0)]
    dynamic_update_slice x5 -> x4, other arithmetic: 9.58 us -> 8.86 us  [body(): lax.dynamic_update_slice_in_dim(anchor_next, value, other + start, 0)]
  transfers between devices with their start and end apart: 18 -> 18, of which waited for: 9 -> 10; matrix products, arithmetic and copies ran while one was open for 24% -> 26% of each run, Pallas kernels for 1% -> 1%
where the time goes in v11:
time: 373 us; the launch traced here: 370 us
  waiting for transfers between devices  239 us (64%)
  other arithmetic  46.2 us (12%)
  starting transfers between devices  30.1 us (8%)
  local copies, waits for them, and re-layouts  26.9 us (7%)
  matrix products  24.1 us (6%)
    ppermute x12, waiting for transfers between devices, swap(): return lax.ppermute(array, 'group', [(0, 1), (1, 0)])  229 us
    ppermute x12, starting transfers between devices, swap(): return lax.ppermute(array, 'group', [(0, 1), (1, 0)])  25.7 us
    unnamed x28, local copies, waits for them, and re-layouts  13.9 us
    dot_general x1, matrix products, rebuild(): lax.dot_general(factors, factor_basis, (((0,), (0,)), ((), ())), precisio...  12.5 us
    add x1, other arithmetic, body(): anchor_next = (1 - rate) * after(down_anchor, parts[0]) + rate / 2 * local  12.1 us
    dot_general x1, matrix products, body(): lax.dot_general(basis, gate_diff, (((1,), (1,)), ((), ())), precision=lax...  11.6 us
    ppermute x6, waiting for transfers between devices, across(): return lax.ppermute(array, 'shard', [(i, i ^ k) for i in range(shards)])  10.4 us
    sub x3, other arithmetic, body(): momentum * old + rows_of(down_anchor, own + start, size)  9.7 us
  transfers between devices with their start and end apart: 18, of which 10 were waited for; matrix products, arithmetic and copies ran while one was open for 26% of the time, Pallas kernels for 1%

profile of v11, /device:TPU:10, one launch (start us, length us, event | category | flops | bytes accessed | tf_op | source)
XLA Modules:
  0.0 370.0 jit_solution(17379896453886834744)
XLA Ops:
  12.4 11.6 %fusion = f32[64,4096]{1,0:T(8,128)S(1)} fusion(f32[64,512]{1,0:T(8,128)S(1)} %constant_dynamic-update-slice_fusion, f32[4096,512]{1,0:T(8,128)} %param.16, f32[1,4096,512]{2,1,0:T(8,128)} %param.17), kind=kOutput, calls=%fused_computation.1 | convolution fusion | flops 1612709888 | bytes 17956864 | tf_op jit(solution)/shard_map/dot_general | solution.py:153
  30.1 2.8 constant_dynamic-slice_fusion.2
  32.9 4.4 %bitcast_subtract_fusion.2 = f32[512,2048]{1,0:T(8,128)S(1)} fusion(f32[512,2048]{1,0:T(8,128)} %param.12, f32[1,1024,2048]{2,1,0:T(8,128)} %param.11, s32[]{:T(128)S(6)} %select_n.93), kind=kLoop, calls=%fused_computation.6 | loop fusion | flops 3145728 | bytes 12582916 | tf_op jit(solution)/shard_map/sub | solution.py:175
  42.3 12.1 %multiply_add_fusion.1 = f32[1024,2048]{1,0:T(8,128)} fusion(f32[1024,2048]{1,0:T(8,128)} %param.10, f32[1,1024,2048]{2,1,0:T(8,128)} %param.11), kind=kLoop, calls=%fused_computation.4 | loop fusion | flops 6291456 | bytes 25165824 | tf_op jit(solution)/shard_map/add | solution.py:176
  54.4 8.0 %copy.17 = f32[1024,2048]{1,0:T(8,128)} copy(f32[1024,2048]{1,0:T(8,128)} %multiply_add_fusion.1) | data formatting | bytes 16777216
  66.2 5.6 %collective-permute-done.8 = f32[16,4096]{1,0:T(8,128)S(1)} collective-permute-done((f32[16,4096]{1,0:T(8,128)S(1)}, f32[16,4096]{1,0:T(8,128)S(1)}, u32[]{:S(2)}, u32[]{:S(2)}) %collective-permute-start.8) | collective-permute-done | bytes 262176 | tf_op jit(solution)/shard_map/ppermute | solution.py:39
  73.4 40.4 %collective-permute-done.4 = f32[96,2048]{1,0:T(8,128)} collective-permute-done((f32[96,2048]{1,0:T(8,128)}, f32[96,2048]{1,0:T(8,128)}, u32[]{:S(2)}, u32[]{:S(2)}) %collective-permute-start.4) | collective-permute-done | bytes 786464 | tf_op jit(solution)/shard_map/ppermute | solution.py:34
  113.8 3.4 collective-permute-start.6
  117.2 3.1 fusion.14
  120.5 52.4 %collective-permute-done.1 = f32[192,2048]{1,0:T(8,128)} collective-permute-done((f32[192,2048]{1,0:T(8,128)}, f32[192,2048]{1,0:T(8,128)}, u32[]{:S(2)}, u32[]{:S(2)}) %collective-permute-start.1) | collective-permute-done | bytes 1572896 | tf_op jit(solution)/shard_map/ppermute | solution.py:34
  172.8 3.4 collective-permute-start.2
  176.2 4.8 %fusion.4 = (f32[192,2048]{1,0:T(8,128)S(1)}, f32[1024,2048]{1,0:T(8,128)}) fusion(f32[192,2048]{1,0:T(8,128)} %collective-permute-done.1, f32[1,1024,2048]{2,1,0:T(8,128)} %param.11, s32[]{:T(128)S(6)} %select_n.98, f32[1024,2048]{1,0:T(8,128)} %param.10, f32[512,2048]{1,0:T(8,128)S(1)} %copy-done, f32[1024,2048]{1,0:T(8,128)} %get-tuple-element.44), kind=kLoop, calls=%fused_computation.14 | loop fusion | flops 3538944 | bytes 11010052 | tf_op jit(solution)/shard_map/sub | solution.py:197
  181.0 50.8 %collective-permute-done.5 = f32[208,2048]{1,0:T(8,128)} collective-permute-done((f32[208,2048]{1,0:T(8,128)}, f32[208,2048]{1,0:T(8,128)}, u32[]{:S(2)}, u32[]{:S(2)}) %collective-permute-start.5) | collective-permute-done | bytes 1703968 | tf_op jit(solution)/shard_map/ppermute | solution.py:34
  231.9 25.2 %collective-permute-done.10 = f32[8,4096]{1,0:T(8,128)S(1)} collective-permute-done((f32[8,4096]{1,0:T(8,128)S(1)}, f32[8,4096]{1,0:T(8,128)S(1)}, u32[]{:S(2)}, u32[]{:S(2)}) %collective-permute-start.10) | collective-permute-done | bytes 131104 | tf_op jit(solution)/shard_map/ppermute | solution.py:34
  258.6 3.4 collective-permute-start.15
  262.0 5.2 %add_dynamic-update-slice_fusion = (f32[1024,2048]{1,0:T(8,128)}, f32[208,2048]{1,0:T(8,128)S(1)}, f32[208,2048]{1,0:T(8,128)S(1)}) fusion(f32[1024,2048]{1,0:T(8,128)} %get-tuple-element.42, s32[]{:T(128)S(6)} %select_n.99, f32[512,2048]{1,0:T(8,128)S(1)} %copy-done, f32[208,2048]{1,0:T(8,128)} %collective-permute-done.5, f32[1,1024,2048]{2,1,0:T(8,128)} %param.11, ...), kind=kLoop, calls=%fused_computation.10 | loop fusion | flops 3833856 | bytes 13631492 | tf_op jit(solution)/shard_map/dynamic_update_slice | solution.py:202
  271.3 4.8 %collective-permute-done.12 = f32[16,4096]{1,0:T(8,128)S(1)} collective-permute-done((f32[16,4096]{1,0:T(8,128)S(1)}, f32[16,4096]{1,0:T(8,128)S(1)}, u32[]{:S(2)}, u32[]{:S(2)}) %collective-permute-start.12) | collective-permute-done | bytes 262176 | tf_op jit(solution)/shard_map/ppermute | solution.py:39
  279.2 12.5 %multiply_subtract_fusion = (f32[4096,512]{1,0:T(8,128)}, f32[4096,512]{1,0:T(8,128)}) fusion(f32[4096,512]{1,0:T(8,128)S(1)} %bitcast.42, f32[4096,512]{1,0:T(8,128)S(1)} %bitcast.44, f32[64,512]{1,0:T(8,128)S(1)} %constant_dynamic-update-slice_fusion, f32[32,4096]{1,0:T(8,128)S(1)} %collective-permute-done.13, f32[16,4096]{1,0:T(8,128)S(1)} %collective-permute-done.12, ...), kind=kOutput, calls=%fused_computation.2 | convolution fusion | flops 1623982080 | bytes 34734080 | tf_op jit(solution)/shard_map/dot_general | solution.py:28
  292.6 26.2 %collective-permute-done.2 = f32[128,2048]{1,0:T(8,128)S(1)} collective-permute-done((f32[128,2048]{1,0:T(8,128)S(1)}, f32[128,2048]{1,0:T(8,128)S(1)}, u32[]{:S(2)}, u32[]{:S(2)}) %collective-permute-start.2) | collective-permute-done | bytes 1048608 | tf_op jit(solution)/shard_map/ppermute | solution.py:34
  318.8 3.4 collective-permute-start.3
  324.5 22.5 %collective-permute-done.14 = f32[80,2048]{1,0:T(8,128)S(1)} collective-permute-done((f32[80,2048]{1,0:T(8,128)}, f32[80,2048]{1,0:T(8,128)S(1)}, u32[]{:S(2)}, u32[]{:S(2)}) %collective-permute-start.14) | collective-permute-done | bytes 655392 | tf_op jit(solution)/shard_map/ppermute | solution.py:34
  347.0 3.3 collective-permute-start.16
  354.5 9.4 %collective-permute-done.3.part = f32[64,2048]{1,0:T(8,128)S(1)} collective-permute-done((f32[64,2048]{1,0:T(8,128)}, f32[64,2048]{1,0:T(8,128)S(1)}, u32[]{:S(2)}, u32[]{:S(2)}) %collective-permute-start.3) | collective-permute-done | bytes 524320 | tf_op jit(solution)/shard_map/ppermute | solution.py:34
  364.7 2.9 shard_map.145
  (78 shorter events, 47.6 us)
Async XLA Ops:
  1.6 31.4 %collective-permute-start = (f32[16,2048]{1,0:T(8,128)S(1)}, f32[16,2048]{1,0:T(8,128)S(1)}, u32[]{:S(2)}, u32[]{:S(2)}) collective-permute-start(f32[16,2048]{1,0:T(8,128)S(1)} %dynamic-slice_bitcast_fusion), channel_id=1, source_target_pairs={{0,16},{16,0},{1,17},{17,1},{2,18},{18,2},{3,19},{19,3},{4,20},{20... | collective-permute-start | bytes 393224 | tf_op jit(solution)/shard_map/ppermute | solution.py:34
  6.3 107.6 %collective-permute-start.4 = (f32[96,2048]{1,0:T(8,128)}, f32[96,2048]{1,0:T(8,128)}, u32[]{:S(2)}, u32[]{:S(2)}) collective-permute-start(f32[96,2048]{1,0:T(8,128)} %constant_dynamic-slice_fusion.5), channel_id=1, source_target_pairs={{0,16},{16,0},{1,17},{17,1},{2,18},{18,2},{3,19},{19,3},{4,20},{20... | collective-permute-start | bytes 2359304 | tf_op jit(solution)/shard_map/ppermute | solution.py:34
  12.4 20.5 %copy-start.3 = (f32[1,2,256]{2,1,0:T(2,128)S(1)}, f32[1,2,256]{2,1,0:T(2,128)}, u32[]{:S(2)}) copy-start(f32[1,2,256]{2,1,0:T(2,128)} %param.14) | copy-start | bytes 6148
  12.4 20.5 %copy-start.4 = (f32[1,256]{1,0:T(1,128)S(1)}, f32[1,256]{1,0:T(1,128)}, u32[]{:S(2)}) copy-start(f32[1,256]{1,0:T(1,128)} %param.15) | copy-start | bytes 3076
  24.8 37.9 %collective-permute-start.7 = (f32[32,4096]{1,0:T(8,128)}, f32[32,4096]{1,0:T(8,128)}, u32[]{:S(2)}, u32[]{:S(2)}) collective-permute-start(f32[32,4096]{1,0:T(8,128)} %slice.70), channel_id=1, source_target_pairs={{0,2},{2,0},{4,6},{6,4},{8,10},{10,8},{12,14},{14,12},{1,3},{3,1},... | collective-permute-start | bytes 1572872 | tf_op jit(solution)/shard_map/ppermute | solution.py:39
  27.5 145.3 %collective-permute-start.1 = (f32[192,2048]{1,0:T(8,128)}, f32[192,2048]{1,0:T(8,128)}, u32[]{:S(2)}, u32[]{:S(2)}) collective-permute-start(f32[192,2048]{1,0:T(8,128)} %constant_dynamic-slice_fusion.4), channel_id=1, source_target_pairs={{0,16},{16,0},{1,17},{17,1},{2,18},{18,2},{3,19},{19,3},{4,20},{20... | collective-permute-start | bytes 4718600 | tf_op jit(solution)/shard_map/ppermute | solution.py:34
  39.4 141.6 %collective-permute-start.17 = (f32[2,256]{1,0:T(2,128)S(1)}, f32[2,256]{1,0:T(2,128)S(1)}, u32[]{:S(2)}, u32[]{:S(2)}) collective-permute-start(f32[2,256]{1,0:T(2,128)S(1)} %subtract_select_fusion), channel_id=1, source_target_pairs={{0,16},{16,0},{1,17},{17,1},{2,18},{18,2},{3,19},{19,3},{4,20},{20... | collective-permute-start | bytes 6152 | tf_op jit(solution)/shard_map/ppermute | solution.py:34
  39.7 192.1 %collective-permute-start.5 = (f32[208,2048]{1,0:T(8,128)}, f32[208,2048]{1,0:T(8,128)}, u32[]{:S(2)}, u32[]{:S(2)}) collective-permute-start(f32[208,2048]{1,0:T(8,128)} %constant_dynamic-slice_fusion.2), channel_id=1, source_target_pairs={{0,16},{16,0},{1,17},{17,1},{2,18},{18,2},{3,19},{19,3},{4,20},{20... | collective-permute-start | bytes 5111816 | tf_op jit(solution)/shard_map/ppermute | solution.py:34
  63.8 7.9 %collective-permute-start.8 = (f32[16,4096]{1,0:T(8,128)S(1)}, f32[16,4096]{1,0:T(8,128)S(1)}, u32[]{:S(2)}, u32[]{:S(2)}) collective-permute-start(f32[16,4096]{1,0:T(8,128)S(1)} %slice.72), channel_id=1, source_target_pairs={{0,4},{2,6},{4,0},{6,2},{8,12},{10,14},{12,8},{14,10},{1,5},{3,7},... | collective-permute-start | bytes 786440 | tf_op jit(solution)/shard_map/ppermute | solution.py:39
  71.8 48.5 %collective-permute-start.9 = (f32[8,4096]{1,0:T(8,128)S(1)}, f32[8,4096]{1,0:T(8,128)S(1)}, u32[]{:S(2)}, u32[]{:S(2)}) collective-permute-start(f32[8,4096]{1,0:T(8,128)S(1)} %slice.74), channel_id=1, source_target_pairs={{0,8},{2,10},{4,12},{6,14},{8,0},{10,2},{12,4},{14,6},{1,9},{3,11}... | collective-permute-start | bytes 393224 | tf_op jit(solution)/shard_map/ppermute | solution.py:39
  113.8 144.8 %collective-permute-start.6 = (f32[128,2048]{1,0:T(8,128)S(1)}, f32[128,2048]{1,0:T(8,128)S(1)}, u32[]{:S(2)}, u32[]{:S(2)}) collective-permute-start(f32[128,2048]{1,0:T(8,128)S(1)} %get-tuple-element.29), channel_id=1, source_target_pairs={{0,16},{16,0},{1,17},{17,1},{2,18},{18,2},{3,19},{19,3},{4,20},{20... | collective-permute-start | bytes 3145736 | tf_op jit(solution)/shard_map/ppermute | solution.py:34
  117.2 141.4 %copy-start.1 = (f32[80,2048]{1,0:T(8,128)S(1)}, f32[80,2048]{1,0:T(8,128)}, u32[]{:S(2)}) copy-start(f32[80,2048]{1,0:T(8,128)} %get-tuple-element.32) | copy-start | bytes 1966084
  120.4 136.6 %collective-permute-start.10 = (f32[8,4096]{1,0:T(8,128)S(1)}, f32[8,4096]{1,0:T(8,128)S(1)}, u32[]{:S(2)}, u32[]{:S(2)}) collective-permute-start(f32[8,4096]{1,0:T(8,128)S(1)} %slice_add_fusion.3), channel_id=1, source_target_pairs={{0,16},{16,0},{1,17},{17,1},{2,18},{18,2},{3,19},{19,3},{4,20},{20... | collective-permute-start | bytes 393224 | tf_op jit(solution)/shard_map/ppermute | solution.py:34
  172.8 146.0 %collective-permute-start.2 = (f32[128,2048]{1,0:T(8,128)S(1)}, f32[128,2048]{1,0:T(8,128)S(1)}, u32[]{:S(2)}, u32[]{:S(2)}) collective-permute-start(f32[128,2048]{1,0:T(8,128)S(1)} %get-tuple-element.24), channel_id=1, source_target_pairs={{0,16},{16,0},{1,17},{17,1},{2,18},{18,2},{3,19},{19,3},{4,20},{20... | collective-permute-start | bytes 3145736 | tf_op jit(solution)/shard_map/ppermute | solution.py:34
  257.0 11.4 %collective-permute-start.11 = (f32[8,4096]{1,0:T(8,128)S(1)}, f32[8,4096]{1,0:T(8,128)S(1)}, u32[]{:S(2)}, u32[]{:S(2)}) collective-permute-start(f32[8,4096]{1,0:T(8,128)S(1)} %add_multiply_fusion), channel_id=1, source_target_pairs={{0,8},{2,10},{4,12},{6,14},{8,0},{10,2},{12,4},{14,6},{1,9},{3,11}... | collective-permute-start | bytes 393224 | tf_op jit(solution)/shard_map/ppermute | solution.py:39
  258.6 93.6 %collective-permute-start.15 = (f32[80,2048]{1,0:T(8,128)S(1)}, f32[80,2048]{1,0:T(8,128)}, u32[]{:S(2)}, u32[]{:S(2)}) collective-permute-start(f32[80,2048]{1,0:T(8,128)S(1)} %copy-done.1), channel_id=1, source_target_pairs={{0,16},{16,0},{1,17},{17,1},{2,18},{18,2},{3,19},{19,3},{4,20},{20... | collective-permute-start | bytes 1966088 | tf_op jit(solution)/shard_map/ppermute | solution.py:34
  262.0 17.1 %slice-start = ((s8[8388608]{0:T(1024)(128)(4,1)}), s8[4194304]{0:T(1024)(128)(4,1)S(1)}, s32[]{:S(2)}) async-start(s8[8388608]{0:T(1024)(128)(4,1)} %bitcast.41), calls=%async_computation | async-start | bytes 8388608
  262.0 17.1 %slice-start.2 = ((s8[8388608]{0:T(1024)(128)(4,1)}), s8[4194304]{0:T(1024)(128)(4,1)S(1)}, s32[]{:S(2)}) async-start(s8[8388608]{0:T(1024)(128)(4,1)} %bitcast.43), calls=%async_computation.2 | async-start | bytes 8388608
  267.3 11.9 %slice-start.3 = ((s8[8388608]{0:T(1024)(128)(4,1)}), s8[4194304]{0:T(1024)(128)(4,1)S(1)}, s32[]{:S(2)}) async-start(s8[8388608]{0:T(1024)(128)(4,1)} %bitcast.43), calls=%async_computation.3 | async-start | bytes 8388608
  268.5 7.6 %collective-permute-start.12 = (f32[16,4096]{1,0:T(8,128)S(1)}, f32[16,4096]{1,0:T(8,128)S(1)}, u32[]{:S(2)}, u32[]{:S(2)}) collective-permute-start(f32[16,4096]{1,0:T(8,128)S(1)} %pad_maximum_fusion.2), channel_id=1, source_target_pairs={{0,4},{2,6},{4,0},{6,2},{8,12},{10,14},{12,8},{14,10},{1,5},{3,7},... | collective-permute-start | bytes 786440 | tf_op jit(solution)/shard_map/ppermute | solution.py:39
  276.1 3.0 collective-permute-start.13
  291.7 55.3 %collective-permute-start.14 = (f32[80,2048]{1,0:T(8,128)}, f32[80,2048]{1,0:T(8,128)S(1)}, u32[]{:S(2)}, u32[]{:S(2)}) collective-permute-start(f32[80,2048]{1,0:T(8,128)} %get-tuple-element.31), channel_id=1, source_target_pairs={{0,16},{16,0},{1,17},{17,1},{2,18},{18,2},{3,19},{19,3},{4,20},{20... | collective-permute-start | bytes 1966088 | tf_op jit(solution)/shard_map/ppermute | solution.py:34
  318.8 45.0 %collective-permute-start.3 = (f32[64,2048]{1,0:T(8,128)}, f32[64,2048]{1,0:T(8,128)S(1)}, u32[]{:S(2)}, u32[]{:S(2)}) collective-permute-start(f32[64,2048]{1,0:T(8,128)} %slice.65), channel_id=1, source_target_pairs={{0,16},{16,0},{1,17},{17,1},{2,18},{18,2},{3,19},{19,3},{4,20},{20... | collective-permute-start | bytes 1572872 | tf_op jit(solution)/shard_map/ppermute | solution.py:34
  347.0 22.3 %collective-permute-start.16 = (f32[32,2048]{1,0:T(8,128)S(1)}, f32[32,2048]{1,0:T(8,128)S(1)}, u32[]{:S(2)}, u32[]{:S(2)}) collective-permute-start(f32[32,2048]{1,0:T(8,128)S(1)} %slice_add_fusion.1), channel_id=1, source_target_pairs={{0,16},{16,0},{1,17},{17,1},{2,18},{18,2},{3,19},{19,3},{4,20},{20... | collective-permute-start | bytes 786440 | tf_op jit(solution)/shard_map/ppermute | solution.py:34
  (4 other events, 31.7 us)

commit v12 on v11

--- a/solution.py
+++ b/solution.py
@@ -93,6 +93,14 @@
     return value
 
 
+def rows_of(array, start, size):
+    return lax.dynamic_slice_in_dim(array, start, size, allow_negative_indices=False)
+
+
+def put_rows(array, rows, start):
+    return lax.dynamic_update_slice_in_dim(array, rows, start, 0, allow_negative_indices=False)
+
+
 def mine_of(shape, half):
     return lax.broadcasted_iota(jnp.int32, shape, 0) // half == lax.axis_index("group")
 
@@ -111,7 +119,7 @@
     anchor_next += jnp.where(mine, (rate / 2) * received - decay * wide, received)
     step = anchor - 0.5 * (local + received)
     own = lax.axis_index("group") * half
-    return anchor_next, momentum * moment + lax.dynamic_slice_in_dim(step, own, half, 0)
+    return anchor_next, momentum * moment + rows_of(step, own, half)
 
 
 def body(
@@ -132,9 +140,6 @@
     half = down_moment.shape[0]
     own = group_index * half
     other = half - own
-
-    def rows_of(array, start, size):
-        return lax.dynamic_slice_in_dim(array, start, size, 0)
 
     spans = list(pieces(half, first_sizes))
     mixed_spans = list(pieces(half, last_sizes))
@@ -199,7 +204,7 @@
             - 0.5 * (rows_of(local, own + start, size) + part)
         )
         value = rows_of(anchor_next, own + start, size) + ((rate / 2) * part - decay * old)
-        anchor_next = lax.dynamic_update_slice_in_dim(anchor_next, value, own + start, 0)
+        anchor_next = put_rows(anchor_next, value, own + start)
     for i, ((start, size), part) in enumerate(zip(mixed_spans, mixed_received)):
         if i == pinned:
             anchor_next = add_rows(anchor_next, part, start, half)
@@ -207,7 +212,7 @@
             value = part
             if i < len(mixed_spans) - 1:
                 value = value + rows_of(anchor_next, other + start, size)
-            anchor_next = lax.dynamic_update_slice_in_dim(anchor_next, value, other + start, 0)
+            anchor_next = put_rows(anchor_next, value, other + start)
     return (
         anchor_next,
         lax.concatenate(moment_next, 0),

time: 373 us -> 373 us (level)
  transfers between devices with their start and end apart: 18 -> 18, of which waited for: 10 -> 9; matrix products, arithmetic and copies ran while one was open for 26% -> 26% of each run, Pallas kernels for 1% -> 1%
where the time goes in v12:
time: 373 us; the launch traced here: 370 us
  waiting for transfers between devices  239 us (64%)
  other arithmetic  46.1 us (12%)
  starting transfers between devices  30.2 us (8%)
  local copies, waits for them, and re-layouts  26.9 us (7%)
  matrix products  24.1 us (6%)
    ppermute x12, waiting for transfers between devices, swap(): return lax.ppermute(array, 'group', [(0, 1), (1, 0)])  229 us
    ppermute x12, starting transfers between devices, swap(): return lax.ppermute(array, 'group', [(0, 1), (1, 0)])  25.7 us
    dynamic_update_slice x5, other arithmetic, put_rows(): lax.dynamic_update_slice_in_dim(array, rows, start, 0, allow_negative_ind...  14.1 us
    unnamed x28, local copies, waits for them, and re-layouts  13.9 us
    dot_general x1, matrix products, rebuild(): lax.dot_general(factors, factor_basis, (((0,), (0,)), ((), ())), precisio...  12.5 us
    add x1, other arithmetic, body(): anchor_next = (1 - rate) * after(down_anchor, parts[0]) + rate / 2 * local  12.1 us
    dot_general x1, matrix products, body(): lax.dot_general(basis, gate_diff, (((1,), (1,)), ((), ())), precision=lax...  11.6 us
    ppermute x6, waiting for transfers between devices, across(): return lax.ppermute(array, 'shard', [(i, i ^ k) for i in range(shards)])  10.4 us
  transfers between devices with their start and end apart: 18, of which 9 were waited for; matrix products, arithmetic and copies ran while one was open for 26% of the time, Pallas kernels for 1%

profile of v12, /device:TPU:10, one launch (start us, length us, event | category | flops | bytes accessed | tf_op | source)
XLA Modules:
  0.0 370.0 jit_solution(9938320676296697503)
XLA Ops:
  12.4 11.6 %fusion = f32[64,4096]{1,0:T(8,128)S(1)} fusion(f32[64,512]{1,0:T(8,128)S(1)} %constant_dynamic-update-slice_fusion, f32[4096,512]{1,0:T(8,128)} %param.16, f32[1,4096,512]{2,1,0:T(8,128)} %param.17), kind=kOutput, calls=%fused_computation.1 | convolution fusion | flops 1612709888 | bytes 17956864 | tf_op jit(solution)/shard_map/dot_general | solution.py:158
  24.8 2.7 constant_dynamic-slice_fusion.4
  30.1 2.8 constant_dynamic-slice_fusion.3
  32.9 4.4 %bitcast_subtract_fusion.2 = f32[512,2048]{1,0:T(8,128)S(1)} fusion(f32[512,2048]{1,0:T(8,128)} %param.12, f32[1,1024,2048]{2,1,0:T(8,128)} %param.11, s32[]{:T(128)S(6)} %mul.187), kind=kLoop, calls=%fused_computation.6 | loop fusion | flops 3145728 | bytes 12582916 | tf_op jit(solution)/shard_map/sub | solution.py:180
  42.3 12.1 %multiply_add_fusion.1 = f32[1024,2048]{1,0:T(8,128)} fusion(f32[1024,2048]{1,0:T(8,128)} %param.10, f32[1,1024,2048]{2,1,0:T(8,128)} %param.11), kind=kLoop, calls=%fused_computation.4 | loop fusion | flops 6291456 | bytes 25165824 | tf_op jit(solution)/shard_map/add | solution.py:181
  54.4 8.0 %copy.17 = f32[1024,2048]{1,0:T(8,128)} copy(f32[1024,2048]{1,0:T(8,128)} %multiply_add_fusion.1) | data formatting | bytes 16777216
  66.2 5.6 %collective-permute-done.8 = f32[16,4096]{1,0:T(8,128)S(1)} collective-permute-done((f32[16,4096]{1,0:T(8,128)S(1)}, f32[16,4096]{1,0:T(8,128)S(1)}, u32[]{:S(2)}, u32[]{:S(2)}) %collective-permute-start.8) | collective-permute-done | bytes 262176 | tf_op jit(solution)/shard_map/ppermute | solution.py:39
  73.4 40.4 %collective-permute-done.4 = f32[96,2048]{1,0:T(8,128)} collective-permute-done((f32[96,2048]{1,0:T(8,128)}, f32[96,2048]{1,0:T(8,128)}, u32[]{:S(2)}, u32[]{:S(2)}) %collective-permute-start.4) | collective-permute-done | bytes 786464 | tf_op jit(solution)/shard_map/ppermute | solution.py:34
  113.8 3.4 collective-permute-start.6
  117.2 3.1 fusion.14
  120.4 52.4 %collective-permute-done.1 = f32[192,2048]{1,0:T(8,128)} collective-permute-done((f32[192,2048]{1,0:T(8,128)}, f32[192,2048]{1,0:T(8,128)}, u32[]{:S(2)}, u32[]{:S(2)}) %collective-permute-start.1) | collective-permute-done | bytes 1572896 | tf_op jit(solution)/shard_map/ppermute | solution.py:34
  172.8 3.4 collective-permute-start.2
  176.2 4.8 %fusion.4 = (f32[192,2048]{1,0:T(8,128)S(1)}, f32[1024,2048]{1,0:T(8,128)}) fusion(f32[192,2048]{1,0:T(8,128)} %collective-permute-done.1, f32[1,1024,2048]{2,1,0:T(8,128)} %param.11, s32[]{:T(128)S(6)} %add.142, f32[1024,2048]{1,0:T(8,128)} %param.10, f32[512,2048]{1,0:T(8,128)S(1)} %copy-done, f32[1024,2048]{1,0:T(8,128)} %get-tuple-element.44), kind=kLoop, calls=%fused_computation.14 | loop fusion | flops 3538944 | bytes 11010052 | tf_op jit(solution)/shard_map/sub | solution.py:202
  181.0 76.0 %collective-permute-done.10 = f32[8,4096]{1,0:T(8,128)S(1)} collective-permute-done((f32[8,4096]{1,0:T(8,128)S(1)}, f32[8,4096]{1,0:T(8,128)S(1)}, u32[]{:S(2)}, u32[]{:S(2)}) %collective-permute-start.10) | collective-permute-done | bytes 131104 | tf_op jit(solution)/shard_map/ppermute | solution.py:34
  258.6 5.2 %add_dynamic-update-slice_fusion = (f32[1024,2048]{1,0:T(8,128)}, f32[208,2048]{1,0:T(8,128)S(1)}, f32[208,2048]{1,0:T(8,128)S(1)}) fusion(f32[1024,2048]{1,0:T(8,128)} %get-tuple-element.42, s32[]{:T(128)S(6)} %add.144, f32[512,2048]{1,0:T(8,128)S(1)} %copy-done, f32[208,2048]{1,0:T(8,128)} %collective-permute-done.5, f32[1,1024,2048]{2,1,0:T(8,128)} %param.11, ...), kind=kLoop, calls=%fused_computation.10 | loop fusion | flops 3833856 | bytes 13631492 | tf_op jit(solution)/shard_map/dynamic_update_slice | solution.py:101
  265.1 3.4 collective-permute-start.15
  271.4 4.8 %collective-permute-done.12 = f32[16,4096]{1,0:T(8,128)S(1)} collective-permute-done((f32[16,4096]{1,0:T(8,128)S(1)}, f32[16,4096]{1,0:T(8,128)S(1)}, u32[]{:S(2)}, u32[]{:S(2)}) %collective-permute-start.12) | collective-permute-done | bytes 262176 | tf_op jit(solution)/shard_map/ppermute | solution.py:39
  279.3 12.5 %multiply_subtract_fusion = (f32[4096,512]{1,0:T(8,128)}, f32[4096,512]{1,0:T(8,128)}) fusion(f32[4096,512]{1,0:T(8,128)S(1)} %bitcast.42, f32[4096,512]{1,0:T(8,128)S(1)} %bitcast.44, f32[64,512]{1,0:T(8,128)S(1)} %constant_dynamic-update-slice_fusion, f32[32,4096]{1,0:T(8,128)S(1)} %collective-permute-done.13, f32[16,4096]{1,0:T(8,128)S(1)} %collective-permute-done.12, ...), kind=kOutput, calls=%fused_computation.2 | convolution fusion | flops 1623982080 | bytes 34734080 | tf_op jit(solution)/shard_map/dot_general | solution.py:28
  292.7 26.1 %collective-permute-done.2 = f32[128,2048]{1,0:T(8,128)S(1)} collective-permute-done((f32[128,2048]{1,0:T(8,128)S(1)}, f32[128,2048]{1,0:T(8,128)S(1)}, u32[]{:S(2)}, u32[]{:S(2)}) %collective-permute-start.2) | collective-permute-done | bytes 1048608 | tf_op jit(solution)/shard_map/ppermute | solution.py:34
  318.8 3.4 collective-permute-start.3
  324.5 22.5 %collective-permute-done.14 = f32[80,2048]{1,0:T(8,128)S(1)} collective-permute-done((f32[80,2048]{1,0:T(8,128)}, f32[80,2048]{1,0:T(8,128)S(1)}, u32[]{:S(2)}, u32[]{:S(2)}) %collective-permute-start.14) | collective-permute-done | bytes 655392 | tf_op jit(solution)/shard_map/ppermute | solution.py:34
  347.0 3.3 collective-permute-start.16
  354.5 9.4 %collective-permute-done.3.part = f32[64,2048]{1,0:T(8,128)S(1)} collective-permute-done((f32[64,2048]{1,0:T(8,128)}, f32[64,2048]{1,0:T(8,128)S(1)}, u32[]{:S(2)}, u32[]{:S(2)}) %collective-permute-start.3) | collective-permute-done | bytes 524320 | tf_op jit(solution)/shard_map/ppermute | solution.py:34
  364.7 2.9 shard_map.145
  (78 shorter events, 44.9 us)
Async XLA Ops:
  1.6 31.4 %collective-permute-start = (f32[16,2048]{1,0:T(8,128)S(1)}, f32[16,2048]{1,0:T(8,128)S(1)}, u32[]{:S(2)}, u32[]{:S(2)}) collective-permute-start(f32[16,2048]{1,0:T(8,128)S(1)} %dynamic-slice_bitcast_fusion), channel_id=1, source_target_pairs={{0,16},{16,0},{1,17},{17,1},{2,18},{18,2},{3,19},{19,3},{4,20},{20... | collective-permute-start | bytes 393224 | tf_op jit(solution)/shard_map/ppermute | solution.py:34
  6.3 107.6 %collective-permute-start.4 = (f32[96,2048]{1,0:T(8,128)}, f32[96,2048]{1,0:T(8,128)}, u32[]{:S(2)}, u32[]{:S(2)}) collective-permute-start(f32[96,2048]{1,0:T(8,128)} %constant_dynamic-slice_fusion.5), channel_id=1, source_target_pairs={{0,16},{16,0},{1,17},{17,1},{2,18},{18,2},{3,19},{19,3},{4,20},{20... | collective-permute-start | bytes 2359304 | tf_op jit(solution)/shard_map/ppermute | solution.py:34
  12.4 20.5 %copy-start.3 = (f32[1,2,256]{2,1,0:T(2,128)S(1)}, f32[1,2,256]{2,1,0:T(2,128)}, u32[]{:S(2)}) copy-start(f32[1,2,256]{2,1,0:T(2,128)} %param.14) | copy-start | bytes 6148
  12.4 20.5 %copy-start.4 = (f32[1,256]{1,0:T(1,128)S(1)}, f32[1,256]{1,0:T(1,128)}, u32[]{:S(2)}) copy-start(f32[1,256]{1,0:T(1,128)} %param.15) | copy-start | bytes 3076
  24.8 37.9 %collective-permute-start.7 = (f32[32,4096]{1,0:T(8,128)}, f32[32,4096]{1,0:T(8,128)}, u32[]{:S(2)}, u32[]{:S(2)}) collective-permute-start(f32[32,4096]{1,0:T(8,128)} %slice.70), channel_id=1, source_target_pairs={{0,2},{2,0},{4,6},{6,4},{8,10},{10,8},{12,14},{14,12},{1,3},{3,1},... | collective-permute-start | bytes 1572872 | tf_op jit(solution)/shard_map/ppermute | solution.py:39
  27.5 145.3 %collective-permute-start.1 = (f32[192,2048]{1,0:T(8,128)}, f32[192,2048]{1,0:T(8,128)}, u32[]{:S(2)}, u32[]{:S(2)}) collective-permute-start(f32[192,2048]{1,0:T(8,128)} %constant_dynamic-slice_fusion.4), channel_id=1, source_target_pairs={{0,16},{16,0},{1,17},{17,1},{2,18},{18,2},{3,19},{19,3},{4,20},{20... | collective-permute-start | bytes 4718600 | tf_op jit(solution)/shard_map/ppermute | solution.py:34
  39.4 225.7 %collective-permute-start.17 = (f32[2,256]{1,0:T(2,128)S(1)}, f32[2,256]{1,0:T(2,128)S(1)}, u32[]{:S(2)}, u32[]{:S(2)}) collective-permute-start(f32[2,256]{1,0:T(2,128)S(1)} %subtract_select_fusion), channel_id=1, source_target_pairs={{0,16},{16,0},{1,17},{17,1},{2,18},{18,2},{3,19},{19,3},{4,20},{20... | collective-permute-start | bytes 6152 | tf_op jit(solution)/shard_map/ppermute | solution.py:34
  39.7 217.3 %collective-permute-start.5 = (f32[208,2048]{1,0:T(8,128)}, f32[208,2048]{1,0:T(8,128)}, u32[]{:S(2)}, u32[]{:S(2)}) collective-permute-start(f32[208,2048]{1,0:T(8,128)} %constant_dynamic-slice_fusion.3), channel_id=1, source_target_pairs={{0,16},{16,0},{1,17},{17,1},{2,18},{18,2},{3,19},{19,3},{4,20},{20... | collective-permute-start | bytes 5111816 | tf_op jit(solution)/shard_map/ppermute | solution.py:34
  63.8 7.9 %collective-permute-start.8 = (f32[16,4096]{1,0:T(8,128)S(1)}, f32[16,4096]{1,0:T(8,128)S(1)}, u32[]{:S(2)}, u32[]{:S(2)}) collective-permute-start(f32[16,4096]{1,0:T(8,128)S(1)} %slice.72), channel_id=1, source_target_pairs={{0,4},{2,6},{4,0},{6,2},{8,12},{10,14},{12,8},{14,10},{1,5},{3,7},... | collective-permute-start | bytes 786440 | tf_op jit(solution)/shard_map/ppermute | solution.py:39
  71.8 48.4 %collective-permute-start.9 = (f32[8,4096]{1,0:T(8,128)S(1)}, f32[8,4096]{1,0:T(8,128)S(1)}, u32[]{:S(2)}, u32[]{:S(2)}) collective-permute-start(f32[8,4096]{1,0:T(8,128)S(1)} %slice.74), channel_id=1, source_target_pairs={{0,8},{2,10},{4,12},{6,14},{8,0},{10,2},{12,4},{14,6},{1,9},{3,11}... | collective-permute-start | bytes 393224 | tf_op jit(solution)/shard_map/ppermute | solution.py:39
  113.8 151.2 %collective-permute-start.6 = (f32[128,2048]{1,0:T(8,128)S(1)}, f32[128,2048]{1,0:T(8,128)S(1)}, u32[]{:S(2)}, u32[]{:S(2)}) collective-permute-start(f32[128,2048]{1,0:T(8,128)S(1)} %get-tuple-element.29), channel_id=1, source_target_pairs={{0,16},{16,0},{1,17},{17,1},{2,18},{18,2},{3,19},{19,3},{4,20},{20... | collective-permute-start | bytes 3145736 | tf_op jit(solution)/shard_map/ppermute | solution.py:34
  120.3 136.7 %collective-permute-start.10 = (f32[8,4096]{1,0:T(8,128)S(1)}, f32[8,4096]{1,0:T(8,128)S(1)}, u32[]{:S(2)}, u32[]{:S(2)}) collective-permute-start(f32[8,4096]{1,0:T(8,128)S(1)} %slice_add_fusion.3), channel_id=1, source_target_pairs={{0,16},{16,0},{1,17},{17,1},{2,18},{18,2},{3,19},{19,3},{4,20},{20... | collective-permute-start | bytes 393224 | tf_op jit(solution)/shard_map/ppermute | solution.py:34
  172.8 146.0 %collective-permute-start.2 = (f32[128,2048]{1,0:T(8,128)S(1)}, f32[128,2048]{1,0:T(8,128)S(1)}, u32[]{:S(2)}, u32[]{:S(2)}) collective-permute-start(f32[128,2048]{1,0:T(8,128)S(1)} %get-tuple-element.24), channel_id=1, source_target_pairs={{0,16},{16,0},{1,17},{17,1},{2,18},{18,2},{3,19},{19,3},{4,20},{20... | collective-permute-start | bytes 3145736 | tf_op jit(solution)/shard_map/ppermute | solution.py:34
  181.0 84.0 %copy-start.1 = (f32[80,2048]{1,0:T(8,128)S(1)}, f32[80,2048]{1,0:T(8,128)}, u32[]{:S(2)}) copy-start(f32[80,2048]{1,0:T(8,128)} %get-tuple-element.32) | copy-start | bytes 1966084
  257.0 11.5 %collective-permute-start.11 = (f32[8,4096]{1,0:T(8,128)S(1)}, f32[8,4096]{1,0:T(8,128)S(1)}, u32[]{:S(2)}, u32[]{:S(2)}) collective-permute-start(f32[8,4096]{1,0:T(8,128)S(1)} %add_multiply_fusion), channel_id=1, source_target_pairs={{0,8},{2,10},{4,12},{6,14},{8,0},{10,2},{12,4},{14,6},{1,9},{3,11}... | collective-permute-start | bytes 393224 | tf_op jit(solution)/shard_map/ppermute | solution.py:39
  258.6 20.6 %slice-start = ((s8[8388608]{0:T(1024)(128)(4,1)}), s8[4194304]{0:T(1024)(128)(4,1)S(1)}, s32[]{:S(2)}) async-start(s8[8388608]{0:T(1024)(128)(4,1)} %bitcast.41), calls=%async_computation | async-start | bytes 8388608
  258.6 20.6 %slice-start.2 = ((s8[8388608]{0:T(1024)(128)(4,1)}), s8[4194304]{0:T(1024)(128)(4,1)S(1)}, s32[]{:S(2)}) async-start(s8[8388608]{0:T(1024)(128)(4,1)} %bitcast.43), calls=%async_computation.2 | async-start | bytes 8388608
  263.9 15.4 %slice-start.3 = ((s8[8388608]{0:T(1024)(128)(4,1)}), s8[4194304]{0:T(1024)(128)(4,1)S(1)}, s32[]{:S(2)}) async-start(s8[8388608]{0:T(1024)(128)(4,1)} %bitcast.43), calls=%async_computation.3 | async-start | bytes 8388608
  265.1 87.2 %collective-permute-start.15 = (f32[80,2048]{1,0:T(8,128)S(1)}, f32[80,2048]{1,0:T(8,128)}, u32[]{:S(2)}, u32[]{:S(2)}) collective-permute-start(f32[80,2048]{1,0:T(8,128)S(1)} %copy-done.1), channel_id=1, source_target_pairs={{0,16},{16,0},{1,17},{17,1},{2,18},{18,2},{3,19},{19,3},{4,20},{20... | collective-permute-start | bytes 1966088 | tf_op jit(solution)/shard_map/ppermute | solution.py:34
  268.5 7.6 %collective-permute-start.12 = (f32[16,4096]{1,0:T(8,128)S(1)}, f32[16,4096]{1,0:T(8,128)S(1)}, u32[]{:S(2)}, u32[]{:S(2)}) collective-permute-start(f32[16,4096]{1,0:T(8,128)S(1)} %pad_maximum_fusion.2), channel_id=1, source_target_pairs={{0,4},{2,6},{4,0},{6,2},{8,12},{10,14},{12,8},{14,10},{1,5},{3,7},... | collective-permute-start | bytes 786440 | tf_op jit(solution)/shard_map/ppermute | solution.py:39
  276.2 3.0 collective-permute-start.13
  291.8 55.2 %collective-permute-start.14 = (f32[80,2048]{1,0:T(8,128)}, f32[80,2048]{1,0:T(8,128)S(1)}, u32[]{:S(2)}, u32[]{:S(2)}) collective-permute-start(f32[80,2048]{1,0:T(8,128)} %get-tuple-element.31), channel_id=1, source_target_pairs={{0,16},{16,0},{1,17},{17,1},{2,18},{18,2},{3,19},{19,3},{4,20},{20... | collective-permute-start | bytes 1966088 | tf_op jit(solution)/shard_map/ppermute | solution.py:34
  318.8 45.0 %collective-permute-start.3 = (f32[64,2048]{1,0:T(8,128)}, f32[64,2048]{1,0:T(8,128)S(1)}, u32[]{:S(2)}, u32[]{:S(2)}) collective-permute-start(f32[64,2048]{1,0:T(8,128)} %slice.65), channel_id=1, source_target_pairs={{0,16},{16,0},{1,17},{17,1},{2,18},{18,2},{3,19},{19,3},{4,20},{20... | collective-permute-start | bytes 1572872 | tf_op jit(solution)/shard_map/ppermute | solution.py:34
  347.0 22.3 %collective-permute-start.16 = (f32[32,2048]{1,0:T(8,128)S(1)}, f32[32,2048]{1,0:T(8,128)S(1)}, u32[]{:S(2)}, u32[]{:S(2)}) collective-permute-start(f32[32,2048]{1,0:T(8,128)S(1)} %slice_add_fusion.1), channel_id=1, source_target_pairs={{0,16},{16,0},{1,17},{17,1},{2,18},{18,2},{3,19},{19,3},{4,20},{20... | collective-permute-start | bytes 786440 | tf_op jit(solution)/shard_map/ppermute | solution.py:34
  (4 other events, 38.6 us)

commit v13 on v12

--- a/solution.py
+++ b/solution.py
@@ -11,7 +11,7 @@
 momentum = 0.9
 rate = outer_rate * (1 + momentum)
 decay = outer_rate * momentum * momentum
-first_sizes = (1, 6, 12, 13)
+first_sizes = (3, 11, 24, 26)
 last_sizes = (8, 8, 5, 5, 4, 2)
 window = 3
 gate_before = 6

time: 373 us -> 373 us (level)
  waiting for transfers between devices: 239 us -> 235 us
    ppermute x6, waiting for transfers between devices: 10.4 us -> 5.65 us  [across(): return lax.ppermute(array, 'shard', [(i, i ^ k) for i in range(shards)])]
  transfers between devices with their start and end apart: 18 -> 18, of which waited for: 9 -> 10; matrix products, arithmetic and copies ran while one was open for 26% -> 26% of each run, Pallas kernels for 1% -> 1%
where the time goes in v13:
time: 373 us; the launch traced here: 370 us
  waiting for transfers between devices  235 us (63%)
  other arithmetic  46.1 us (12%)
  starting transfers between devices  33.5 us (9%)
  local copies, waits for them, and re-layouts  26.9 us (7%)
  matrix products  24.9 us (7%)
    ppermute x12, waiting for transfers between devices, swap(): return lax.ppermute(array, 'group', [(0, 1), (1, 0)])  229 us
    ppermute x12, starting transfers between devices, swap(): return lax.ppermute(array, 'group', [(0, 1), (1, 0)])  29 us
    dynamic_update_slice x5, other arithmetic, put_rows(): lax.dynamic_update_slice_in_dim(array, rows, start, 0, allow_negative_ind...  14.1 us
    unnamed x28, local copies, waits for them, and re-layouts  13.9 us
    dot_general x1, matrix products, rebuild(): lax.dot_general(factors, factor_basis, (((0,), (0,)), ((), ())), precisio...  13.3 us
    add x1, other arithmetic, body(): anchor_next = (1 - rate) * after(down_anchor, parts[0]) + rate / 2 * local  12.1 us
    dot_general x1, matrix products, body(): lax.dot_general(basis, gate_diff, (((1,), (1,)), ((), ())), precision=lax...  11.6 us
    sub x3, other arithmetic, body(): momentum * old + rows_of(down_anchor, own + start, size)  9.62 us
  transfers between devices with their start and end apart: 18, of which 10 were waited for; matrix products, arithmetic and copies ran while one was open for 26% of the time, Pallas kernels for 1%

profile of v13, /device:TPU:10, one launch (start us, length us, event | category | flops | bytes accessed | tf_op | source)
XLA Modules:
  0.0 370.0 jit_solution(13514429256093180719)
XLA Ops:
  12.3 11.6 %fusion = f32[64,4096]{1,0:T(8,128)S(1)} fusion(f32[64,512]{1,0:T(8,128)S(1)} %constant_dynamic-update-slice_fusion, f32[4096,512]{1,0:T(8,128)} %param.16, f32[1,4096,512]{2,1,0:T(8,128)} %param.17), kind=kOutput, calls=%fused_computation.1 | convolution fusion | flops 1612709888 | bytes 17956864 | tf_op jit(solution)/shard_map/dot_general | solution.py:158
  30.0 2.8 constant_dynamic-slice_fusion.3
  32.9 4.4 %bitcast_subtract_fusion.2 = f32[512,2048]{1,0:T(8,128)S(1)} fusion(f32[512,2048]{1,0:T(8,128)} %param.12, f32[1,1024,2048]{2,1,0:T(8,128)} %param.11, s32[]{:T(128)S(6)} %mul.187), kind=kLoop, calls=%fused_computation.6 | loop fusion | flops 3145728 | bytes 12582916 | tf_op jit(solution)/shard_map/sub | solution.py:180
  42.3 12.1 %multiply_add_fusion.1 = f32[1024,2048]{1,0:T(8,128)} fusion(f32[1024,2048]{1,0:T(8,128)} %param.10, f32[1,1024,2048]{2,1,0:T(8,128)} %param.11), kind=kLoop, calls=%fused_computation.4 | loop fusion | flops 6291456 | bytes 25165824 | tf_op jit(solution)/shard_map/add | solution.py:181
  54.4 8.0 %copy.17 = f32[1024,2048]{1,0:T(8,128)} copy(f32[1024,2048]{1,0:T(8,128)} %multiply_add_fusion.1) | data formatting | bytes 16777216
  66.3 47.6 %collective-permute-done.4 = f32[88,2048]{1,0:T(8,128)} collective-permute-done((f32[88,2048]{1,0:T(8,128)}, f32[88,2048]{1,0:T(8,128)}, u32[]{:S(2)}, u32[]{:S(2)}) %collective-permute-start.4) | collective-permute-done | bytes 720928 | tf_op jit(solution)/shard_map/ppermute | solution.py:34
  113.9 3.4 collective-permute-start.6
  118.9 2.9 fusion.14
  122.8 50.1 %collective-permute-done.1 = f32[192,2048]{1,0:T(8,128)} collective-permute-done((f32[192,2048]{1,0:T(8,128)}, f32[192,2048]{1,0:T(8,128)}, u32[]{:S(2)}, u32[]{:S(2)}) %collective-permute-start.1) | collective-permute-done | bytes 1572896 | tf_op jit(solution)/shard_map/ppermute | solution.py:34
  172.8 3.4 collective-permute-start.2
  176.2 4.8 %fusion.4 = (f32[192,2048]{1,0:T(8,128)S(1)}, f32[1024,2048]{1,0:T(8,128)}) fusion(f32[192,2048]{1,0:T(8,128)} %collective-permute-done.1, f32[1,1024,2048]{2,1,0:T(8,128)} %param.11, s32[]{:T(128)S(6)} %add.142, f32[1024,2048]{1,0:T(8,128)} %param.10, f32[512,2048]{1,0:T(8,128)S(1)} %copy-done, f32[1024,2048]{1,0:T(8,128)} %get-tuple-element.44), kind=kLoop, calls=%fused_computation.14 | loop fusion | flops 3538944 | bytes 11010052 | tf_op jit(solution)/shard_map/sub | solution.py:202
  181.1 73.2 %collective-permute-done.6 = f32[128,2048]{1,0:T(8,128)S(1)} collective-permute-done((f32[128,2048]{1,0:T(8,128)S(1)}, f32[128,2048]{1,0:T(8,128)S(1)}, u32[]{:S(2)}, u32[]{:S(2)}) %collective-permute-start.6) | collective-permute-done | bytes 1048608 | tf_op jit(solution)/shard_map/ppermute | solution.py:34
  254.2 3.4 collective-permute-start.15
  257.6 13.5 %collective-permute-done.10 = f32[8,4096]{1,0:T(8,128)S(1)} collective-permute-done((f32[8,4096]{1,0:T(8,128)S(1)}, f32[8,4096]{1,0:T(8,128)S(1)}, u32[]{:S(2)}, u32[]{:S(2)}) %collective-permute-start.10) | collective-permute-done | bytes 131104 | tf_op jit(solution)/shard_map/ppermute | solution.py:34
  272.7 5.2 %add_dynamic-update-slice_fusion = (f32[1024,2048]{1,0:T(8,128)}, f32[208,2048]{1,0:T(8,128)S(1)}, f32[208,2048]{1,0:T(8,128)S(1)}) fusion(f32[1024,2048]{1,0:T(8,128)} %get-tuple-element.42, s32[]{:T(128)S(6)} %add.144, f32[512,2048]{1,0:T(8,128)S(1)} %copy-done, f32[208,2048]{1,0:T(8,128)} %collective-permute-done.5, f32[1,1024,2048]{2,1,0:T(8,128)} %param.11, ...), kind=kLoop, calls=%fused_computation.10 | loop fusion | flops 3833856 | bytes 13631492 | tf_op jit(solution)/shard_map/dynamic_update_slice | solution.py:101
  282.0 5.0 %collective-permute-done.12 = f32[16,4096]{1,0:T(8,128)S(1)} collective-permute-done((f32[16,4096]{1,0:T(8,128)S(1)}, f32[16,4096]{1,0:T(8,128)S(1)}, u32[]{:S(2)}, u32[]{:S(2)}) %collective-permute-start.12) | collective-permute-done | bytes 262176 | tf_op jit(solution)/shard_map/ppermute | solution.py:39
  290.2 13.3 %multiply_subtract_fusion = (f32[4096,512]{1,0:T(8,128)}, f32[4096,512]{1,0:T(8,128)}) fusion(f32[4096,512]{1,0:T(8,128)S(1)} %bitcast.42, f32[4096,512]{1,0:T(8,128)S(1)} %bitcast.44, f32[64,512]{1,0:T(8,128)S(1)} %constant_dynamic-update-slice_fusion, f32[32,4096]{1,0:T(8,128)} %collective-permute-done.13, f32[16,4096]{1,0:T(8,128)S(1)} %collective-permute-done.12, ...), kind=kOutput, calls=%fused_computation.2 | convolution fusion | flops 1623982080 | bytes 34734080 | tf_op jit(solution)/shard_map/dot_general | solution.py:28
  303.5 3.4 collective-permute-start.14
  307.5 11.4 %collective-permute-done.2 = f32[128,2048]{1,0:T(8,128)S(1)} collective-permute-done((f32[128,2048]{1,0:T(8,128)S(1)}, f32[128,2048]{1,0:T(8,128)S(1)}, u32[]{:S(2)}, u32[]{:S(2)}) %collective-permute-start.2) | collective-permute-done | bytes 1048608 | tf_op jit(solution)/shard_map/ppermute | solution.py:34
  318.8 3.4 collective-permute-start.3
  324.6 22.5 %collective-permute-done.14 = f32[80,2048]{1,0:T(8,128)S(1)} collective-permute-done((f32[80,2048]{1,0:T(8,128)}, f32[80,2048]{1,0:T(8,128)S(1)}, u32[]{:S(2)}, u32[]{:S(2)}) %collective-permute-start.14) | collective-permute-done | bytes 655392 | tf_op jit(solution)/shard_map/ppermute | solution.py:34
  347.0 3.3 collective-permute-start.16
  354.5 9.4 %collective-permute-done.3.part = f32[64,2048]{1,0:T(8,128)S(1)} collective-permute-done((f32[64,2048]{1,0:T(8,128)}, f32[64,2048]{1,0:T(8,128)S(1)}, u32[]{:S(2)}, u32[]{:S(2)}) %collective-permute-start.3) | collective-permute-done | bytes 524320 | tf_op jit(solution)/shard_map/ppermute | solution.py:34
  364.7 2.9 shard_map.145
  (78 shorter events, 48.2 us)
Async XLA Ops:
  1.6 31.3 %collective-permute-start = (f32[24,2048]{1,0:T(8,128)S(1)}, f32[24,2048]{1,0:T(8,128)S(1)}, u32[]{:S(2)}, u32[]{:S(2)}) collective-permute-start(f32[24,2048]{1,0:T(8,128)S(1)} %dynamic-slice_bitcast_fusion), channel_id=1, source_target_pairs={{0,16},{16,0},{1,17},{17,1},{2,18},{18,2},{3,19},{19,3},{4,20},{20... | collective-permute-start | bytes 589832 | tf_op jit(solution)/shard_map/ppermute | solution.py:34
  6.2 107.6 %collective-permute-start.4 = (f32[88,2048]{1,0:T(8,128)}, f32[88,2048]{1,0:T(8,128)}, u32[]{:S(2)}, u32[]{:S(2)}) collective-permute-start(f32[88,2048]{1,0:T(8,128)} %constant_dynamic-slice_fusion.5), channel_id=1, source_target_pairs={{0,16},{16,0},{1,17},{17,1},{2,18},{18,2},{3,19},{19,3},{4,20},{20... | collective-permute-start | bytes 2162696 | tf_op jit(solution)/shard_map/ppermute | solution.py:34
  12.3 20.5 %copy-start.3 = (f32[1,2,256]{2,1,0:T(2,128)S(1)}, f32[1,2,256]{2,1,0:T(2,128)}, u32[]{:S(2)}) copy-start(f32[1,2,256]{2,1,0:T(2,128)} %param.14) | copy-start | bytes 6148
  12.3 20.5 %copy-start.4 = (f32[1,256]{1,0:T(1,128)S(1)}, f32[1,256]{1,0:T(1,128)}, u32[]{:S(2)}) copy-start(f32[1,256]{1,0:T(1,128)} %param.15) | copy-start | bytes 3076
  24.7 37.9 %collective-permute-start.7 = (f32[32,4096]{1,0:T(8,128)}, f32[32,4096]{1,0:T(8,128)}, u32[]{:S(2)}, u32[]{:S(2)}) collective-permute-start(f32[32,4096]{1,0:T(8,128)} %slice.70), channel_id=1, source_target_pairs={{0,2},{2,0},{4,6},{6,4},{8,10},{10,8},{12,14},{14,12},{1,3},{3,1},... | collective-permute-start | bytes 1572872 | tf_op jit(solution)/shard_map/ppermute | solution.py:39
  27.5 145.4 %collective-permute-start.1 = (f32[192,2048]{1,0:T(8,128)}, f32[192,2048]{1,0:T(8,128)}, u32[]{:S(2)}, u32[]{:S(2)}) collective-permute-start(f32[192,2048]{1,0:T(8,128)} %constant_dynamic-slice_fusion.4), channel_id=1, source_target_pairs={{0,16},{16,0},{1,17},{17,1},{2,18},{18,2},{3,19},{19,3},{4,20},{20... | collective-permute-start | bytes 4718600 | tf_op jit(solution)/shard_map/ppermute | solution.py:34
  39.3 239.8 %collective-permute-start.17 = (f32[2,256]{1,0:T(2,128)S(1)}, f32[2,256]{1,0:T(2,128)S(1)}, u32[]{:S(2)}, u32[]{:S(2)}) collective-permute-start(f32[2,256]{1,0:T(2,128)S(1)} %subtract_select_fusion), channel_id=1, source_target_pairs={{0,16},{16,0},{1,17},{17,1},{2,18},{18,2},{3,19},{19,3},{4,20},{20... | collective-permute-start | bytes 6152 | tf_op jit(solution)/shard_map/ppermute | solution.py:34
  39.7 231.4 %collective-permute-start.5 = (f32[208,2048]{1,0:T(8,128)}, f32[208,2048]{1,0:T(8,128)}, u32[]{:S(2)}, u32[]{:S(2)}) collective-permute-start(f32[208,2048]{1,0:T(8,128)} %constant_dynamic-slice_fusion.3), channel_id=1, source_target_pairs={{0,16},{16,0},{1,17},{17,1},{2,18},{18,2},{3,19},{19,3},{4,20},{20... | collective-permute-start | bytes 5111816 | tf_op jit(solution)/shard_map/ppermute | solution.py:34
  63.8 53.4 %collective-permute-start.8 = (f32[16,4096]{1,0:T(8,128)S(1)}, f32[16,4096]{1,0:T(8,128)S(1)}, u32[]{:S(2)}, u32[]{:S(2)}) collective-permute-start(f32[16,4096]{1,0:T(8,128)S(1)} %slice.72), channel_id=1, source_target_pairs={{0,4},{2,6},{4,0},{6,2},{8,12},{10,14},{12,8},{14,10},{1,5},{3,7},... | collective-permute-start | bytes 786440 | tf_op jit(solution)/shard_map/ppermute | solution.py:39
  113.9 140.4 %collective-permute-start.6 = (f32[128,2048]{1,0:T(8,128)S(1)}, f32[128,2048]{1,0:T(8,128)S(1)}, u32[]{:S(2)}, u32[]{:S(2)}) collective-permute-start(f32[128,2048]{1,0:T(8,128)S(1)} %get-tuple-element.29), channel_id=1, source_target_pairs={{0,16},{16,0},{1,17},{17,1},{2,18},{18,2},{3,19},{19,3},{4,20},{20... | collective-permute-start | bytes 3145736 | tf_op jit(solution)/shard_map/ppermute | solution.py:34
  117.3 137.0 %copy-start.1 = (f32[80,2048]{1,0:T(8,128)S(1)}, f32[80,2048]{1,0:T(8,128)}, u32[]{:S(2)}) copy-start(f32[80,2048]{1,0:T(8,128)} %get-tuple-element.32) | copy-start | bytes 1966084
  117.3 5.1 %collective-permute-start.9 = (f32[8,4096]{1,0:T(8,128)S(1)}, f32[8,4096]{1,0:T(8,128)S(1)}, u32[]{:S(2)}, u32[]{:S(2)}) collective-permute-start(f32[8,4096]{1,0:T(8,128)S(1)} %slice.74), channel_id=1, source_target_pairs={{0,8},{2,10},{4,12},{6,14},{8,0},{10,2},{12,4},{14,6},{1,9},{3,11}... | collective-permute-start | bytes 393224 | tf_op jit(solution)/shard_map/ppermute | solution.py:39
  122.4 148.7 %collective-permute-start.10 = (f32[8,4096]{1,0:T(8,128)S(1)}, f32[8,4096]{1,0:T(8,128)S(1)}, u32[]{:S(2)}, u32[]{:S(2)}) collective-permute-start(f32[8,4096]{1,0:T(8,128)S(1)} %slice_add_fusion.3), channel_id=1, source_target_pairs={{0,16},{16,0},{1,17},{17,1},{2,18},{18,2},{3,19},{19,3},{4,20},{20... | collective-permute-start | bytes 393224 | tf_op jit(solution)/shard_map/ppermute | solution.py:34
  172.8 146.0 %collective-permute-start.2 = (f32[128,2048]{1,0:T(8,128)S(1)}, f32[128,2048]{1,0:T(8,128)S(1)}, u32[]{:S(2)}, u32[]{:S(2)}) collective-permute-start(f32[128,2048]{1,0:T(8,128)S(1)} %get-tuple-element.24), channel_id=1, source_target_pairs={{0,16},{16,0},{1,17},{17,1},{2,18},{18,2},{3,19},{19,3},{4,20},{20... | collective-permute-start | bytes 3145736 | tf_op jit(solution)/shard_map/ppermute | solution.py:34
  254.2 98.1 %collective-permute-start.15 = (f32[80,2048]{1,0:T(8,128)S(1)}, f32[80,2048]{1,0:T(8,128)}, u32[]{:S(2)}, u32[]{:S(2)}) collective-permute-start(f32[80,2048]{1,0:T(8,128)S(1)} %copy-done.1), channel_id=1, source_target_pairs={{0,16},{16,0},{1,17},{17,1},{2,18},{18,2},{3,19},{19,3},{4,20},{20... | collective-permute-start | bytes 1966088 | tf_op jit(solution)/shard_map/ppermute | solution.py:34
  271.1 8.0 %collective-permute-start.11 = (f32[8,4096]{1,0:T(8,128)S(1)}, f32[8,4096]{1,0:T(8,128)S(1)}, u32[]{:S(2)}, u32[]{:S(2)}) collective-permute-start(f32[8,4096]{1,0:T(8,128)S(1)} %add_multiply_fusion), channel_id=1, source_target_pairs={{0,8},{2,10},{4,12},{6,14},{8,0},{10,2},{12,4},{14,6},{1,9},{3,11}... | collective-permute-start | bytes 393224 | tf_op jit(solution)/shard_map/ppermute | solution.py:39
  272.7 17.4 %slice-start = ((s8[8388608]{0:T(1024)(128)(4,1)}), s8[4194304]{0:T(1024)(128)(4,1)S(1)}, s32[]{:S(2)}) async-start(s8[8388608]{0:T(1024)(128)(4,1)} %bitcast.41), calls=%async_computation | async-start | bytes 8388608
  272.7 17.4 %slice-start.2 = ((s8[8388608]{0:T(1024)(128)(4,1)}), s8[4194304]{0:T(1024)(128)(4,1)S(1)}, s32[]{:S(2)}) async-start(s8[8388608]{0:T(1024)(128)(4,1)} %bitcast.43), calls=%async_computation.2 | async-start | bytes 8388608
  278.0 12.2 %slice-start.3 = ((s8[8388608]{0:T(1024)(128)(4,1)}), s8[4194304]{0:T(1024)(128)(4,1)S(1)}, s32[]{:S(2)}) async-start(s8[8388608]{0:T(1024)(128)(4,1)} %bitcast.43), calls=%async_computation.3 | async-start | bytes 8388608
  279.2 7.9 %collective-permute-start.12 = (f32[16,4096]{1,0:T(8,128)S(1)}, f32[16,4096]{1,0:T(8,128)S(1)}, u32[]{:S(2)}, u32[]{:S(2)}) collective-permute-start(f32[16,4096]{1,0:T(8,128)S(1)} %pad_maximum_fusion.2), channel_id=1, source_target_pairs={{0,4},{2,6},{4,0},{6,2},{8,12},{10,14},{12,8},{14,10},{1,5},{3,7},... | collective-permute-start | bytes 786440 | tf_op jit(solution)/shard_map/ppermute | solution.py:39
  287.1 3.0 collective-permute-start.13
  303.5 43.5 %collective-permute-start.14 = (f32[80,2048]{1,0:T(8,128)}, f32[80,2048]{1,0:T(8,128)S(1)}, u32[]{:S(2)}, u32[]{:S(2)}) collective-permute-start(f32[80,2048]{1,0:T(8,128)} %get-tuple-element.31), channel_id=1, source_target_pairs={{0,16},{16,0},{1,17},{17,1},{2,18},{18,2},{3,19},{19,3},{4,20},{20... | collective-permute-start | bytes 1966088 | tf_op jit(solution)/shard_map/ppermute | solution.py:34
  318.8 45.0 %collective-permute-start.3 = (f32[64,2048]{1,0:T(8,128)}, f32[64,2048]{1,0:T(8,128)S(1)}, u32[]{:S(2)}, u32[]{:S(2)}) collective-permute-start(f32[64,2048]{1,0:T(8,128)} %slice.65), channel_id=1, source_target_pairs={{0,16},{16,0},{1,17},{17,1},{2,18},{18,2},{3,19},{19,3},{4,20},{20... | collective-permute-start | bytes 1572872 | tf_op jit(solution)/shard_map/ppermute | solution.py:34
  347.0 22.3 %collective-permute-start.16 = (f32[32,2048]{1,0:T(8,128)S(1)}, f32[32,2048]{1,0:T(8,128)S(1)}, u32[]{:S(2)}, u32[]{:S(2)}) collective-permute-start(f32[32,2048]{1,0:T(8,128)S(1)} %slice_add_fusion.1), channel_id=1, source_target_pairs={{0,16},{16,0},{1,17},{17,1},{2,18},{18,2},{3,19},{19,3},{4,20},{20... | collective-permute-start | bytes 786440 | tf_op jit(solution)/shard_map/ppermute | solution.py:34
  (4 other events, 32.2 us)
